TPU v7x, 32 devices: a whole 2x2x4 slice. The times are simulated.
32 devices in a mesh: batch: 2 (over core), expert: 16 (over z, y, x).
Axes of the slice: x: 2, y: 2, z: 4, core: 2. Of those that a mesh axis runs over, the one named last changes fastest.
Arguments:
- patches: bfloat16 [43520, 384], P(('batch', 'expert')), may hold values from -6 to 6
- slot_len: int32 [32, 5], P(('batch', 'expert')), may hold values from 0 to 576, as said below
- attn_weight: float32 [384, 1536], P('expert')
- attn_first: float32 [384, 1536], P('expert'), may hold values from -0.005859375 to 0.005859375
- attn_second: float32 [384, 1536], P('expert'), may hold values from 1.0850695e-06 to 4.340278e-06
- phi_weight: float32 [384, 16], P('expert'), may hold values from -0.078125 to 0.078125
- phi_first: float32 [384, 16], P('expert'), may hold values from -0.005859375 to 0.005859375
- phi_second: float32 [384, 16], P('expert'), may hold values from 1.0850695e-06 to 4.340278e-06
- norm_params: float32 [4, 384], P(None, 'expert')
- norm_first: float32 [4, 384], P(None, 'expert'), may hold values from -0.0078125 to 0.0078125
- norm_second: float32 [4, 384], P(None, 'expert'), may hold values from 1.695421e-06 to 6.781684e-06
- expert_in: float32 [16, 384, 1536], P('expert', None, 'batch'), may hold values from -2.5 to 2.5
- in_first: float32 [16, 384, 1536], P('expert', None, 'batch'), may hold values from -1.5258789e-05 to 1.5258789e-05
- in_second: float32 [16, 384, 1536], P('expert', None, 'batch'), may hold values from 6.781684e-12 to 2.7126737e-11
- expert_out: float32 [16, 1536, 384], P('expert', 'batch'), may hold values from -2.5 to 2.5
- out_first: float32 [16, 1536, 384], P('expert', 'batch'), may hold values from -2.2888184e-05 to 2.2888184e-05
- out_second: float32 [16, 1536, 384], P('expert', 'batch'), may hold values from 1.5258789e-11 to 6.1035156e-11
- cotangent: bfloat16 [43520, 384], P(('batch', 'expert')), may hold values from -6 to 6
Outputs:
- block_output: bfloat16 [43520, 384], P(('batch', 'expert'))
- input_grad: bfloat16 [43520, 384], P(('batch', 'expert'))
- grad_norm: float32 [], replicated
- attn_new: float32 [384, 1536], P('expert')
- attn_first_new: float32 [384, 1536], P('expert')
- attn_second_new: float32 [384, 1536], P('expert')
- phi_new: float32 [384, 16], P('expert')
- phi_first_new: float32 [384, 16], P('expert')
- phi_second_new: float32 [384, 16], P('expert')
- norm_new: float32 [4, 384], P(None, 'expert')
- norm_first_new: float32 [4, 384], P(None, 'expert')
- norm_second_new: float32 [4, 384], P(None, 'expert')
- in_new: float32 [16, 384, 1536], P('expert', None, 'batch')
- in_first_new: float32 [16, 384, 1536], P('expert', None, 'batch')
- in_second_new: float32 [16, 384, 1536], P('expert', None, 'batch')
- out_new: float32 [16, 1536, 384], P('expert', 'batch')
- out_first_new: float32 [16, 1536, 384], P('expert', 'batch')
- out_second_new: float32 [16, 1536, 384], P('expert', 'batch')
Inputs may be any that keep to these rules, and one draw needn't show every extreme that they name: `slot_len`: row r lists the images of device r (batch index times the size of expert plus expert index) in the order in which they lie in its buffer from its first row on; every length is 196 or 576, a row holds at most one of 576 and at least one image, unused slots are 0 and come last, and the buffer rows after the last image are padding. In every draw some row holds 5 images that fill all 1360 rows.
All inputs are finite; a program needn't handle non-finite values.
Results may differ from a plain program's by a relative error of at most 0.02.
The roundings to bfloat16 on the way count: a program that leaves them out, or rounds other values in their place, can miss the bound.
Values may be sent and summed in bfloat16 or wider, within the bound.
A program may use at most 256 MiB of HBM per device.

v0:
```python
import math

import jax
import jax.numpy as jnp
from jax import lax
from jax.sharding import PartitionSpec as P

D = 384
HEADS = 6
HEAD_DIM = 64
FF = 1536
STEP = 3


NORM_EPS = 1e-06
CLIP_NORM = 1.0
BETA_FIRST = 0.5
BETA_SECOND = 0.5
ADAM_EPS = 1e-08
WEIGHT_DECAY = 0.05
MASKED = -1e30


def layout(lengths, tokens_count):
    image_end = jnp.cumsum(lengths, dtype=jnp.int32)
    image_start = image_end - lengths
    position = jnp.arange(tokens_count, dtype=jnp.int32)
    inside = (position[None, :] >= image_start[:, None]) & (position[None, :] < image_end[:, None])
    member = inside.astype(jnp.float32)
    validity = jnp.sum(member, axis=0)
    numbers = jnp.arange(lengths.shape[0], dtype=jnp.int32)
    inside_int = inside.astype(jnp.int32)
    segment = jnp.sum(inside_int * numbers[:, None], axis=0, dtype=jnp.int32)
    segment = segment + lengths.shape[0] * (1 - jnp.sum(inside_int, axis=0, dtype=jnp.int32))
    return (member, validity, segment)


def normalize(values, scaling, offset):
    centred = values - jnp.mean(values, axis=-1, keepdims=True)
    variance = jnp.mean(centred * centred, axis=-1, keepdims=True)
    inverse = lax.rsqrt(variance + NORM_EPS)
    normed = centred * inverse
    return (normed, inverse, normed * scaling + offset)


def norm_back(grad_shaped, normed, inverse, scaling):
    grad_normed = grad_shaped * scaling
    grad_values = inverse * (
        grad_normed
        - jnp.mean(grad_normed, axis=-1, keepdims=True)
        - normed * jnp.mean(grad_normed * normed, axis=-1, keepdims=True)
    )
    return (grad_values, jnp.sum(grad_shaped * normed, axis=0), jnp.sum(grad_shaped, axis=0))


def row_softmax(scores):
    row_peak = jnp.max(scores, axis=-1, keepdims=True)
    exponent = jnp.exp(scores - row_peak)
    return exponent / jnp.sum(exponent, axis=-1, keepdims=True)


def dispatch_weights(logits, member):
    inside = member[:, :, None] > 0.5
    col_peak = jnp.max(jnp.where(inside, logits[None, :, :], MASKED), axis=1, keepdims=True)
    present = jnp.max(member, axis=1)[:, None, None]
    col_peak = jnp.where(present > 0.5, col_peak, 0.0)
    exponent = jnp.where(
        inside, jnp.exp(jnp.where(inside, logits[None, :, :] - col_peak, 0.0)), 0.0
    )
    col_total = jnp.sum(exponent, axis=1, keepdims=True) + (1.0 - present)
    return exponent / col_total


def block_scores(rows_query, key_heads, rows_segment, segment, score_scale):
    scores = (
        jnp.einsum("rhd,thd->hrt", rows_query, key_heads, preferred_element_type=jnp.float32)
        * score_scale
    )
    same = rows_segment[:, None] == segment[None, :]
    return jnp.where(same[None, :, :], scores, MASKED)


def adam_update(weight, first_moment, second_moment, gradient, factor, learning_rate, decay_rate):
    clipped = gradient * factor
    first_new = BETA_FIRST * first_moment + (1.0 - BETA_FIRST) * clipped
    second_new = BETA_SECOND * second_moment + (1.0 - BETA_SECOND) * clipped * clipped
    first_hat = first_new / (1.0 - BETA_FIRST**STEP)
    second_hat = second_new / (1.0 - BETA_SECOND**STEP)
    weight_new = weight - learning_rate * (
        first_hat / (jnp.sqrt(second_hat) + ADAM_EPS) + decay_rate * weight
    )
    return (weight_new, first_new, second_new)


def local(
    patches,
    slot_len,
    attn_weight,
    attn_first,
    attn_second,
    phi_weight,
    phi_first,
    phi_second,
    norm_params,
    norm_first,
    norm_second,
    expert_in,
    in_first,
    in_second,
    expert_out,
    out_first,
    out_second,
    cotangent,
):
    attn_full, phi_full, norm_full = (
        lax.all_gather(attn_weight.astype(jnp.bfloat16), "expert", axis=0, tiled=True),
        lax.all_gather(phi_weight.astype(jnp.bfloat16), "expert", axis=0, tiled=True),
        lax.all_gather(norm_params.astype(jnp.bfloat16), "expert", axis=1, tiled=True),
    )
    w_qkv = attn_full[:, : 3 * D]
    w_proj = attn_full[:, 3 * D :]
    norm_values = norm_full.astype(jnp.float32)
    gain_one = norm_values[0]
    bias_one = norm_values[1]
    gain_two = norm_values[2]
    bias_two = norm_values[3]
    tokens_count = patches.shape[0]
    half_rows = tokens_count // 2
    score_scale = HEAD_DIM ** (-0.5)
    member, validity, segment = layout(slot_len[0], tokens_count)
    inputs = patches.astype(jnp.float32)
    normed_one, inverse_one, shaped_one = normalize(inputs, gain_one, bias_one)
    hidden_one = shaped_one.astype(jnp.bfloat16)
    qkv_low = jnp.dot(hidden_one, w_qkv, preferred_element_type=jnp.float32).astype(jnp.bfloat16)
    query_heads = qkv_low[:, :D].reshape(tokens_count, HEADS, HEAD_DIM)
    key_heads = qkv_low[:, D : 2 * D].reshape(tokens_count, HEADS, HEAD_DIM)
    value_heads = qkv_low[:, 2 * D :].reshape(tokens_count, HEADS, HEAD_DIM)
    attended_blocks = []
    logsum_blocks = []
    for block_index in range(2):
        first_row = block_index * half_rows
        rows_query = query_heads[first_row : first_row + half_rows]
        scores = block_scores(
            rows_query, key_heads, segment[first_row : first_row + half_rows], segment, score_scale
        )
        row_peak = jnp.max(scores, axis=-1, keepdims=True)
        exponent = jnp.exp(scores - row_peak)
        row_total = jnp.sum(exponent, axis=-1, keepdims=True)
        attn_probs = (exponent / row_total).astype(jnp.bfloat16)
        block_out = jnp.einsum(
            "hrt,thd->rhd", attn_probs, value_heads, preferred_element_type=jnp.float32
        )
        attended_blocks.append(block_out.reshape(half_rows, D).astype(jnp.bfloat16))
        logsum_blocks.append(row_peak + jnp.log(row_total))
    attended = jnp.concatenate(attended_blocks, axis=0)
    residual = inputs + jnp.dot(attended, w_proj, preferred_element_type=jnp.float32)
    normed_two, inverse_two, shaped_two = normalize(residual, gain_two, bias_two)
    hidden_two = shaped_two.astype(jnp.bfloat16)
    logits = jnp.dot(hidden_two, phi_full, preferred_element_type=jnp.float32)
    dispatch = dispatch_weights(logits, member)
    dispatch_low = dispatch.astype(jnp.bfloat16)
    slot_in = jnp.einsum(
        "kte,td->ked", dispatch_low, hidden_two, preferred_element_type=jnp.float32
    ).astype(jnp.bfloat16)
    combine = row_softmax(logits)
    mix_weights = (member[:, :, None] * combine[None, :, :]).astype(jnp.bfloat16)
    expert_rows = lax.all_to_all(slot_in, "expert", split_axis=1, concat_axis=0, tiled=True)
    half_in = expert_in.astype(jnp.bfloat16)
    half_out = expert_out.astype(jnp.bfloat16)
    pair_rows = lax.all_gather(expert_rows, "batch", axis=0, tiled=True)
    pre_act = jnp.einsum("nsd,sdf->nsf", pair_rows, half_in, preferred_element_type=jnp.float32)
    activated = jax.nn.gelu(pre_act).astype(jnp.bfloat16)
    partial_result = jnp.einsum(
        "nsf,sfd->nsd", activated, half_out, preferred_element_type=jnp.float32
    )
    expert_result = lax.psum_scatter(
        partial_result.astype(jnp.bfloat16), "batch", scatter_dimension=0, tiled=True
    )
    returned = lax.all_to_all(expert_result, "expert", split_axis=0, concat_axis=1, tiled=True)
    mixture = jnp.einsum("kte,ked->td", mix_weights, returned, preferred_element_type=jnp.float32)
    block_output = (validity[:, None] * (residual + mixture)).astype(jnp.bfloat16)
    grad_output = cotangent.astype(jnp.float32) * validity[:, None]
    grad_mixture = grad_output.astype(jnp.bfloat16)
    per_image = jnp.einsum(
        "td,ked->kte", grad_mixture, returned, preferred_element_type=jnp.float32
    )
    grad_combine = jnp.sum(member[:, :, None] * per_image, axis=0)
    grad_returned = jnp.einsum(
        "kte,td->ked", mix_weights, grad_mixture, preferred_element_type=jnp.float32
    ).astype(jnp.bfloat16)
    grad_logits = combine * (grad_combine - jnp.sum(combine * grad_combine, axis=-1, keepdims=True))
    grad_rows = lax.all_to_all(grad_returned, "expert", split_axis=1, concat_axis=0, tiled=True)
    grad_pair = lax.all_gather(grad_rows, "batch", axis=0, tiled=True)
    pre_again = jnp.einsum("nsd,sdf->nsf", pair_rows, half_in, preferred_element_type=jnp.float32)
    act_again, gelu_back = jax.vjp(jax.nn.gelu, pre_again)
    act_low = act_again.astype(jnp.bfloat16)
    grad_act = jnp.einsum("nsd,sfd->nsf", grad_pair, half_out, preferred_element_type=jnp.float32)
    grad_pre = gelu_back(grad_act)[0].astype(jnp.bfloat16)
    grad_out_half = jnp.einsum(
        "nsf,nsd->sfd", act_low, grad_pair, preferred_element_type=jnp.float32
    )
    grad_in_half = jnp.einsum(
        "nsd,nsf->sdf", pair_rows, grad_pre, preferred_element_type=jnp.float32
    )
    partial_back = jnp.einsum("nsf,sdf->nsd", grad_pre, half_in, preferred_element_type=jnp.float32)
    grad_slots = lax.psum_scatter(
        partial_back.astype(jnp.bfloat16), "batch", scatter_dimension=0, tiled=True
    )
    grad_slot_in = lax.all_to_all(grad_slots, "expert", split_axis=0, concat_axis=1, tiled=True)
    grad_dispatch = jnp.einsum(
        "td,ked->kte", hidden_two, grad_slot_in, preferred_element_type=jnp.float32
    )
    grad_hidden_two = jnp.einsum(
        "kte,ked->td", dispatch_low, grad_slot_in, preferred_element_type=jnp.float32
    )
    grad_logits = grad_logits + jnp.sum(
        dispatch * (grad_dispatch - jnp.sum(dispatch * grad_dispatch, axis=1, keepdims=True)),
        axis=0,
    )
    logits_low = grad_logits.astype(jnp.bfloat16)
    grad_phi = jnp.einsum("td,te->de", hidden_two, logits_low, preferred_element_type=jnp.float32)
    grad_hidden_two = grad_hidden_two + jnp.einsum(
        "te,de->td", logits_low, phi_full, preferred_element_type=jnp.float32
    )
    grad_norm_two, grad_gain_two, grad_bias_two = norm_back(
        grad_hidden_two, normed_two, inverse_two, gain_two
    )
    grad_residual = grad_output + grad_norm_two
    branch_low = grad_residual.astype(jnp.bfloat16)
    grad_proj = jnp.einsum("td,te->de", attended, branch_low, preferred_element_type=jnp.float32)
    grad_attended = jnp.einsum("te,de->td", branch_low, w_proj, preferred_element_type=jnp.float32)
    grad_attended = grad_attended.astype(jnp.bfloat16).reshape(tokens_count, HEADS, HEAD_DIM)
    grad_keys = jnp.zeros((tokens_count, HEADS, HEAD_DIM), jnp.float32)
    grad_values = jnp.zeros((tokens_count, HEADS, HEAD_DIM), jnp.float32)
    query_blocks = []
    for block_index in range(2):
        first_row = block_index * half_rows
        rows_query = query_heads[first_row : first_row + half_rows]
        rows_grad = grad_attended[first_row : first_row + half_rows]
        scores = block_scores(
            rows_query, key_heads, segment[first_row : first_row + half_rows], segment, score_scale
        )
        attn_probs = jnp.exp(scores - logsum_blocks[block_index])
        grad_probs = jnp.einsum(
            "rhd,thd->hrt", rows_grad, value_heads, preferred_element_type=jnp.float32
        )
        row_inner = jnp.sum(attn_probs * grad_probs, axis=-1, keepdims=True)
        grad_scores = (attn_probs * (grad_probs - row_inner)).astype(jnp.bfloat16)
        query_blocks.append(
            jnp.einsum("hrt,thd->rhd", grad_scores, key_heads, preferred_element_type=jnp.float32)
            * score_scale
        )
        grad_keys = (
            grad_keys
            + jnp.einsum(
                "hrt,rhd->thd", grad_scores, rows_query, preferred_element_type=jnp.float32
            )
            * score_scale
        )
        grad_values = grad_values + jnp.einsum(
            "hrt,rhd->thd",
            attn_probs.astype(jnp.bfloat16),
            rows_grad,
            preferred_element_type=jnp.float32,
        )
    grad_qkv = jnp.concatenate(
        [
            jnp.concatenate(query_blocks, axis=0).reshape(tokens_count, D),
            grad_keys.reshape(tokens_count, D),
            grad_values.reshape(tokens_count, D),
        ],
        axis=1,
    ).astype(jnp.bfloat16)
    grad_w_qkv = jnp.einsum("td,tc->dc", hidden_one, grad_qkv, preferred_element_type=jnp.float32)
    grad_hidden_one = jnp.einsum("tc,dc->td", grad_qkv, w_qkv, preferred_element_type=jnp.float32)
    grad_norm_one, grad_gain_one, grad_bias_one = norm_back(
        grad_hidden_one, normed_one, inverse_one, gain_one
    )
    input_grad = (grad_residual + grad_norm_one).astype(jnp.bfloat16)
    grad_attn = jnp.concatenate([grad_w_qkv, grad_proj], axis=1)
    grad_norms = jnp.stack([grad_gain_one, grad_bias_one, grad_gain_two, grad_bias_two], axis=0)
    attn_part, phi_part, norm_part = (
        lax.psum_scatter(grad_attn, "expert", scatter_dimension=0, tiled=True),
        lax.psum_scatter(grad_phi, "expert", scatter_dimension=0, tiled=True),
        lax.psum_scatter(grad_norms, "expert", scatter_dimension=1, tiled=True),
    )
    attn_part, phi_part, norm_part = lax.psum((attn_part, phi_part, norm_part), "batch")
    expert_squares = jnp.sum(grad_in_half * grad_in_half) + jnp.sum(grad_out_half * grad_out_half)
    shared_squares = (
        jnp.sum(attn_part * attn_part)
        + jnp.sum(phi_part * phi_part)
        + jnp.sum(norm_part * norm_part)
    )
    last_copy = lax.axis_index("batch") == lax.axis_size("batch") - 1
    squares = expert_squares + jnp.where(last_copy, shared_squares, jnp.float32(0.0))
    grad_norm = jnp.sqrt(lax.psum(squares, ("batch", "expert")))
    factor = CLIP_NORM / jnp.maximum(grad_norm, CLIP_NORM)
    attn_new, attn_first_new, attn_second_new = adam_update(
        attn_weight, attn_first, attn_second, attn_part, factor, 1.0 / math.sqrt(D), WEIGHT_DECAY
    )
    phi_new, phi_first_new, phi_second_new = adam_update(
        phi_weight, phi_first, phi_second, phi_part, factor, 0.25 / math.sqrt(D), WEIGHT_DECAY
    )
    norm_new, norm_first_new, norm_second_new = adam_update(
        norm_params, norm_first, norm_second, norm_part, factor, 0.8, 0.0
    )
    in_new, in_first_new, in_second_new = adam_update(
        expert_in, in_first, in_second, grad_in_half, factor, 4.0 / math.sqrt(D), WEIGHT_DECAY
    )
    out_new, out_first_new, out_second_new = adam_update(
        expert_out, out_first, out_second, grad_out_half, factor, 8.0 / math.sqrt(FF), WEIGHT_DECAY
    )
    return (
        block_output,
        input_grad,
        grad_norm,
        attn_new,
        attn_first_new,
        attn_second_new,
        phi_new,
        phi_first_new,
        phi_second_new,
        norm_new,
        norm_first_new,
        norm_second_new,
        in_new,
        in_first_new,
        in_second_new,
        out_new,
        out_first_new,
        out_second_new,
    )


def solution(mesh):
    in_specs = (
        P(("batch", "expert"), None),
        P(("batch", "expert"), None),
        P("expert", None),
        P("expert", None),
        P("expert", None),
        P("expert", None),
        P("expert", None),
        P("expert", None),
        P(None, "expert"),
        P(None, "expert"),
        P(None, "expert"),
        P("expert", None, "batch"),
        P("expert", None, "batch"),
        P("expert", None, "batch"),
        P("expert", "batch", None),
        P("expert", "batch", None),
        P("expert", "batch", None),
        P(("batch", "expert"), None),
    )
    out_specs = (
        P(("batch", "expert"), None),
        P(("batch", "expert"), None),
        P(),
        P("expert", None),
        P("expert", None),
        P("expert", None),
        P("expert", None),
        P("expert", None),
        P("expert", None),
        P(None, "expert"),
        P(None, "expert"),
        P(None, "expert"),
        P("expert", None, "batch"),
        P("expert", None, "batch"),
        P("expert", None, "batch"),
        P("expert", "batch", None),
        P("expert", "batch", None),
        P("expert", "batch", None),
    )
    return jax.shard_map(local, mesh=mesh, in_specs=in_specs, out_specs=out_specs, check_vma=False)
```

profile of v0, /device:TPU:0, one launch (start us, length us, event | category | flops | bytes accessed | tf_op | source)
XLA Modules:
  0.0 597.8 jit_solution(7023342995462843690)
XLA Ops:
  14.3 42.4 %all-gather = bf16[16,24,4]{1,2,0:T(4,128)(2,1)S(1)} all-gather(bf16[1,24,4]{1,2,0:T(4,128)(2,1)S(1)} %convert_bitcast_fusion.1), channel_id=1, replica_groups=mesh['batch'=2,'expert'=16] {'expert'}, dimensions={0}, use_global_device_ids=true | all-gather | bytes 3264 | tf_op jit(solution)/shard_map/all_gather | solution.py:118
  56.8 35.9 %all-gather.1 = bf16[16,24,16]{1,2,0:T(8,128)(2,1)S(1)} all-gather(bf16[1,24,16]{1,2,0:T(8,128)(2,1)S(1)} %convert_bitcast_fusion), channel_id=1, replica_groups=mesh['batch'=2,'expert'=16] {'expert'}, dimensions={0}, use_global_device_ids=true | all-gather | bytes 13056 | tf_op jit(solution)/shard_map/all_gather | solution.py:117
  93.7 2.0 broadcast_compare_fusion.1
  95.7 3.3 convolution_convert_fusion
  102.5 2.1 copy.85
  104.5 2.1 copy.87
  108.4 12.0 %fusion.150 = (f32[6,680]{1,0:T(8,128)S(1)}, f32[6,680,1360]{2,1,0:T(8,128)}) fusion(bf16[680,6,64]{0,2,1:T(8,128)(2,1)} %bitcast.221, bf16[1360,6,64]{0,2,1:T(8,128)(2,1)S(1)} %bitcast.213, pred[680,1360]{1,0:T(8,128)(4,1)} %get-tuple-element.62), kind=kOutput, calls=%fused_computation.234 | convolution fusion | flops 726888704 | bytes 24703040 | tf_op jit(solution)/shard_map/rhd,thd->hrt/dot_general | solution.py:76
  120.4 9.9 %fusion.2 = f32[6,680]{1,0:T(8,128)S(1)} fusion(f32[6,680,1360]{2,1,0:T(8,128)} %get-tuple-element.68, f32[6,680]{1,0:T(8,128)S(1)} %get-tuple-element.67), kind=kLoop, calls=%fused_computation.14 | loop fusion | flops 11093520 | bytes 22227840 | tf_op jit(solution)/shard_map/reduce_sum | solution.py:148
  130.3 9.7 %fusion.42 = bf16[6,64,680]{2,1,0:T(8,128)(2,1)S(1)} fusion(bf16[1360,6,64]{0,2,1:T(8,128)(2,1)S(1)} %bitcast.217, f32[6,680,1360]{2,1,0:T(8,128)} %get-tuple-element.68, f32[6,680]{1,0:T(8,128)S(1)} %fusion.2, f32[6,680]{1,0:T(8,128)S(1)} %get-tuple-element.67), kind=kOutput, calls=%fused_computation.78 | convolution fusion | flops 727153920 | bytes 23794560 | tf_op jit(solution)/shard_map/hrt,thd->rhd/dot_general | solution.py:150
  140.1 10.0 %fusion.151 = (f32[6,680]{1,0:T(8,128)S(1)}, f32[6,680,1360]{2,1,0:T(8,128)}) fusion(bf16[680,6,64]{0,2,1:T(8,128)(2,1)S(1)} %bitcast.223, bf16[1360,6,64]{0,2,1:T(8,128)(2,1)S(1)} %bitcast.214, pred[680,1360]{1,0:T(8,128)(4,1)S(1)} %get-tuple-element.61), kind=kOutput, calls=%fused_computation.235 | convolution fusion | flops 726888704 | bytes 24703040 | tf_op jit(solution)/shard_map/rhd,thd->hrt/dot_general | solution.py:76
  150.1 10.1 %fusion.1 = f32[6,680]{1,0:T(8,128)S(1)} fusion(f32[6,680,1360]{2,1,0:T(8,128)} %get-tuple-element.70, f32[6,680]{1,0:T(8,128)S(1)} %get-tuple-element.69), kind=kLoop, calls=%fused_computation.13 | loop fusion | flops 11093520 | bytes 22227840 | tf_op jit(solution)/shard_map/reduce_sum | solution.py:148
  160.2 9.8 %fusion.43 = bf16[6,64,680]{2,1,0:T(8,128)(2,1)S(1)} fusion(bf16[1360,6,64]{0,2,1:T(8,128)(2,1)S(1)} %bitcast.218, f32[6,680,1360]{2,1,0:T(8,128)} %get-tuple-element.70, f32[6,680]{1,0:T(8,128)S(1)} %fusion.1, f32[6,680]{1,0:T(8,128)S(1)} %get-tuple-element.69), kind=kOutput, calls=%fused_computation.79 | convolution fusion | flops 727153920 | bytes 23794560 | tf_op jit(solution)/shard_map/hrt,thd->rhd/dot_general | solution.py:150
  170.0 2.3 fusion.152
  174.9 10.8 %all_to_all.72 = bf16[5,16,384]{2,0,1:T(8,128)(2,1)S(1)} all-to-all(bf16[5,16,384]{2,0,1:T(8,128)(2,1)S(1)} %copy.89), channel_id=1, replica_groups=mesh['batch'=2,'expert'=16] {'expert'}, dimensions={1} | all-to-all | bytes 122880 | tf_op jit(solution)/shard_map/all_to_all | solution.py:167
  185.8 2.0 all_gather.18
  191.2 4.6 reduce-scatter.6.cloned.1.call-done
  198.6 6.8 %all-to-all-start.1 = ((bf16[16,2,960]{2,1,0:T(2,128)(2,1)}), bf16[16,2,960]{2,1,0:T(2,128)(2,1)}, u32[]{:S(2)}, u32[]{:S(2)}) async-start(bf16[16,2,960]{2,1,0:T(2,128)(2,1)} %reshape.424), calls=%async_computation.2 | async-start | bytes 131072 | tf_op jit(solution)/shard_map/all_to_all | solution.py:179
  205.5 7.5 %all-to-all-done.1 = bf16[16,2,960]{2,1,0:T(2,128)(2,1)} async-done(((bf16[16,2,960]{2,1,0:T(2,128)(2,1)}), bf16[16,2,960]{2,1,0:T(2,128)(2,1)}, u32[]{:S(2)}, u32[]{:S(2)}) %all-to-all-start.1) | async-done | bytes 61472 | tf_op jit(solution)/shard_map/all_to_all | solution.py:179
  220.0 10.3 %all_to_all.73 = bf16[5,16,384]{2,0,1:T(8,128)(2,1)S(1)} all-to-all(bf16[5,16,384]{2,0,1:T(8,128)(2,1)S(1)} %copy.92), channel_id=1, replica_groups=mesh['batch'=2,'expert'=16] {'expert'}, dimensions={1} | all-to-all | bytes 122880 | tf_op jit(solution)/shard_map/all_to_all | solution.py:192
  230.3 2.0 all_gather.19
  233.0 1.9 fusion.82
  236.7 4.5 reduce-scatter.8.cloned.1.call-done
  243.4 6.8 %all-to-all-start.3 = ((bf16[16,2,960]{2,1,0:T(2,128)(2,1)}), bf16[16,2,960]{2,1,0:T(2,128)(2,1)}, u32[]{:S(2)}, u32[]{:S(2)}) async-start(bf16[16,2,960]{2,1,0:T(2,128)(2,1)} %reshape.426), calls=%async_computation.5 | async-start | bytes 131072 | tf_op jit(solution)/shard_map/all_to_all | solution.py:209
  251.5 6.4 %all-to-all-done.3 = bf16[16,2,960]{2,1,0:T(2,128)(2,1)} async-done(((bf16[16,2,960]{2,1,0:T(2,128)(2,1)}), bf16[16,2,960]{2,1,0:T(2,128)(2,1)}, u32[]{:S(2)}, u32[]{:S(2)}) %all-to-all-start.3) | async-done | bytes 61472 | tf_op jit(solution)/shard_map/all_to_all | solution.py:209
  272.3 2.1 copy.95
  274.4 14.7 %multiply_reduce_fusion.1 = (f32[6,680]{1,0:T(8,128)S(1)}, f32[6,680,1360]{2,1,0:T(8,128)}) fusion(f32[6,680,1360]{2,1,0:T(8,128)} %get-tuple-element.70, f32[6,680]{1,0:T(8,128)S(1)} %log_add_fusion.1, bf16[680,6,64]{0,2,1:T(8,128)(2,1)} %bitcast.225, bf16[1360,6,64]{0,2,1:T(8,128)(2,1)} %bitcast.219), kind=kOutput, calls=%fused_computation.5 | convolution fusion | flops 726888704 | bytes 45989760 | tf_op jit(solution)/shard_map/rhd,thd->hrt/dot_general | solution.py:244
  289.1 15.4 %multiply_convert_fusion.1 = bf16[6,680,1360]{2,1,0:T(8,128)(2,1)S(1)} fusion(f32[6,680,1360]{2,1,0:T(8,128)} %get-tuple-element.77, f32[6,680,1360]{2,1,0:T(8,128)} %get-tuple-element.70, f32[6,680]{1,0:T(8,128)S(1)} %get-tuple-element.76, f32[6,680]{1,0:T(8,128)S(1)} %log_add_fusion.1), kind=kLoop, calls=%fused_computation.4 | loop fusion | flops 22195200 | bytes 55520640 | tf_op jit(solution)/shard_map/convert_element_type | solution.py:248
  304.5 4.4 fusion.49
  308.9 3.4 fusion.155
  312.4 2.1 copy.96
  314.4 13.7 %fusion.5 = f32[6,64,1360]{2,1,0:T(8,128)} fusion(bf16[680,6,64]{0,2,1:T(8,128)(2,1)} %bitcast.227, f32[6,680,1360]{2,1,0:T(8,128)} %get-tuple-element.68, f32[6,680]{1,0:T(8,128)S(1)} %log_add_fusion), kind=kOutput, calls=%fused_computation.17 | convolution fusion | flops 721344000 | bytes 24822720 | tf_op jit(solution)/shard_map/hrt,rhd->thd/dot_general | solution.py:260
  328.2 18.3 %multiply_reduce_fusion = (f32[6,680]{1,0:T(8,128)S(1)}, f32[6,680,1360]{2,1,0:T(8,128)}) fusion(f32[6,680,1360]{2,1,0:T(8,128)} %get-tuple-element.68, f32[6,680]{1,0:T(8,128)S(1)} %log_add_fusion, bf16[680,6,64]{0,2,1:T(8,128)(2,1)S(1)} %bitcast.228, bf16[1360,6,64]{0,2,1:T(8,128)(2,1)S(1)} %bitcast.220), kind=kOutput, calls=%fused_computation.2 | convolution fusion | flops 726888704 | bytes 45989760 | tf_op jit(solution)/shard_map/rhd,thd->hrt/dot_general | solution.py:244
  346.5 11.7 %fusion.19 = bf16[6,64,1360]{2,1,0:T(8,128)(2,1)} fusion(f32[6,64,1360]{2,1,0:T(8,128)} %fusion.5, bf16[680,6,64]{0,2,1:T(8,128)(2,1)S(1)} %bitcast.226, f32[6,680,1360]{2,1,0:T(8,128)} %get-tuple-element.70, f32[6,680]{1,0:T(8,128)S(1)} %log_add_fusion.1), kind=kOutput, calls=%fused_computation.36 | convolution fusion | flops 722388480 | bytes 25867200 | tf_op jit(solution)/shard_map/hrt,rhd->thd/dot_general | solution.py:260
  358.2 15.2 %multiply_convert_fusion = bf16[6,680,1360]{2,1,0:T(8,128)(2,1)S(1)} fusion(f32[6,680,1360]{2,1,0:T(8,128)} %get-tuple-element.79, f32[6,680,1360]{2,1,0:T(8,128)} %get-tuple-element.68, f32[6,680]{1,0:T(8,128)S(1)} %get-tuple-element.78, f32[6,680]{1,0:T(8,128)S(1)} %log_add_fusion), kind=kLoop, calls=%fused_computation.1 | loop fusion | flops 22195200 | bytes 55520640 | tf_op jit(solution)/shard_map/convert_element_type | solution.py:248
  373.5 4.4 fusion.48
  377.8 3.8 fusion.23
  384.1 2.3 fusion.46
  391.6 2.0 multiply_reduce_fusion.8
  393.6 2.0 multiply_reduce_fusion.7
  397.0 6.4 %fusion.39 = (f32[384]{0:T(512)S(1)}, f32[1360]{0:T(1024)S(1)}, f32[1360]{0:T(1024)S(1)}, f32[384]{0:T(512)S(1)}, f32[1360,384]{1,0:T(8,128)}) fusion(bf16[1360,384]{1,0:T(8,128)(2,1)S(1)} %copy-done.11, f32[1360]{0:T(1024)S(1)} %copy-done.69, f32[1360]{0:T(1024)S(1)} %copy-done.62, f32[384]{0:T(512)S(1)} %copy-done.75, ...), kind=kOutput, calls=%fused_computation.58 | convolution fusion | flops 1217860096 | bytes 7288576 | tf_op jit(solution)/shard_map/tc,dc->td/dot_general | solution.py:275
  403.7 72.7 %all-reduce.2 = (f32[384,16]{0,1:T(8,128)S(1)}, f32[4,384]{1,0:T(4,128)S(1)}) all-reduce(f32[384,16]{0,1:T(8,128)S(1)} %fusion.156, f32[4,384]{1,0:T(4,128)S(1)} %pad_maximum_fusion.8), channel_id=5, replica_groups=mesh['batch'=2,'expert'=16] {'expert'}, use_global_device_ids=true, to_apply=%region_34.35.clone | all-reduce | flops 7680 | bytes 61440
  476.6 3.3 all-reduce.3
  479.9 32.8 %reduce-scatter.10.cloned.1.call-done = f32[24,1536]{1,0:T(8,128)} async-done(((f32[384,1536]{1,0:T(8,128)}), f32[24,1536]{1,0:T(8,128)}) %reduce-scatter.10.cloned.1.call-update) | async-done | bytes 147472 | tf_op jit(solution)/shard_map/reduce_scatter | solution.py:283
  514.0 18.2 %all-reduce.6.cloned.1.call-done = f32[24,1536]{1,0:T(8,128)} async-done(((f32[24,1536]{1,0:T(8,128)}), f32[24,1536]{1,0:T(8,128)}) %all-reduce.6.cloned.1.call-update) | async-done | bytes 147472 | tf_op jit(solution)/shard_map/psum | solution.py:287
  535.8 3.2 fusion.38
  538.9 40.5 %psum.31 = f32[]{:T(128)} all-reduce(f32[]{:T(128)S(6)} %add.245), channel_id=1, replica_groups=mesh['batch'=2,'expert'=16] {'batch','expert'}, use_global_device_ids=true, to_apply=%region_44.45 | all-reduce | flops 1 | bytes 8 | tf_op jit(solution)/shard_map/psum | solution.py:296
  581.4 4.9 multiply_subtract_fusion
  586.4 2.5 multiply_subtract_fusion.1
  (276 shorter events, 61.2 us)
Async XLA Ops:
  7.2 6.5 %copy-start.8 = (bf16[1360,384]{1,0:T(8,128)(2,1)S(1)}, bf16[1360,384]{1,0:T(8,128)(2,1)}, u32[]{:S(2)}) copy-start(bf16[1360,384]{1,0:T(8,128)(2,1)} %param.18) | copy-start | bytes 3133444
  7.2 88.5 %all-gather.4.cloned.1.call-start = ((), (), s32[]{:S(2)}) async-start(), calls=%async_computation.7 | async-start | bytes 1253376 | tf_op jit(solution)/shard_map/all_gather | solution.py:116
  8.9 186.9 %reduce-scatter.6.cloned.1.call-start = ((), (), s32[]{:S(2)}) async-start(), calls=%async_computation.8 | async-start | bytes 184320 | tf_op jit(solution)/shard_map/reduce_scatter | solution.py:176
  10.6 207.6 %copy-start.70 = (f32[1360]{0:T(1024)}, f32[1360]{0:T(1024)S(1)}, u32[]{:S(2)}) copy-start(f32[1360]{0:T(1024)S(1)} %get-tuple-element.31) | copy-start | bytes 16324
  13.7 85.3 %copy-start.61 = (f32[1360]{0:T(1024)}, f32[1360]{0:T(1024)S(1)}, u32[]{:S(2)}) copy-start(f32[1360]{0:T(1024)S(1)} %broadcast_multiply_fusion.5) | copy-start | bytes 16324
  56.8 42.2 %copy-start.74 = (f32[384]{0:T(512)}, f32[384]{0:T(512)S(1)}, u32[]{:S(2)}) copy-start(f32[384]{0:T(512)S(1)} %get-tuple-element.29) | copy-start | bytes 4612
  56.8 42.2 %copy-start.83 = (f32[384]{0:T(512)}, f32[384]{0:T(512)S(1)}, u32[]{:S(2)}) copy-start(f32[384]{0:T(512)S(1)} %get-tuple-element.28) | copy-start | bytes 4612
  56.8 116.0 %copy-start.66 = (f32[384]{0:T(512)}, f32[384]{0:T(512)S(1)}, u32[]{:S(2)}) copy-start(f32[384]{0:T(512)S(1)} %get-tuple-element.26) | copy-start | bytes 4612
  92.9 80.4 %copy-start.54 = (bf16[384,16]{0,1:T(8,128)(2,1)}, bf16[384,16]{0,1:T(8,128)(2,1)S(1)}, u32[]{:S(2)}) copy-start(bf16[384,16]{0,1:T(8,128)(2,1)S(1)} %reshape.406) | copy-start | bytes 36868
  93.0 6.0 %copy-start.68 = (f32[1360]{0:T(1024)}, f32[1360]{0:T(1024)S(1)}, u32[]{:S(2)}) copy-start(f32[1360]{0:T(1024)S(1)} %add_rsqrt_fusion.1) | copy-start | bytes 16324
  93.7 80.6 %copy-start.63 = (pred[5,1360]{1,0:T(8,128)(4,1)}, pred[5,1360]{1,0:T(8,128)(4,1)S(1)}, u32[]{:S(2)}) copy-start(pred[5,1360]{1,0:T(8,128)(4,1)S(1)} %get-tuple-element.65) | copy-start | bytes 20404
  108.3 51.8 %copy-start.6 = (bf16[1360,384]{0,1:T(8,128)(2,1)}, bf16[1360,384]{0,1:T(8,128)(2,1)S(1)}, u32[]{:S(2)}) copy-start(bf16[1360,384]{0,1:T(8,128)(2,1)S(1)} %copy.84) | copy-start | bytes 3133444
  120.4 9.9 %copy-start.44 = (f32[6,680]{1,0:T(8,128)}, f32[6,680]{1,0:T(8,128)S(1)}, u32[]{:S(2)}) copy-start(f32[6,680]{1,0:T(8,128)S(1)} %get-tuple-element.67) | copy-start | bytes 48964
  130.3 9.8 %copy-start.57 = (f32[6,680]{1,0:T(8,128)}, f32[6,680]{1,0:T(8,128)S(1)}, u32[]{:S(2)}) copy-start(f32[6,680]{1,0:T(8,128)S(1)} %fusion.2) | copy-start | bytes 48964
  130.3 9.8 %copy-start.13 = (bf16[680,384]{0,1:T(8,128)(2,1)S(1)}, bf16[680,384]{0,1:T(8,128)(2,1)}, u32[]{:S(2)}) copy-start(bf16[680,384]{0,1:T(8,128)(2,1)} %copy.85) | copy-start | bytes 1566724
  140.1 30.0 %copy-start.34 = (bf16[6,64,680]{2,1,0:T(8,128)(2,1)}, bf16[6,64,680]{2,1,0:T(8,128)(2,1)S(1)}, u32[]{:S(2)}) copy-start(bf16[6,64,680]{2,1,0:T(8,128)(2,1)S(1)} %fusion.42) | copy-start | bytes 1566724
  150.1 10.1 %copy-start.42 = (f32[6,680]{1,0:T(8,128)}, f32[6,680]{1,0:T(8,128)S(1)}, u32[]{:S(2)}) copy-start(f32[6,680]{1,0:T(8,128)S(1)} %get-tuple-element.69) | copy-start | bytes 48964
  160.2 9.8 %copy-start.56 = (f32[6,680]{1,0:T(8,128)}, f32[6,680]{1,0:T(8,128)S(1)}, u32[]{:S(2)}) copy-start(f32[6,680]{1,0:T(8,128)S(1)} %fusion.1) | copy-start | bytes 48964
  160.2 9.8 %copy-start.9 = (bf16[1360,384]{1,0:T(8,128)(2,1)S(1)}, bf16[1360,384]{1,0:T(8,128)(2,1)}, u32[]{:S(2)}) copy-start(bf16[1360,384]{1,0:T(8,128)(2,1)} %param.18) | copy-start | bytes 3133444
  185.8 4.4 copy-start.17
  198.6 14.4 %all-to-all-start.1 = ((bf16[16,2,960]{2,1,0:T(2,128)(2,1)}), bf16[16,2,960]{2,1,0:T(2,128)(2,1)}, u32[]{:S(2)}, u32[]{:S(2)}) async-start(bf16[16,2,960]{2,1,0:T(2,128)(2,1)} %reshape.424), calls=%async_computation.2 | async-start | bytes 131072 | tf_op jit(solution)/shard_map/all_to_all | solution.py:179
  205.4 35.8 %reduce-scatter.8.cloned.1.call-start = ((), (), s32[]{:S(2)}) async-start(), calls=%async_computation.9 | async-start | bytes 184320 | tf_op jit(solution)/shard_map/reduce_scatter | solution.py:206
  217.6 12.7 %copy-start.40 = (f32[16,1360]{1,0:T(8,128)}, f32[16,1360]{1,0:T(8,128)S(1)}, u32[]{:S(2)}) copy-start(f32[16,1360]{1,0:T(8,128)S(1)} %fusion.56) | copy-start | bytes 261124
  218.2 12.1 %copy-start.38 = (f32[1360,16]{0,1:T(8,128)}, f32[1360,16]{0,1:T(8,128)S(1)}, u32[]{:S(2)}) copy-start(f32[1360,16]{0,1:T(8,128)S(1)} %get-tuple-element.54) | copy-start | bytes 261124
  230.3 5.3 copy-start.4
  233.0 17.7 %copy-start.43 = (f32[6,680]{1,0:T(8,128)S(1)}, f32[6,680]{1,0:T(8,128)}, u32[]{:S(2)}) copy-start(f32[6,680]{1,0:T(8,128)} %copy-done.42) | copy-start | bytes 48964
  243.4 14.4 %all-to-all-start.3 = ((bf16[16,2,960]{2,1,0:T(2,128)(2,1)}), bf16[16,2,960]{2,1,0:T(2,128)(2,1)}, u32[]{:S(2)}, u32[]{:S(2)}) async-start(bf16[16,2,960]{2,1,0:T(2,128)(2,1)} %reshape.426), calls=%async_computation.5 | async-start | bytes 131072 | tf_op jit(solution)/shard_map/all_to_all | solution.py:209
  250.3 262.5 %reduce-scatter.10.cloned.1.call-start = ((), (), s32[]{:S(2)}) async-start(), calls=%async_computation.10 | async-start | bytes 2506752 | tf_op jit(solution)/shard_map/reduce_scatter | solution.py:283
  304.5 4.4 copy-start.14
  314.4 13.8 %copy-start.7 = (bf16[1360,384]{0,1:T(8,128)(2,1)S(1)}, bf16[1360,384]{0,1:T(8,128)(2,1)}, u32[]{:S(2)}) copy-start(bf16[1360,384]{0,1:T(8,128)(2,1)} %copy-done.6) | copy-start | bytes 3133444
  314.4 13.8 %copy-start.16 = (bf16[680,384]{0,1:T(8,128)(2,1)S(1)}, bf16[680,384]{0,1:T(8,128)(2,1)}, u32[]{:S(2)}) copy-start(bf16[680,384]{0,1:T(8,128)(2,1)} %copy.96) | copy-start | bytes 1566724
  328.2 18.3 %copy-start.15 = (bf16[680,384]{0,1:T(8,128)(2,1)S(1)}, bf16[680,384]{0,1:T(8,128)(2,1)}, u32[]{:S(2)}) copy-start(bf16[680,384]{0,1:T(8,128)(2,1)} %copy.95) | copy-start | bytes 1566724
  373.4 4.4 copy-start.12
  381.7 4.7 copy-start.27
  388.2 144.0 %all-reduce.6.cloned.1.call-start = ((), (), s32[]{:S(2)}) async-start(), calls=%async_computation.11 | async-start | bytes 294912 | tf_op jit(solution)/shard_map/psum | solution.py:287
  391.6 5.3 copy-start.11
  397.0 6.5 %copy-start.3 = (bf16[1360,384]{1,0:T(8,128)(2,1)S(1)}, bf16[1360,384]{1,0:T(8,128)(2,1)}, u32[]{:S(2)}) copy-start(bf16[1360,384]{1,0:T(8,128)(2,1)} %copy-done.2) | copy-start | bytes 3133444
  397.0 138.7 %copy-start.1 = (f32[1360,384]{1,0:T(8,128)S(1)}, f32[1360,384]{1,0:T(8,128)}, u32[]{:S(2)}) copy-start(f32[1360,384]{1,0:T(8,128)} %copy-done) | copy-start | bytes 6266884
  535.7 44.4 %copy-start.78 = (f32[4,24]{1,0:T(4,128)S(1)}, f32[4,24]{1,0:T(4,128)}, u32[]{:S(2)}) copy-start(f32[4,24]{1,0:T(4,128)} %param.26) | copy-start | bytes 1156
  535.7 44.4 %copy-start.85 = (f32[4,24]{1,0:T(4,128)S(1)}, f32[4,24]{1,0:T(4,128)}, u32[]{:S(2)}) copy-start(f32[4,24]{1,0:T(4,128)} %param.27) | copy-start | bytes 1156
  535.7 44.4 %copy-start.86 = (f32[4,24]{1,0:T(4,128)S(1)}, f32[4,24]{1,0:T(4,128)}, u32[]{:S(2)}) copy-start(f32[4,24]{1,0:T(4,128)} %param.28) | copy-start | bytes 1156
  535.7 45.0 %copy-start.73 = (f32[24,16]{0,1:T(8,128)S(1)}, f32[24,16]{0,1:T(8,128)}, u32[]{:S(2)}) copy-start(f32[24,16]{0,1:T(8,128)} %param.23) | copy-start | bytes 4612
  535.7 45.0 %copy-start.76 = (f32[24,16]{0,1:T(8,128)S(1)}, f32[24,16]{0,1:T(8,128)}, u32[]{:S(2)}) copy-start(f32[24,16]{0,1:T(8,128)} %param.24) | copy-start | bytes 4612
  535.8 45.0 %copy-start.77 = (f32[24,16]{0,1:T(8,128)S(1)}, f32[24,16]{0,1:T(8,128)}, u32[]{:S(2)}) copy-start(f32[24,16]{0,1:T(8,128)} %param.25) | copy-start | bytes 4612
  581.4 5.0 copy-start.5
  581.4 5.0 copy-start.18
  581.4 5.0 copy-start.24
  581.4 5.0 copy-start.25
  (47 other events, 91.6 us)
Sparse Core Ops, SparseCore 0:
  11.4 58.8 all-gather.3
  191.3 4.4 reduce-scatter.5
  236.7 4.4 reduce-scatter.7
  388.3 124.4 reduce-scatter.9
  515.0 17.0 all-reduce.5
where the time goes:
time: 609 us; the launch traced here: 598 us
  blocking collectives  220 us (36%)
  matrix products  154 us (25%)
  other arithmetic  87.2 us (14%)
  waiting for transfers between devices  74.1 us (12%)
  local copies, waits for them, and re-layouts  26.9 us (4%)
  between operations  21.3 us (3%)
  starting transfers between devices  14.5 us (2%)
    unnamed x1, blocking collectives  72.7 us
    all_gather x1, blocking collectives, local(): lax.all_gather(norm_params.astype(jnp.bfloat16), 'expert', axis=1, tiled=...  42.4 us
    psum x1, blocking collectives, local(): grad_norm = jnp.sqrt(lax.psum(squares, ('batch', 'expert')))  40.5 us
    all_gather x1, blocking collectives, local(): lax.all_gather(phi_weight.astype(jnp.bfloat16), 'expert', axis=0, tiled=T...  35.9 us
    dot_general x2, matrix products, local(): jnp.einsum('rhd,thd->hrt', rows_grad, value_heads, preferred_element_type...  33 us
    reduce_scatter x1, waiting for transfers between devices, local(): lax.psum_scatter(grad_attn, 'expert', scatter_dimension=0, tiled=True)  32.8 us
    convert_element_type x2, other arithmetic, local(): grad_scores = (attn_probs * (grad_probs - row_inner)).astype(jnp.bfloat16)  30.6 us
    dot_general x2, matrix products, local(): jnp.einsum('hrt,rhd->thd', attn_probs.astype(jnp.bfloat16), rows_grad, pr...  25.5 us
  transfers between devices with their start and end apart: 7, of which 6 were waited for; matrix products, arithmetic and copies ran while one was open for 4% of the time, Pallas kernels for 0%

commit v1 on v0

v1 whole, which is shorter than its diff:
```python
import functools
import math

import jax
import jax.numpy as jnp
from jax import lax
from jax.experimental import pallas as pl
from jax.experimental.pallas import tpu as pltpu
from jax.sharding import PartitionSpec as P

D = 384
HEADS = 6
HEAD_DIM = 64
FF = 1536
STEP = 3
SHORT_LEN = 196
LONG_LEN = 576
IMAGES = 5
SLOT_ROWS = 8
PAIRS = 3
GROUPS = 16
GROUP_ROWS = D // GROUPS

NORM_EPS = 1e-06
CLIP_NORM = 1.0
BETA_FIRST = 0.5
BETA_SECOND = 0.5
ADAM_EPS = 1e-08
WEIGHT_DECAY = 0.05
MASKED = -1e30
SCORE_SCALE = HEAD_DIM ** (-0.5)

MESH = pl.DeviceIdType.MESH
F32 = jnp.float32
BF16 = jnp.bfloat16
VMEM_BYTES = 58 * 1024 * 1024


def whole(count):
    return [pl.BlockSpec(memory_space=pltpu.VMEM)] * count


def round_up(value, unit):
    return -(-value // unit) * unit


def mm(left, right):
    return jnp.dot(left, right, preferred_element_type=F32)


def mm_nt(left, right):
    return lax.dot_general(left, right, (((1,), (1,)), ((), ())), preferred_element_type=F32)


def mm_tn(left, right):
    return lax.dot_general(left, right, (((0,), (0,)), ((), ())), preferred_element_type=F32)


def gather_kernel(experts, attn_ref, small_ref, main_out, small_out, stage, send_sem, recv_sem,
                  small_send, small_recv, pair_send, pair_recv):
    core = lax.axis_index("batch")
    me = lax.axis_index("expert")
    rows = attn_ref.shape[0]
    barrier = pltpu.get_barrier_semaphore()

    @pl.loop(1, experts)
    def _(j):
        peer = lax.rem(me + j, experts)
        pl.semaphore_signal(barrier, inc=1, device_id=(core, peer), device_id_type=MESH)

    pl.semaphore_signal(barrier, inc=1, device_id=(1 - core, me), device_id_type=MESH)
    if stage.shape[0] > 2 * rows:
        stage[...] = jnp.zeros_like(stage)
    first = pl.multiple_of(core * (2 * D), 128)
    stage[0:rows, :] = attn_ref[:, pl.ds(first, D)]
    stage[rows : 2 * rows, :] = attn_ref[:, pl.ds(first + D, D)]
    main_out[me, core] = stage[...].astype(BF16)
    small_out[me] = small_ref[...]
    pl.semaphore_wait(barrier, experts)

    def main_copy(j, block, peer):
        return pltpu.make_async_remote_copy(
            src_ref=main_out.at[block, core],
            dst_ref=main_out.at[block, core],
            send_sem=send_sem.at[j],
            recv_sem=recv_sem.at[j],
            device_id=(core, peer),
            device_id_type=MESH,
        )

    def small_copy(j, block, peer):
        return pltpu.make_async_remote_copy(
            src_ref=small_out.at[block],
            dst_ref=small_out.at[block],
            send_sem=small_send.at[j],
            recv_sem=small_recv.at[j],
            device_id=(core, peer),
            device_id_type=MESH,
        )

    def pair_copy(j, block, side):
        return pltpu.make_async_remote_copy(
            src_ref=main_out.at[block, side],
            dst_ref=main_out.at[block, side],
            send_sem=pair_send.at[j],
            recv_sem=pair_recv.at[j],
            device_id=(1 - core, me),
            device_id_type=MESH,
        )

    @pl.loop(1, experts)
    def _(j):
        peer = lax.rem(me + j, experts)
        main_copy(j, me, peer).start()
        small_copy(j, me, peer).start()

    pair_copy(0, me, core).start()

    @pl.loop(1, experts)
    def _(j):
        source = lax.rem(me - j + experts, experts)
        main_copy(j, source, source).wait_recv()
        pair_copy(j, source, core).start()

    @pl.loop(1, experts)
    def _(j):
        source = lax.rem(me - j + experts, experts)
        small_copy(j, source, source).wait_recv()
        main_copy(j, me, source).wait_send()
        small_copy(j, me, source).wait_send()

    @pl.loop(0, experts)
    def _(j):
        source = lax.rem(me - j + experts, experts)
        pair_copy(j, source, core).wait_send()
        pair_copy(j, source, 1 - core).wait_recv()


def gather_weights(attn_weight, small, experts):
    rows = attn_weight.shape[0]
    main_rows = round_up(2 * rows, 16)
    return pl.pallas_call(
        functools.partial(gather_kernel, experts),
        out_shape=(
            jax.ShapeDtypeStruct((experts, 2, main_rows, D), BF16),
            jax.ShapeDtypeStruct((experts,) + small.shape, BF16),
        ),
        in_specs=whole(2),
        out_specs=tuple(whole(2)),
        scratch_shapes=[pltpu.VMEM((main_rows, D), F32)]
        + [pltpu.SemaphoreType.DMA((experts,))] * 6,
        compiler_params=pltpu.CompilerParams(
            collective_id=0, has_side_effects=True, vmem_limit_bytes=VMEM_BYTES
        ),
        name="gather_weights",
    )(attn_weight, small)


def unpack_weight(main_ref, side, part):
    block = main_ref[:, side].astype(F32)[:, part * GROUP_ROWS : (part + 1) * GROUP_ROWS, :]
    return block.reshape(D, D).astype(BF16)


def unpack_small(small_ref, experts):
    lanes = small_ref.shape[2]
    columns = experts * SLOT_ROWS
    values = small_ref[...].astype(F32)[:, :GROUP_ROWS, :].reshape(D, lanes).astype(BF16)
    row = lax.broadcasted_iota(jnp.int32, (lanes, columns), 0)
    column = lax.broadcasted_iota(jnp.int32, (lanes, columns), 1)
    spread = jnp.where(row == column // SLOT_ROWS, 1.0, 0.0).astype(BF16)
    phi = mm(values, spread).astype(BF16)
    row = lax.broadcasted_iota(jnp.int32, (8, lanes), 0)
    column = lax.broadcasted_iota(jnp.int32, (8, lanes), 1)
    pick = jnp.where(column == row + experts, 1.0, 0.0).astype(BF16)
    return phi, mm_nt(pick, values)


def slot_bounds(len_ref, columns):
    image = lax.broadcasted_iota(jnp.int32, (1, columns), 1) % SLOT_ROWS
    starts = jnp.zeros((1, columns), jnp.int32)
    ends = jnp.zeros((1, columns), jnp.int32)
    start = jnp.int32(0)
    for k in range(IMAGES):
        end = start + len_ref[0, k]
        starts = jnp.where(image == k, start, starts)
        ends = jnp.where(image == k, end, ends)
        start = end
    return starts, ends, start


def normed(values):
    centred = values - jnp.mean(values, axis=-1, keepdims=True)
    variance = jnp.mean(centred * centred, axis=-1, keepdims=True)
    inverse = lax.rsqrt(variance + NORM_EPS)
    return centred * inverse, inverse


def norm_back(grad_shaped, normal, inverse, scaling):
    grad_normal = grad_shaped * scaling
    return inverse * (
        grad_normal
        - jnp.mean(grad_normal, axis=-1, keepdims=True)
        - normal * jnp.mean(grad_normal * normal, axis=-1, keepdims=True)
    )


def over_images(len_ref, tokens, body):
    def step(k, start):
        length = len_ref[0, k]
        for full in (SHORT_LEN, LONG_LEN):

            @pl.when(length == full)
            def _():
                window = round_up(full + 12, 16)
                first = jnp.minimum((start // 16) * 16, tokens - window)
                body(pl.multiple_of(first, 16), start - first, full, window)

        return start + length

    lax.fori_loop(0, IMAGES, step, jnp.int32(0))


def window_masks(shift, full, window):
    column = lax.broadcasted_iota(jnp.int32, (1, window), 1)
    row = lax.broadcasted_iota(jnp.int32, (window, 1), 0)
    bias = jnp.where((column >= shift) & (column < shift + full), 0.0, MASKED)
    inside = (row >= shift) & (row < shift + full)
    return bias, inside


def forward_kernel(experts, len_ref, patch_ref, main_ref, small_ref, cot_ref, qkv_ref, o_ref,
                   lse_ref, x1_ref, h2_ref, disp_ref, comb_ref, gy_ref, pack_ref, logit, packf):
    tokens = patch_ref.shape[0]
    columns = experts * SLOT_ROWS
    tile = tokens // 5
    phi, norms = unpack_small(small_ref, experts)
    starts, ends, total = slot_bounds(len_ref, columns)
    w_q, w_k = unpack_weight(main_ref, 0, 0), unpack_weight(main_ref, 0, 1)
    w_v = unpack_weight(main_ref, 1, 0)
    w_qkv = jnp.concatenate([w_q, w_k, w_v], axis=1)
    for t in range(5):
        rows = pl.ds(t * tile, tile)
        normal, _ = normed(patch_ref[rows, :].astype(F32))
        h1 = (normal * norms[0:1] + norms[1:2]).astype(BF16)
        qkv = mm(h1, w_qkv).astype(BF16)
        for c in range(9):
            qkv_ref[c, rows, :] = qkv[:, c * 128 : (c + 1) * 128]
    o_ref[...] = jnp.zeros_like(o_ref)
    lse_ref[...] = jnp.zeros_like(lse_ref)
    low_lane = lax.broadcasted_iota(jnp.int32, (1, 128), 1) < HEAD_DIM
    lane = lax.broadcasted_iota(jnp.int32, (1, 128), 1)

    def attend(first, shift, full, window):
        bias, inside = window_masks(shift, full, window)
        rows = pl.ds(first, window)

        @pl.loop(0, PAIRS)
        def _(p):
            query = qkv_ref[p, rows, :].astype(F32) * SCORE_SCALE
            keys = qkv_ref[PAIRS + p, rows, :]
            values = qkv_ref[2 * PAIRS + p, rows, :]
            outs = []
            sums = lse_ref[rows, :]
            for h in range(2):
                mine = low_lane if h == 0 else jnp.logical_not(low_lane)
                scores = mm_nt(jnp.where(mine, query, 0.0).astype(BF16), keys) + bias
                peak = jnp.max(scores, axis=-1, keepdims=True)
                exponent = jnp.exp(scores - peak)
                summed = jnp.sum(exponent, axis=-1, keepdims=True)
                probs = (exponent * (1.0 / summed)).astype(BF16)
                outs.append(mm(probs, values))
                sums = jnp.where(inside & (lane == 2 * p + h), peak + jnp.log(summed), sums)
            lse_ref[rows, :] = sums
            lanes = pl.ds(pl.multiple_of(p * 128, 128), 128)
            old = o_ref[rows, lanes].astype(F32)
            merged = jnp.where(inside, jnp.where(low_lane, outs[0], outs[1]), old)
            o_ref[rows, lanes] = merged.astype(BF16)

    over_images(len_ref, tokens, attend)

    w_o = unpack_weight(main_ref, 1, 1)
    for t in range(5):
        rows = pl.ds(t * tile, tile)
        x1 = patch_ref[rows, :].astype(F32) + mm(o_ref[rows, :], w_o)
        normal, _ = normed(x1)
        h2 = (normal * norms[2:3] + norms[3:4]).astype(BF16)
        h2_ref[rows, :] = h2
        logit[rows, :] = mm(h2, phi)
        position = t * tile + lax.broadcasted_iota(jnp.int32, (tile, 1), 0)
        valid = position < total
        x1_ref[rows, :] = jnp.where(valid, x1, 0.0)
        gy_ref[rows, :] = jnp.where(valid, cot_ref[rows, :].astype(F32), 0.0).astype(BF16)

    position = lax.broadcasted_iota(jnp.int32, (tokens, columns), 0)
    member = (position >= starts) & (position < ends)
    present = ends > starts
    logits = logit[...]
    peak = jnp.max(jnp.where(member, logits, MASKED), axis=0, keepdims=True)
    peak = jnp.where(present, peak, 0.0)
    exponent = jnp.where(member, jnp.exp(jnp.where(member, logits - peak, 0.0)), 0.0)
    summed = jnp.sum(exponent, axis=0, keepdims=True) + jnp.where(present, 0.0, 1.0)
    dispatch = exponent / summed
    disp_ref[...] = dispatch
    slots = mm_tn(dispatch.astype(BF16), h2_ref[...])
    row_peak = jnp.max(logits, axis=-1, keepdims=True)
    exponent = jnp.exp(logits - row_peak)
    summed = jnp.sum(exponent, axis=-1, keepdims=True) * (1.0 / SLOT_ROWS)
    combine = jnp.where(member, exponent / summed, 0.0)
    comb_ref[...] = combine
    grad_result = mm_tn(combine.astype(BF16), gy_ref[...])
    for part, matrix in enumerate((slots, grad_result)):
        pack_rows(packf, matrix.reshape(experts, SLOT_ROWS, D))
        pack_ref[:, part * 16 : (part + 1) * 16, :] = packf[...].astype(BF16)


def pack_rows(packf, blocks):
    packf[...] = jnp.zeros_like(packf)
    for c in range(3):
        packf[:, c * IMAGES : (c + 1) * IMAGES, :] = blocks[:, :IMAGES, c * 128 : (c + 1) * 128]


def unpack_rows(packf, wide):
    wide[...] = jnp.zeros_like(wide)
    for c in range(3):
        wide[:, 0:IMAGES, c * 128 : (c + 1) * 128] = packf[:, c * IMAGES : (c + 1) * IMAGES, :]


def forward_local(lengths, patches, main, small, cotangent, experts):
    tokens = patches.shape[0]
    columns = experts * SLOT_ROWS
    shape = jax.ShapeDtypeStruct
    return pl.pallas_call(
        functools.partial(forward_kernel, experts),
        out_shape=(
            shape((9, tokens, 128), BF16),
            shape((tokens, D), BF16),
            shape((tokens, 128), F32),
            shape((tokens, D), F32),
            shape((tokens, D), BF16),
            shape((tokens, columns), F32),
            shape((tokens, columns), F32),
            shape((tokens, D), BF16),
            shape((experts, 32, 128), BF16),
        ),
        in_specs=[pl.BlockSpec(memory_space=pltpu.SMEM)] + whole(4),
        out_specs=tuple(whole(9)),
        scratch_shapes=[pltpu.VMEM((tokens, columns), F32), pltpu.VMEM((experts, 16, 128), F32)],
        compiler_params=pltpu.CompilerParams(vmem_limit_bytes=VMEM_BYTES),
        name="forward_local",
    )(lengths, patches, main, small, cotangent)


def expert_kernel(experts, pack_ref, in_ref, out_ref, result_ref, gslot_ref, gin_ref, gout_ref,
                  square_ref, inbox, outbox, back, packf, wide, packe, widee, send_one, recv_one,
                  send_two, recv_two):
    core = lax.axis_index("batch")
    chip = lax.axis_index("expert")
    devices = 2 * experts
    me = core * experts + chip
    barrier = pltpu.get_barrier_semaphore()

    @pl.loop(1, devices)
    def _(j):
        peer = lax.rem(me + j, devices)
        pl.semaphore_signal(
            barrier, inc=1, device_id=(peer // experts, lax.rem(peer, experts)), device_id_type=MESH
        )

    w_in = in_ref[0].astype(BF16)
    w_out = out_ref[0].astype(BF16)
    inbox[me] = pack_ref[chip]
    pl.semaphore_wait(barrier, devices - 1)

    def first(j, peer):
        return pltpu.make_async_remote_copy(
            src_ref=pack_ref.at[lax.rem(peer, experts)],
            dst_ref=inbox.at[me],
            send_sem=send_one.at[j],
            recv_sem=recv_one.at[j],
            device_id=(peer // experts, lax.rem(peer, experts)),
            device_id_type=MESH,
        )

    def first_arrival(j, peer):
        return pltpu.make_async_remote_copy(
            src_ref=pack_ref.at[lax.rem(peer, experts)],
            dst_ref=inbox.at[peer],
            send_sem=send_one.at[j],
            recv_sem=recv_one.at[j],
            device_id=(peer // experts, lax.rem(peer, experts)),
            device_id_type=MESH,
        )

    def second(j, peer):
        return pltpu.make_async_remote_copy(
            src_ref=outbox.at[peer],
            dst_ref=back.at[me],
            send_sem=send_two.at[j],
            recv_sem=recv_two.at[j],
            device_id=(peer // experts, lax.rem(peer, experts)),
            device_id_type=MESH,
        )

    def second_arrival(j, peer):
        return pltpu.make_async_remote_copy(
            src_ref=outbox.at[peer],
            dst_ref=back.at[peer],
            send_sem=send_two.at[j],
            recv_sem=recv_two.at[j],
            device_id=(peer // experts, lax.rem(peer, experts)),
            device_id_type=MESH,
        )

    @pl.loop(1, devices)
    def _(j):
        first(j, lax.rem(me + j, devices)).start()

    @pl.loop(1, devices)
    def _(j):
        first_arrival(j, lax.rem(me - j + devices, devices)).wait_recv()

    rows = devices * SLOT_ROWS
    packf[...] = inbox[:, 0:16, :].astype(F32)
    unpack_rows(packf, wide)
    slots = wide[...].reshape(rows, D).astype(BF16)
    packf[...] = inbox[:, 16:32, :].astype(F32)
    unpack_rows(packf, wide)
    grads = wide[...].reshape(rows, D).astype(BF16)

    hidden = mm(slots, w_in)
    cubed = hidden * hidden * hidden
    root = math.sqrt(2.0 / math.pi)
    bent = jnp.tanh(root * (hidden + 0.044715 * cubed))
    half = 0.5 * (1.0 + bent)
    act = (hidden * half).astype(BF16)
    slope = half + 0.5 * hidden * (1.0 - bent * bent) * (
        root * (1.0 + 3.0 * 0.044715 * (hidden * hidden))
    )
    result = mm(act, w_out)
    pack_rows(packf, result.reshape(devices, SLOT_ROWS, D))
    outbox[:, 0:16, :] = packf[...].astype(BF16)
    grad_hidden = (mm_nt(grads, w_out) * slope).astype(BF16)
    grad_slots = mm_nt(grad_hidden, w_in)
    pack_rows(packf, grad_slots.reshape(devices, SLOT_ROWS, D))
    outbox[:, 16:32, :] = packf[...].astype(BF16)
    back[me] = outbox[me]

    @pl.loop(1, devices)
    def _(j):
        second(j, lax.rem(me + j, devices)).start()

    grad_out = mm_tn(act, grads)
    gout_ref[0] = grad_out
    grad_in = mm_tn(slots, grad_hidden)
    gin_ref[0] = grad_in
    squares = jnp.sum(grad_out * grad_out) + jnp.sum(grad_in * grad_in)
    square_ref[...] = jnp.full(square_ref.shape, squares, F32)

    @pl.loop(1, devices)
    def _(j):
        second_arrival(j, lax.rem(me - j + devices, devices)).wait_recv()

    for part, target in enumerate((result_ref, gslot_ref)):
        block = slice(part * 16, (part + 1) * 16)
        both = back[0:experts, block, :].astype(F32) + back[experts:devices, block, :].astype(F32)
        packe[...] = both.astype(BF16).astype(F32)
        unpack_rows(packe, widee)
        target[...] = widee[...].reshape(experts * SLOT_ROWS, D).astype(BF16)

    @pl.loop(1, devices)
    def _(j):
        peer = lax.rem(me + j, devices)
        first(j, peer).wait_send()
        second(j, peer).wait_send()


def run_experts(packed, expert_in, expert_out, experts):
    devices = 2 * experts
    shape = jax.ShapeDtypeStruct
    return pl.pallas_call(
        functools.partial(expert_kernel, experts),
        out_shape=(
            shape((experts * SLOT_ROWS, D), BF16),
            shape((experts * SLOT_ROWS, D), BF16),
            shape(expert_in.shape, F32),
            shape(expert_out.shape, F32),
            shape((8, 128), F32),
        ),
        in_specs=whole(3),
        out_specs=tuple(whole(5)),
        scratch_shapes=[
            pltpu.VMEM((devices, 32, 128), BF16),
            pltpu.VMEM((devices, 32, 128), BF16),
            pltpu.VMEM((devices, 32, 128), BF16),
            pltpu.VMEM((devices, 16, 128), F32),
            pltpu.VMEM((devices, SLOT_ROWS, D), F32),
            pltpu.VMEM((experts, 16, 128), F32),
            pltpu.VMEM((experts, SLOT_ROWS, D), F32),
        ]
        + [pltpu.SemaphoreType.DMA((devices,))] * 4,
        compiler_params=pltpu.CompilerParams(
            collective_id=1, has_side_effects=True, vmem_limit_bytes=VMEM_BYTES
        ),
        name="run_experts",
    )(packed, expert_in, expert_out)


def backward_kernel(experts, len_ref, patch_ref, main_ref, small_ref, qkv_ref, o_ref, lse_ref,
                    x1_ref, h2_ref, disp_ref, comb_ref, gy_ref, result_ref, gslot_ref, block_ref,
                    input_ref, gw_ref, gphi_ref, gnorm_ref, gdisp, glog, gx1, branch, go, gqkv,
                    h1_all):
    tokens = patch_ref.shape[0]
    columns = experts * SLOT_ROWS
    tile = tokens // 5
    phi, norms = unpack_small(small_ref, experts)
    result = result_ref[...]
    gslots = gslot_ref[...]

    inner = jnp.zeros((1, columns), F32)
    for t in range(5):
        rows = pl.ds(t * tile, tile)
        grad_dispatch = mm_nt(h2_ref[rows, :], gslots)
        gdisp[rows, :] = grad_dispatch
        inner = inner + jnp.sum(disp_ref[rows, :] * grad_dispatch, axis=0, keepdims=True)

    w_o = unpack_weight(main_ref, 1, 1)
    gain_two = jnp.zeros((1, D), F32)
    bias_two = jnp.zeros((1, D), F32)
    for t in range(5):
        rows = pl.ds(t * tile, tile)
        dispatch, combine, gy = disp_ref[rows, :], comb_ref[rows, :], gy_ref[rows, :]
        x1 = x1_ref[rows, :]
        mixed = mm(combine.astype(BF16), result)
        block_ref[rows, :] = (x1 + mixed).astype(BF16)
        weighted = combine * mm_nt(gy, result)
        grad_logits = (
            weighted
            - combine * jnp.sum(weighted, axis=-1, keepdims=True)
            + dispatch * (gdisp[rows, :] - inner)
        ).astype(BF16)
        glog[rows, :] = grad_logits
        grad_h2 = mm(dispatch.astype(BF16), gslots) + mm_nt(grad_logits, phi)
        normal, inverse = normed(x1)
        gain_two = gain_two + jnp.sum(grad_h2 * normal, axis=0, keepdims=True)
        bias_two = bias_two + jnp.sum(grad_h2, axis=0, keepdims=True)
        grad_x1 = gy.astype(F32) + norm_back(grad_h2, normal, inverse, norms[2:3])
        gx1[rows, :] = grad_x1
        grad_branch = grad_x1.astype(BF16)
        branch[rows, :] = grad_branch
        grad_o = mm_nt(grad_branch, w_o).astype(BF16)
        for c in range(PAIRS):
            go[c, rows, :] = grad_o[:, c * 128 : (c + 1) * 128]

    lanes = gphi_ref.shape[1]
    row = lax.broadcasted_iota(jnp.int32, (columns, lanes), 0)
    column = lax.broadcasted_iota(jnp.int32, (columns, lanes), 1)
    fold = jnp.where(column == row // SLOT_ROWS, 1.0, 0.0).astype(BF16)
    folded = mm(glog[...], fold).astype(BF16)
    gphi_ref[...] = mm_tn(h2_ref[...], folded)

    def put(side, part, value):
        gw_ref[side, :, part * GROUP_ROWS : (part + 1) * GROUP_ROWS, :] = value.reshape(
            GROUPS, GROUP_ROWS, D
        )

    put(1, 1, mm_tn(o_ref[...], branch[...]))

    gqkv[...] = jnp.zeros_like(gqkv)
    low_lane = lax.broadcasted_iota(jnp.int32, (1, 128), 1) < HEAD_DIM
    lane = lax.broadcasted_iota(jnp.int32, (1, 128), 1)

    def attend(first, shift, full, window):
        bias, inside = window_masks(shift, full, window)
        rows = pl.ds(first, window)
        sums = lse_ref[rows, :]

        @pl.loop(0, PAIRS)
        def _(p):
            query_low = qkv_ref[p, rows, :]
            query = query_low.astype(F32) * SCORE_SCALE
            keys = qkv_ref[PAIRS + p, rows, :]
            values = qkv_ref[2 * PAIRS + p, rows, :]
            grads_low = go[p, rows, :]
            grads = grads_low.astype(F32)
            parts = []
            for h in range(2):
                mine = low_lane if h == 0 else jnp.logical_not(low_lane)
                scores = mm_nt(jnp.where(mine, query, 0.0).astype(BF16), keys) + bias
                summed = jnp.sum(jnp.where(lane == 2 * p + h, sums, 0.0), axis=-1, keepdims=True)
                probs = jnp.exp(scores - jnp.where(inside, summed, 1e30))
                grad_probs = mm_nt(jnp.where(mine, grads, 0.0).astype(BF16), values)
                dot = jnp.sum(probs * grad_probs, axis=-1, keepdims=True)
                grad_scores = (probs * (grad_probs - dot)).astype(BF16)
                parts.append(
                    (
                        mm(grad_scores, keys) * SCORE_SCALE,
                        mm_tn(grad_scores, query_low) * SCORE_SCALE,
                        mm_tn(probs.astype(BF16), grads_low),
                    )
                )
            for c in range(3):
                old = gqkv[c * PAIRS + p, rows, :].astype(F32)
                new = jnp.where(low_lane, parts[0][c], parts[1][c])
                gqkv[c * PAIRS + p, rows, :] = jnp.where(inside, new, old).astype(BF16)

    over_images(len_ref, tokens, attend)

    w_q, w_k = unpack_weight(main_ref, 0, 0), unpack_weight(main_ref, 0, 1)
    w_v = unpack_weight(main_ref, 1, 0)
    w_qkv = jnp.concatenate([w_q, w_k, w_v], axis=1)
    gain_one = jnp.zeros((1, D), F32)
    bias_one = jnp.zeros((1, D), F32)
    for t in range(5):
        rows = pl.ds(t * tile, tile)
        grad_qkv = jnp.concatenate([gqkv[c, rows, :] for c in range(9)], axis=1)
        grad_h1 = mm_nt(grad_qkv, w_qkv)
        normal, inverse = normed(patch_ref[rows, :].astype(F32))
        h1_all[rows, :] = (normal * norms[0:1] + norms[1:2]).astype(BF16)
        gain_one = gain_one + jnp.sum(grad_h1 * normal, axis=0, keepdims=True)
        bias_one = bias_one + jnp.sum(grad_h1, axis=0, keepdims=True)
        grad_x = gx1[rows, :] + norm_back(grad_h1, normal, inverse, norms[0:1])
        input_ref[rows, :] = grad_x.astype(BF16)
    for c, (side, part) in enumerate(((0, 0), (0, 1), (1, 0))):
        grad = jnp.concatenate([gqkv[c * PAIRS + p] for p in range(PAIRS)], axis=1)
        put(side, part, mm_tn(h1_all[...], grad))
    gnorm_ref[...] = jnp.concatenate(
        [gain_one, bias_one, gain_two, bias_two, jnp.zeros((4, D), F32)], axis=0
    )


def backward_local(lengths, patches, main, small, saved, result, gslots, experts):
    tokens = patches.shape[0]
    columns = experts * SLOT_ROWS
    shape = jax.ShapeDtypeStruct
    return pl.pallas_call(
        functools.partial(backward_kernel, experts),
        out_shape=(
            shape((tokens, D), BF16),
            shape((tokens, D), BF16),
            shape((2, GROUPS, 2 * GROUP_ROWS, D), F32),
            shape((D, round_up(experts, 128)), F32),
            shape((8, D), F32),
        ),
        in_specs=[pl.BlockSpec(memory_space=pltpu.SMEM)] + whole(13),
        out_specs=tuple(whole(5)),
        scratch_shapes=[
            pltpu.VMEM((tokens, columns), F32),
            pltpu.VMEM((tokens, columns), BF16),
            pltpu.VMEM((tokens, D), F32),
            pltpu.VMEM((tokens, D), BF16),
            pltpu.VMEM((PAIRS, tokens, 128), BF16),
            pltpu.VMEM((9, tokens, 128), BF16),
            pltpu.VMEM((tokens, D), BF16),
        ],
        compiler_params=pltpu.CompilerParams(vmem_limit_bytes=VMEM_BYTES),
        name="backward_local",
    )(lengths, patches, main, small, *saved, result, gslots)


def reduce_kernel(experts, gw_ref, gs_ref, square_ref, main_out, small_out, norm_ref, pair_in,
                  pair_small, box, small_box, inbox, small_in, scalars, pair_send, pair_recv,
                  pair_small_send, pair_small_recv, send_sem, recv_sem, small_send, small_recv,
                  swap_sem, norm_send, norm_recv):
    core = lax.axis_index("batch")
    chip = lax.axis_index("expert")
    devices = 2 * experts
    me = core * experts + chip
    barrier = pltpu.get_barrier_semaphore()

    @pl.loop(1, devices)
    def _(j):
        peer = lax.rem(me + j, devices)
        pl.semaphore_signal(
            barrier, inc=1, device_id=(peer // experts, lax.rem(peer, experts)), device_id_type=MESH
        )

    pl.semaphore_wait(barrier, devices - 1)

    def pair_copy(target):
        return pltpu.make_async_remote_copy(
            src_ref=gw_ref.at[1 - core, target],
            dst_ref=pair_in.at[target],
            send_sem=pair_send.at[target],
            recv_sem=pair_recv.at[target],
            device_id=(1 - core, chip),
            device_id_type=MESH,
        )

    def pair_small_copy(target):
        return pltpu.make_async_remote_copy(
            src_ref=gs_ref.at[target],
            dst_ref=pair_small.at[target],
            send_sem=pair_small_send.at[target],
            recv_sem=pair_small_recv.at[target],
            device_id=(1 - core, chip),
            device_id_type=MESH,
        )

    def main_copy(j, block, peer):
        return pltpu.make_async_remote_copy(
            src_ref=box.at[peer],
            dst_ref=inbox.at[block],
            send_sem=send_sem.at[j],
            recv_sem=recv_sem.at[j],
            device_id=(core, peer),
            device_id_type=MESH,
        )

    def small_copy(j, block, peer):
        return pltpu.make_async_remote_copy(
            src_ref=small_box.at[peer],
            dst_ref=small_in.at[block],
            send_sem=small_send.at[j],
            recv_sem=small_recv.at[j],
            device_id=(core, peer),
            device_id_type=MESH,
        )

    @pl.loop(1, experts + 1)
    def _(j):
        target = lax.rem(chip + j, experts)
        pair_copy(target).start()
        pair_small_copy(target).start()

    @pl.loop(1, experts)
    def _(j):
        target = lax.rem(chip + j, experts)
        pair_copy(target).wait_recv()
        box[target] = (gw_ref[core, target] + pair_in[target]).astype(BF16)
        main_copy(j, chip, target).start()
        pair_small_copy(target).wait_recv()
        small_box[target] = (gs_ref[target] + pair_small[target]).astype(BF16)
        small_copy(j, chip, target).start()

    pair_copy(chip).wait_recv()
    pair_small_copy(chip).wait_recv()
    main_out[core] = gw_ref[core, chip] + pair_in[chip]
    small_out[...] = gs_ref[chip] + pair_small[chip]

    @pl.loop(1, experts)
    def _(j):
        source = lax.rem(chip - j + experts, experts)
        main_copy(j, source, source).wait_recv()
        main_out[core] += inbox[source].astype(F32)
        small_copy(j, source, source).wait_recv()
        small_out[...] += small_in[source].astype(F32)

    def swap(side):
        return pltpu.make_async_remote_copy(
            src_ref=main_out.at[side],
            dst_ref=main_out.at[side],
            send_sem=swap_sem.at[0],
            recv_sem=swap_sem.at[1],
            device_id=(1 - core, chip),
            device_id_type=MESH,
        )

    swap(core).start()
    own = main_out[core]
    shared = small_out[...]
    small_square = jnp.where(core == 0, jnp.sum(shared * shared), 0.0)
    squares = jnp.sum(own * own) + small_square
    scalars[me] = square_ref[...] + squares

    def norm_copy(j, block, peer):
        return pltpu.make_async_remote_copy(
            src_ref=scalars.at[block],
            dst_ref=scalars.at[block],
            send_sem=norm_send.at[j],
            recv_sem=norm_recv.at[j],
            device_id=(peer // experts, lax.rem(peer, experts)),
            device_id_type=MESH,
        )

    @pl.loop(1, devices)
    def _(j):
        norm_copy(j, me, lax.rem(me + j, devices)).start()

    @pl.loop(1, devices)
    def _(j):
        source = lax.rem(me - j + devices, devices)
        norm_copy(j, source, source).wait_recv()

    norm_ref[...] = jnp.sqrt(jnp.sum(scalars[...], axis=0))
    swap(1 - core).wait_recv()
    swap(core).wait_send()

    @pl.loop(1, experts + 1)
    def _(j):
        target = lax.rem(chip + j, experts)
        pair_copy(target).wait_send()
        pair_small_copy(target).wait_send()

    @pl.loop(1, experts)
    def _(j):
        target = lax.rem(chip + j, experts)
        main_copy(j, chip, target).wait_send()
        small_copy(j, chip, target).wait_send()

    @pl.loop(1, devices)
    def _(j):
        norm_copy(j, me, lax.rem(me + j, devices)).wait_send()


def reduce_grads(main, small, squares, experts):
    devices = 2 * experts
    block = main.shape[2:]
    part = small.shape[1:]
    shape = jax.ShapeDtypeStruct
    dma = pltpu.SemaphoreType.DMA
    return pl.pallas_call(
        functools.partial(reduce_kernel, experts),
        out_shape=(shape((2,) + block, F32), shape(part, F32), shape((8, 128), F32)),
        in_specs=whole(3),
        out_specs=tuple(whole(3)),
        scratch_shapes=[
            pltpu.VMEM((experts,) + block, F32),
            pltpu.VMEM((experts,) + part, F32),
            pltpu.VMEM((experts,) + block, BF16),
            pltpu.VMEM((experts,) + part, BF16),
            pltpu.VMEM((experts,) + block, BF16),
            pltpu.VMEM((experts,) + part, BF16),
            pltpu.VMEM((devices, 8, 128), F32),
        ]
        + [dma((experts,))] * 8
        + [dma((2,)), dma((devices,)), dma((devices,))],
        compiler_params=pltpu.CompilerParams(
            collective_id=2, has_side_effects=True, vmem_limit_bytes=VMEM_BYTES
        ),
        name="reduce_grads",
    )(main, small, squares)


def adam_update(weight, first_moment, second_moment, gradient, factor, learning_rate, decay_rate):
    clipped = gradient * factor
    first_new = BETA_FIRST * first_moment + (1.0 - BETA_FIRST) * clipped
    second_new = BETA_SECOND * second_moment + (1.0 - BETA_SECOND) * clipped * clipped
    first_hat = first_new / (1.0 - BETA_FIRST**STEP)
    second_hat = second_new / (1.0 - BETA_SECOND**STEP)
    weight_new = weight - learning_rate * (
        first_hat / (jnp.sqrt(second_hat) + ADAM_EPS) + decay_rate * weight
    )
    return (weight_new, first_new, second_new)


def pad_to(array, shape):
    return jnp.pad(array, [(0, full - size) for size, full in zip(array.shape, shape)])


def regroup_weights(main, small, experts):
    rows = D // experts
    if rows == GROUP_ROWS:
        return main, small
    lanes = small.shape[2]
    main = main[:, :, : 2 * rows].reshape(experts, 2, 2, rows, D).transpose(1, 2, 0, 3, 4)
    main = main.reshape(2, 2, GROUPS, GROUP_ROWS, D).transpose(2, 0, 1, 3, 4)
    small = small[:, :rows].reshape(GROUPS, GROUP_ROWS, lanes)
    return main.reshape(GROUPS, 2, 2 * GROUP_ROWS, D), pad_to(small, (GROUPS, 32, lanes))


def regroup_grads(main, small_rows, experts):
    rows = D // experts
    lanes = small_rows.shape[1]
    block_rows = round_up(rows, 16)
    small = pad_to(small_rows.reshape(experts, rows, lanes), (experts, block_rows, lanes))
    if rows == GROUP_ROWS:
        return main, small
    main = main.reshape(2, GROUPS, 2, GROUP_ROWS, D).transpose(0, 2, 1, 3, 4)
    main = main.reshape(2, 2, experts, rows, D).transpose(0, 2, 1, 3, 4)
    main = main.reshape(2, experts, 2 * rows, D)
    return pad_to(main, (2, experts, round_up(2 * rows, 16), D)), small


def local(
    patches,
    slot_len,
    attn_weight,
    attn_first,
    attn_second,
    phi_weight,
    phi_first,
    phi_second,
    norm_params,
    norm_first,
    norm_second,
    expert_in,
    in_first,
    in_second,
    expert_out,
    out_first,
    out_second,
    cotangent,
):
    experts = lax.axis_size("expert")
    rows = attn_weight.shape[0]
    lanes = round_up(experts + 4, 128)
    small = jnp.concatenate([phi_weight, norm_params.T], axis=1).astype(BF16)
    small = pad_to(small, (round_up(rows, 16), lanes))
    main, small = gather_weights(attn_weight, small, experts)
    main, small = regroup_weights(main, small, experts)
    *saved, packed = forward_local(slot_len, patches, main, small, cotangent, experts)
    result, gslots, grad_in, grad_out, squares = run_experts(packed, expert_in, expert_out, experts)
    block_output, input_grad, grad_main, grad_phi, grad_norms = backward_local(
        slot_len, patches, main, small, saved, result, gslots, experts
    )
    small_rows = jnp.concatenate([grad_phi[:, :experts], grad_norms[:4].T], axis=1)
    grad_main, grad_small = regroup_grads(grad_main, pad_to(small_rows, (D, lanes)), experts)
    main_part, small_part, norm_tile = reduce_grads(grad_main, grad_small, squares, experts)
    attn_part = main_part[:, : 2 * rows].reshape(2, 2, rows, D).transpose(2, 0, 1, 3)
    attn_part = attn_part.reshape(rows, 4 * D)
    phi_part = small_part[:rows, :experts]
    norm_part = small_part[:rows, experts : experts + 4].T
    grad_norm = norm_tile[0, 0]
    factor = CLIP_NORM / jnp.maximum(grad_norm, CLIP_NORM)
    attn_new, attn_first_new, attn_second_new = adam_update(
        attn_weight, attn_first, attn_second, attn_part, factor, 1.0 / math.sqrt(D), WEIGHT_DECAY
    )
    phi_new, phi_first_new, phi_second_new = adam_update(
        phi_weight, phi_first, phi_second, phi_part, factor, 0.25 / math.sqrt(D), WEIGHT_DECAY
    )
    norm_new, norm_first_new, norm_second_new = adam_update(
        norm_params, norm_first, norm_second, norm_part, factor, 0.8, 0.0
    )
    in_new, in_first_new, in_second_new = adam_update(
        expert_in, in_first, in_second, grad_in, factor, 4.0 / math.sqrt(D), WEIGHT_DECAY
    )
    out_new, out_first_new, out_second_new = adam_update(
        expert_out, out_first, out_second, grad_out, factor, 8.0 / math.sqrt(FF), WEIGHT_DECAY
    )
    return (
        block_output,
        input_grad,
        grad_norm,
        attn_new,
        attn_first_new,
        attn_second_new,
        phi_new,
        phi_first_new,
        phi_second_new,
        norm_new,
        norm_first_new,
        norm_second_new,
        in_new,
        in_first_new,
        in_second_new,
        out_new,
        out_first_new,
        out_second_new,
    )


def solution(mesh):
    in_specs = (
        P(("batch", "expert"), None),
        P(("batch", "expert"), None),
        P("expert", None),
        P("expert", None),
        P("expert", None),
        P("expert", None),
        P("expert", None),
        P("expert", None),
        P(None, "expert"),
        P(None, "expert"),
        P(None, "expert"),
        P("expert", None, "batch"),
        P("expert", None, "batch"),
        P("expert", None, "batch"),
        P("expert", "batch", None),
        P("expert", "batch", None),
        P("expert", "batch", None),
        P(("batch", "expert"), None),
    )
    out_specs = (
        P(("batch", "expert"), None),
        P(("batch", "expert"), None),
        P(),
        P("expert", None),
        P("expert", None),
        P("expert", None),
        P("expert", None),
        P("expert", None),
        P("expert", None),
        P(None, "expert"),
        P(None, "expert"),
        P(None, "expert"),
        P("expert", None, "batch"),
        P("expert", None, "batch"),
        P("expert", None, "batch"),
        P("expert", "batch", None),
        P("expert", "batch", None),
        P("expert", "batch", None),
    )
    return jax.shard_map(local, mesh=mesh, in_specs=in_specs, out_specs=out_specs, check_vma=False)
```

time: 609 us -> 174 us (0.29); the launches traced: 598 us -> 174 us
  blocking collectives: 220 us -> 0 us
  Pallas kernels: 0 us -> 155 us
  matrix products: 154 us -> 0 us
  other arithmetic: 87.2 us -> 9.45 us
  waiting for transfers between devices: 74.1 us -> 0 us
  between operations: 21.3 us -> 1.6 us
  local copies, waits for them, and re-layouts: 26.9 us -> 8.81 us
  starting transfers between devices: 14.5 us -> 0 us
    pallas_call x0 -> x5, Pallas kernels: none -> 155 us  [the longest x1 49.8 us: reduce_grads(): pl.pallas_call(functools.partial(reduce_kernel, experts), out_shape=(shap...]
    dot_general x33 -> x0, matrix products: 154 us -> none  [the longest x2 33 us: local(): jnp.einsum('rhd,thd->hrt', rows_grad, value_heads, preferred_element_type...]
    all_gather x4 -> x0, blocking collectives: 82.4 us -> none  [the longest x1 42.4 us: local(): lax.all_gather(norm_params.astype(jnp.bfloat16), 'expert', axis=1, tiled=...]
    unnamed x1 -> x0, blocking collectives: 72.7 us -> none
    psum x2 -> x0, blocking collectives: 43.8 us -> none  [the longest x1 40.5 us: local(): grad_norm = jnp.sqrt(lax.psum(squares, ('batch', 'expert')))]
    reduce_scatter x3 -> x0, waiting for transfers between devices: 42 us -> none  [the longest x1 32.8 us: local(): lax.psum_scatter(grad_attn, 'expert', scatter_dimension=0, tiled=True)]
    convert_element_type x7 -> x0, other arithmetic: 35.8 us -> none  [the longest x2 30.6 us: local(): grad_scores = (attn_probs * (grad_probs - row_inner)).astype(jnp.bfloat16)]
    reduce_sum x12 -> x0, other arithmetic: 26.3 us -> none  [the longest x2 19.9 us: local(): row_total = jnp.sum(exponent, axis=-1, keepdims=True)]
  transfers between devices with their start and end apart: 7 -> 0, of which waited for: 6 -> 0; matrix products, arithmetic and copies ran while one was open for 4% -> 0% of each run, Pallas kernels for 0% -> 0%
where the time goes in v1:
time: 174 us
  Pallas kernels  155 us (89%)
  other arithmetic  9.45 us (5%)
  local copies, waits for them, and re-layouts  8.81 us (5%)
    pallas_call x1, Pallas kernels, reduce_grads(): pl.pallas_call(functools.partial(reduce_kernel, experts), out_shape=(shap...  49.8 us
    pallas_call x1, Pallas kernels, run_experts(): pl.pallas_call(functools.partial(expert_kernel, experts), out_shape=(shap...  38.5 us
    pallas_call x1, Pallas kernels, backward_local(): pl.pallas_call(functools.partial(backward_kernel, experts), out_shape=(sh...  26.5 us
    pallas_call x1, Pallas kernels, gather_weights(): pl.pallas_call(functools.partial(gather_kernel, experts), out_shape=(jax....  21.5 us
    pallas_call x1, Pallas kernels, forward_local(): pl.pallas_call(functools.partial(forward_kernel, experts), out_shape=(sha...  18.3 us
    sub x5, other arithmetic, adam_update(): weight - learning_rate * (first_hat / (jnp.sqrt(second_hat) + ADAM_EPS) +...  7.28 us
    unnamed x47, local copies, waits for them, and re-layouts  4.48 us

profile of v1, /device:TPU:0, one launch (start us, length us, event | category | flops | bytes accessed | tf_op | source)
XLA Modules:
  0.0 174.4 jit_solution(15627335548030225155)
XLA Ops:
  0.7 0.8 broadcast_multiply_fusion.1
  1.4 0.1 copy.79
  1.5 0.7 convert.7
  2.2 0.1 copy.80
  2.3 0.7 fusion.10.small_ref
  3.0 21.5 %gather_weights.1 = (bf16[16,2,48,384]{3,2,1,0:T(8,128)(2,1)}, bf16[16,32,128]{2,1,0:T(8,128)(2,1)}) custom-call(f32[24,1536]{1,0:T(8,128)} %attn_ref.1, bf16[32,128]{1,0:T(8,128)(2,1)} %fusion.10.small_ref), custom_call_target="tpu_custom_call" | custom-call | tf_op jit(solution)/shard_map/gather_weights/pallas_call | solution.py:142
  24.4 18.3 %forward_local.1 = (bf16[9,1360,128]{2,1,0:T(8,128)(2,1)}, bf16[1360,384]{1,0:T(8,128)(2,1)}, f32[1360,128]{1,0:T(8,128)}, f32[1360,384]{1,0:T(8,128)}, bf16[136...) custom-call(s32[1,5]{1,0:T(1,128)} %len_ref.3, ...), custom_call_target="tpu_custom_call" | custom-call | tf_op jit(solution)/shard_map/forward_local/pallas_call | solution.py:332
  42.8 38.5 %run_experts.1 = (bf16[128,384]{1,0:T(8,128)(2,1)}, bf16[128,384]{1,0:T(8,128)(2,1)}, f32[1,384,768]{2,1,0:T(8,128)}, f32[1,768,384]{2,1,0:T(8,128)}, f32[8,128]{1,0:T(8,128)}) custom-call(bf16[16,32,128]{2,1,0:T(8,128)(2,1)} %get-tuple-element.52.pack_ref, f32[1,384,768]{2,1,0:T(8,128)} %in_ref.1, f32[1,768,384]{2,1,0:T(8,128)} %out_ref.1), custom_call_target="tpu_custom_call" | custom-call | tf_op jit(solution)/shard_map/run_experts/pallas_call | solution.py:480
  81.3 26.5 %backward_local.1 = (bf16[1360,384]{1,0:T(8,128)(2,1)}, bf16[1360,384]{1,0:T(8,128)(2,1)}, f32[2,16,48,384]{3,2,1,0:T(8,128)}, f32[384,128]{1,0:T(8,128)}, f32[8,384]{1,0:T(8,128)}) custom-call(s32[1,5]{1,0:T(1,128)} %len_ref.3, bf16[1360,384]{1,0:T(8,128)(2,1)} %patch_ref.3, bf16[16,2,48,384]{3,2,1,0:T(8,128)(2,1)} %get-tuple-element.42.main_ref, ...), custom_call_target="tpu_custom_call" | custom-call | tf_op jit(solution)/shard_map/backward_local/pallas_call | solution.py:635
  107.7 1.0 copy.81
  108.7 0.7 slice_bitcast_fusion
  109.5 0.1 copy.102
  109.7 0.7 pad.14.gs_ref
  110.4 49.8 %reduce_grads.1 = (f32[2,48,384]{2,1,0:T(8,128)}, f32[32,128]{1,0:T(8,128)}, f32[8,128]{1,0:T(8,128)}) custom-call(f32[2,16,48,384]{3,2,1,0:T(8,128)} %get-tuple-element.57.gw_ref, f32[16,32,128]{2,1,0:T(8,128)} %pad.14.gs_ref, f32[8,128]{1,0:T(8,128)} %get-tuple-element.60.square_ref), custom_call_target="tpu_custom_call" | custom-call | tf_op jit(solution)/shard_map/reduce_grads/pallas_call | solution.py:811
  160.2 1.2 slice.17
  162.1 0.0 copy-done.3
  162.1 0.0 copy-done
  162.2 0.0 copy-done.2
  162.2 0.0 copy-start.1
  162.2 0.0 copy-start.4
  162.2 0.0 copy-start.5
  162.2 3.9 %multiply_subtract_fusion = (f32[1,768,384]{2,1,0:T(8,128)}, f32[1,768,384]{2,1,0:T(8,128)}, f32[1,768,384]{2,1,0:T(8,128)}) fusion(f32[1,768,384]{2,1,0:T(8,128)S(1)} %copy-done, f32[1,768,384]{2,1,0:T(8,128)} %get-tuple-element.65, f32[]{:T(128)S(6)} %div.48, f32[1,768,384]{2,1,0:T(8,128)S(1)} %copy-done.2, f32[1,768,384]{2,1,0:T(8,128)S(1)} %copy-done.3), kind=kLoop, calls=%fused_computation.6 | loop fusion | flops 4423680 | bytes 8257540 | tf_op jit(solution)/shard_map/sub | solution.py:840
  166.1 0.0 copy-done.4
  166.1 0.0 copy-start.16
  166.1 0.0 copy-start.17
  166.1 0.0 copy-start.13
  166.1 0.0 copy-start.14
  166.2 0.0 copy-start.15
  166.2 0.0 copy-start.12
  166.2 2.5 %multiply_subtract_fusion.1 = (f32[1,384,768]{2,1,0:T(8,128)}, f32[1,384,768]{2,1,0:T(8,128)}, f32[1,384,768]{2,1,0:T(8,128)}) fusion(f32[1,384,768]{2,1,0:T(8,128)S(1)} %copy-done.1, f32[1,384,768]{2,1,0:T(8,128)S(1)} %copy-done.6, f32[]{:T(128)S(6)} %div.48, f32[1,384,768]{2,1,0:T(8,128)S(1)} %copy-done.4, f32[1,384,768]{2,1,0:T(8,128)S(1)} %copy-done.5), kind=kLoop, calls=%fused_computation.7 | loop fusion | flops 4423680 | bytes 8257540 | tf_op jit(solution)/shard_map/sub | solution.py:840
  168.7 0.1 copy.94
  168.8 0.0 copy-done.16
  168.8 0.1 copy.92
  168.9 0.1 copy.93
  168.9 0.1 copy.95
  169.0 0.1 multiply_subtract_fusion.3
  169.1 0.7 copy.100
  169.8 0.7 copy.101
  170.4 0.7 copy.99
  171.1 0.1 copy.84
  171.2 0.1 copy.87
  171.2 0.1 copy.90
  171.3 0.7 copy.96
  172.0 0.7 copy.97
  172.7 0.7 copy.98
  173.4 0.1 copy.83
  173.5 0.1 mul.172
  173.6 0.8 multiply_subtract_fusion.2
  (28 shorter events, 0.1 us)
Async XLA Ops:
  109.5 52.6 %copy-start.3 = (f32[1,768,384]{2,1,0:T(8,128)S(1)}, f32[1,768,384]{2,1,0:T(8,128)}, u32[]{:S(2)}) copy-start(f32[1,768,384]{2,1,0:T(8,128)} %param.34) | copy-start | bytes 3538948
  110.4 51.8 %copy-start = (f32[1,768,384]{2,1,0:T(8,128)S(1)}, f32[1,768,384]{2,1,0:T(8,128)}, u32[]{:S(2)}) copy-start(f32[1,768,384]{2,1,0:T(8,128)} %out_ref.1) | copy-start | bytes 3538948
  110.4 51.8 %copy-start.2 = (f32[1,768,384]{2,1,0:T(8,128)S(1)}, f32[1,768,384]{2,1,0:T(8,128)}, u32[]{:S(2)}) copy-start(f32[1,768,384]{2,1,0:T(8,128)} %param.33) | copy-start | bytes 3538948
  162.2 3.9 %copy-start.1 = (f32[1,384,768]{2,1,0:T(8,128)S(1)}, f32[1,384,768]{2,1,0:T(8,128)}, u32[]{:S(2)}) copy-start(f32[1,384,768]{2,1,0:T(8,128)} %in_ref.1) | copy-start | bytes 3538948
  162.2 3.9 %copy-start.4 = (f32[1,384,768]{2,1,0:T(8,128)S(1)}, f32[1,384,768]{2,1,0:T(8,128)}, u32[]{:S(2)}) copy-start(f32[1,384,768]{2,1,0:T(8,128)} %param.30) | copy-start | bytes 3538948
  162.2 3.9 %copy-start.5 = (f32[1,384,768]{2,1,0:T(8,128)S(1)}, f32[1,384,768]{2,1,0:T(8,128)}, u32[]{:S(2)}) copy-start(f32[1,384,768]{2,1,0:T(8,128)} %param.31) | copy-start | bytes 3538948
  162.2 3.9 %copy-start.6 = (f32[1,384,768]{2,1,0:T(8,128)S(1)}, f32[1,384,768]{2,1,0:T(8,128)}, u32[]{:S(2)}) copy-start(f32[1,384,768]{2,1,0:T(8,128)} %get-tuple-element.64) | copy-start | bytes 3538948
  166.1 2.7 %copy-start.16 = (f32[4,24]{1,0:T(4,128)S(1)}, f32[4,24]{1,0:T(4,128)}, u32[]{:S(2)}) copy-start(f32[4,24]{1,0:T(4,128)} %param.27) | copy-start | bytes 1156
  166.1 2.7 %copy-start.17 = (f32[4,24]{1,0:T(4,128)S(1)}, f32[4,24]{1,0:T(4,128)}, u32[]{:S(2)}) copy-start(f32[4,24]{1,0:T(4,128)} %param.28) | copy-start | bytes 1156
  166.1 2.8 %copy-start.13 = (f32[4,24]{1,0:T(4,128)S(1)}, f32[4,24]{1,0:T(4,128)}, u32[]{:S(2)}) copy-start(f32[4,24]{1,0:T(4,128)} %param.26) | copy-start | bytes 1156
  166.1 2.9 %copy-start.11 = (f32[32,128]{1,0:T(8,128)S(1)}, f32[32,128]{1,0:T(8,128)}, u32[]{:S(2)}) copy-start(f32[32,128]{1,0:T(8,128)} %get-tuple-element.63) | copy-start | bytes 49156
  166.1 4.9 %copy-start.14 = (f32[24,16]{0,1:T(8,128)S(1)}, f32[24,16]{0,1:T(8,128)}, u32[]{:S(2)}) copy-start(f32[24,16]{0,1:T(8,128)} %param.24) | copy-start | bytes 4612
  166.2 5.0 %copy-start.15 = (f32[24,16]{0,1:T(8,128)S(1)}, f32[24,16]{0,1:T(8,128)}, u32[]{:S(2)}) copy-start(f32[24,16]{0,1:T(8,128)} %param.25) | copy-start | bytes 4612
  166.2 5.1 %copy-start.12 = (f32[24,16]{0,1:T(8,128)S(1)}, f32[24,16]{0,1:T(8,128)}, u32[]{:S(2)}) copy-start(f32[24,16]{0,1:T(8,128)} %param.23) | copy-start | bytes 4612
  166.2 7.2 %copy-start.8 = (f32[2,48,384]{2,1,0:T(8,128)S(1)}, f32[2,48,384]{2,1,0:T(8,128)}, u32[]{:S(2)}) copy-start(f32[2,48,384]{2,1,0:T(8,128)} %get-tuple-element.62) | copy-start | bytes 442372
  168.7 4.9 %copy-start.7 = (f32[24,1536]{1,0:T(8,128)S(1)}, f32[24,1536]{1,0:T(8,128)}, u32[]{:S(2)}) copy-start(f32[24,1536]{1,0:T(8,128)} %attn_ref.1) | copy-start | bytes 442372
  168.7 4.9 %copy-start.9 = (f32[24,1536]{1,0:T(8,128)S(1)}, f32[24,1536]{1,0:T(8,128)}, u32[]{:S(2)}) copy-start(f32[24,1536]{1,0:T(8,128)} %param.21) | copy-start | bytes 442372
  168.7 4.9 %copy-start.10 = (f32[24,1536]{1,0:T(8,128)S(1)}, f32[24,1536]{1,0:T(8,128)}, u32[]{:S(2)}) copy-start(f32[24,1536]{1,0:T(8,128)} %param.22) | copy-start | bytes 442372

commit v2 on v1

v2 whole, which is shorter than its diff:
```python
import functools
import math

import jax
import jax.numpy as jnp
from jax import lax
from jax.experimental import pallas as pl
from jax.experimental.pallas import tpu as pltpu
from jax.sharding import PartitionSpec as P

D = 384
HEADS = 6
HEAD_DIM = 64
FF = 1536
STEP = 3
SHORT_LEN = 196
LONG_LEN = 576
IMAGES = 5
SLOT_ROWS = 8
PAIRS = 3
GROUPS = 16
GROUP_ROWS = D // GROUPS

NORM_EPS = 1e-06
CLIP_NORM = 1.0
BETA_FIRST = 0.5
BETA_SECOND = 0.5
ADAM_EPS = 1e-08
WEIGHT_DECAY = 0.05
MASKED = -1e30
SCORE_SCALE = HEAD_DIM ** (-0.5)

MESH = pl.DeviceIdType.MESH
F32 = jnp.float32
BF16 = jnp.bfloat16
VMEM_BYTES = 58 * 1024 * 1024


def whole(count):
    return [pl.BlockSpec(memory_space=pltpu.VMEM)] * count


def round_up(value, unit):
    return -(-value // unit) * unit


def mm(left, right):
    return jnp.dot(left, right, preferred_element_type=F32)


def mm_nt(left, right):
    return lax.dot_general(left, right, (((1,), (1,)), ((), ())), preferred_element_type=F32)


def mm_tn(left, right):
    return lax.dot_general(left, right, (((0,), (0,)), ((), ())), preferred_element_type=F32)


def block_rows(experts):
    rows = D // experts
    return round_up(6 * rows + max(experts, 4), 16)


def ring(experts):
    core = lax.axis_index("batch")
    chip = lax.axis_index("expert")
    first = chip ^ (1 + core)
    second = chip ^ (2 - core)
    return core, chip, first, second


def gather_kernel(experts, attn_ref, phi_ref, norm_ref, out, stage, send_z, send_first,
                  send_second, send_pair, recv, recv_pair):
    core, chip, first, second = ring(experts)
    rows = attn_ref.shape[0]
    column = lax.rem(chip, 4)
    layers = experts // 4
    layer = chip // 4
    barrier = pltpu.get_barrier_semaphore()

    @pl.loop(1, layers)
    def _(d):
        peer = lax.rem(layer + d, layers) * 4 + column
        pl.semaphore_signal(barrier, inc=1, device_id=(core, peer), device_id_type=MESH)

    pl.semaphore_signal(barrier, inc=1, device_id=(core, first), device_id_type=MESH)
    pl.semaphore_signal(barrier, inc=1, device_id=(core, second), device_id_type=MESH)
    pl.semaphore_signal(barrier, inc=1, device_id=(1 - core, chip), device_id_type=MESH)
    stage[...] = jnp.zeros_like(stage)
    for part in range(2):
        for g in range(3):
            lanes = pl.multiple_of(core * (2 * D) + (part * D + g * 128), 128)
            place = (2 * g + part) * rows
            stage[place : place + rows, :] = attn_ref[:, pl.ds(lanes, 128)]

    @pl.when(core == 0)
    def _():
        stage[6 * rows : 6 * rows + experts, 0:rows] = phi_ref[...]

    @pl.when(core == 1)
    def _():
        stage[6 * rows : 6 * rows + 4, 0:rows] = norm_ref[...]

    out[chip, core] = stage[...].astype(BF16)
    pl.semaphore_wait(barrier, layers + 2)

    def copy(block, side, sems, sem, arrivals, device):
        return pltpu.make_async_remote_copy(
            src_ref=out.at[block, side],
            dst_ref=out.at[block, side],
            send_sem=sems.at[sem],
            recv_sem=arrivals.at[block],
            device_id=device,
            device_id_type=MESH,
        )

    def along_z(d):
        peer = lax.rem(layer + d, layers) * 4 + column
        return copy(chip, core, send_z, d, recv, (core, peer))

    def to_first(block):
        return copy(block, core, send_first, block, recv, (core, first))

    def to_second(block):
        return copy(block, core, send_second, block, recv, (core, second))

    def to_pair(block):
        return copy(block, core, send_pair, block, recv_pair, (1 - core, chip))

    @pl.loop(1, layers)
    def _(d):
        along_z(d).start()

    to_first(chip).start()
    to_second(chip).start()
    to_pair(chip).start()

    @pl.loop(1, layers)
    def _(d):
        block = lax.rem(layer - d + layers, layers) * 4 + column
        to_first(block).wait_recv()
        to_first(block).start()
        to_second(block).start()
        to_pair(block).start()

    @pl.loop(0, layers)
    def _(d):
        block = lax.rem(layer - d + layers, layers) * 4 + lax.rem(first, 4)
        to_first(block).wait_recv()
        to_second(block).start()
        to_pair(block).start()

    @pl.loop(0, 2 * layers)
    def _(d):
        other = jnp.where(lax.rem(d, 2) == 0, lax.rem(second, 4), lax.rem(3 - column, 4))
        block = lax.rem(layer - d // 2 + layers, layers) * 4 + other
        to_first(block).wait_recv()
        to_pair(block).start()

    @pl.loop(1, layers)
    def _(d):
        along_z(d).wait_send()

    @pl.loop(0, layers)
    def _(d):
        block = d * 4 + column
        to_first(block).wait_send()
        to_second(block).wait_send()
        to_second(d * 4 + lax.rem(first, 4)).wait_send()

    @pl.loop(0, experts)
    def _(block):
        to_pair(block).wait_send()
        copy(block, 1 - core, send_pair, block, recv_pair, (1 - core, chip)).wait_recv()


def gather_weights(attn_weight, phi_turned, norm_params, experts):
    rows = block_rows(experts)
    dma = pltpu.SemaphoreType.DMA
    return pl.pallas_call(
        functools.partial(gather_kernel, experts),
        out_shape=jax.ShapeDtypeStruct((experts, 2, rows, 128), BF16),
        in_specs=whole(3),
        out_specs=whole(1)[0],
        scratch_shapes=[pltpu.VMEM((rows, 128), F32), dma((experts // 4,))]
        + [dma((experts,))] * 5,
        compiler_params=pltpu.CompilerParams(
            collective_id=0, has_side_effects=True, vmem_limit_bytes=16 * 1024 * 1024
        ),
        name="gather_weights",
    )(attn_weight, phi_turned, norm_params)


def unpack_weight(main_ref, side, part):
    blocks = main_ref[:, side].astype(F32)
    columns = []
    for g in range(3):
        place = (2 * g + part) * GROUP_ROWS
        columns.append(blocks[:, place : place + GROUP_ROWS, :].reshape(D, 128))
    return jnp.concatenate(columns, axis=1).astype(BF16)


def group_lanes():
    lane = lax.broadcasted_iota(jnp.int32, (128, D), 0)
    column = lax.broadcasted_iota(jnp.int32, (128, D), 1)
    return jnp.where(column % GROUP_ROWS == lane, 1.0, 0.0).astype(BF16)


def unpack_turned(main_ref, side, rows):
    first = 6 * GROUP_ROWS
    blocks = main_ref[:, side].astype(F32)[:, first : first + rows, :]
    spread = mm(blocks.reshape(GROUPS * rows, 128).astype(BF16), group_lanes())
    spread = spread.reshape(GROUPS, rows, D)
    group = lax.broadcasted_iota(jnp.int32, (GROUPS, 1, D), 0)
    column = lax.broadcasted_iota(jnp.int32, (GROUPS, 1, D), 2)
    return jnp.sum(jnp.where(column // GROUP_ROWS == group, spread, 0.0), axis=0)


def pack_turned(values):
    rows = values.shape[0]
    group = lax.broadcasted_iota(jnp.int32, (GROUPS, 1, D), 0)
    column = lax.broadcasted_iota(jnp.int32, (GROUPS, 1, D), 2)
    spread = jnp.where(column // GROUP_ROWS == group, values[None], 0.0)
    spread = spread.reshape(GROUPS * rows, D).astype(BF16)
    return mm_nt(spread, group_lanes()).reshape(GROUPS, rows, 128)


def unpack_small(main_ref, experts):
    turned = unpack_turned(main_ref, 0, max(experts, 16)).astype(BF16)
    row = lax.broadcasted_iota(jnp.int32, (experts * SLOT_ROWS, turned.shape[0]), 0)
    column = lax.broadcasted_iota(jnp.int32, (experts * SLOT_ROWS, turned.shape[0]), 1)
    spread = jnp.where(column == row // SLOT_ROWS, 1.0, 0.0).astype(BF16)
    return mm(spread, turned).astype(BF16), unpack_turned(main_ref, 1, 8)


def slot_bounds(len_ref, columns):
    image = lax.broadcasted_iota(jnp.int32, (1, columns), 1) % SLOT_ROWS
    starts = jnp.zeros((1, columns), jnp.int32)
    ends = jnp.zeros((1, columns), jnp.int32)
    start = jnp.int32(0)
    for k in range(IMAGES):
        end = start + len_ref[0, k]
        starts = jnp.where(image == k, start, starts)
        ends = jnp.where(image == k, end, ends)
        start = end
    return starts, ends, start


def normed(values):
    centred = values - jnp.mean(values, axis=-1, keepdims=True)
    variance = jnp.mean(centred * centred, axis=-1, keepdims=True)
    inverse = lax.rsqrt(variance + NORM_EPS)
    return centred * inverse, inverse


def norm_back(grad_shaped, normal, inverse, scaling):
    grad_normal = grad_shaped * scaling
    return inverse * (
        grad_normal
        - jnp.mean(grad_normal, axis=-1, keepdims=True)
        - normal * jnp.mean(grad_normal * normal, axis=-1, keepdims=True)
    )


def over_images(len_ref, tokens, body):
    def step(k, start):
        length = len_ref[0, k]
        for full in (SHORT_LEN, LONG_LEN):

            @pl.when(length == full)
            def _():
                window = round_up(full + 12, 16)
                first = jnp.minimum((start // 16) * 16, tokens - window)
                body(pl.multiple_of(first, 16), start - first, full, window)

        return start + length

    lax.fori_loop(0, IMAGES, step, jnp.int32(0))


def window_masks(shift, full, window):
    column = lax.broadcasted_iota(jnp.int32, (1, window), 1)
    row = lax.broadcasted_iota(jnp.int32, (window, 1), 0)
    bias = jnp.where((column >= shift) & (column < shift + full), 0.0, MASKED)
    inside = (row >= shift) & (row < shift + full)
    return bias, inside


def forward_kernel(experts, len_ref, patch_ref, main_ref, cot_ref, qkv_ref, o_ref, lse_ref, x1_ref,
                   h2_ref, disp_ref, comb_ref, gy_ref, pack_ref, logit, packf):
    tokens = patch_ref.shape[0]
    columns = experts * SLOT_ROWS
    tile = tokens // 5
    phi, norms = unpack_small(main_ref, experts)
    starts, ends, total = slot_bounds(len_ref, columns)
    w_q, w_k = unpack_weight(main_ref, 0, 0), unpack_weight(main_ref, 0, 1)
    w_v = unpack_weight(main_ref, 1, 0)
    w_qkv = jnp.concatenate([w_q, w_k, w_v], axis=1)
    for t in range(5):
        rows = pl.ds(t * tile, tile)
        normal, _ = normed(patch_ref[rows, :].astype(F32))
        h1 = (normal * norms[0:1] + norms[1:2]).astype(BF16)
        qkv = mm(h1, w_qkv).astype(BF16)
        for c in range(9):
            qkv_ref[c, rows, :] = qkv[:, c * 128 : (c + 1) * 128]
    o_ref[...] = jnp.zeros_like(o_ref)
    lse_ref[...] = jnp.zeros_like(lse_ref)
    low_lane = lax.broadcasted_iota(jnp.int32, (1, 128), 1) < HEAD_DIM
    lane = lax.broadcasted_iota(jnp.int32, (1, 128), 1)

    def attend(first, shift, full, window):
        bias, inside = window_masks(shift, full, window)
        rows = pl.ds(first, window)

        @pl.loop(0, PAIRS)
        def _(p):
            query = qkv_ref[p, rows, :].astype(F32) * SCORE_SCALE
            keys = qkv_ref[PAIRS + p, rows, :]
            values = qkv_ref[2 * PAIRS + p, rows, :]
            outs = []
            sums = lse_ref[rows, :]
            for h in range(2):
                mine = low_lane if h == 0 else jnp.logical_not(low_lane)
                scores = mm_nt(jnp.where(mine, query, 0.0).astype(BF16), keys) + bias
                peak = jnp.max(scores, axis=-1, keepdims=True)
                exponent = jnp.exp(scores - peak)
                summed = jnp.sum(exponent, axis=-1, keepdims=True)
                probs = (exponent * (1.0 / summed)).astype(BF16)
                outs.append(mm(probs, values))
                sums = jnp.where(inside & (lane == 2 * p + h), peak + jnp.log(summed), sums)
            lse_ref[rows, :] = sums
            lanes = pl.ds(pl.multiple_of(p * 128, 128), 128)
            old = o_ref[rows, lanes].astype(F32)
            merged = jnp.where(inside, jnp.where(low_lane, outs[0], outs[1]), old)
            o_ref[rows, lanes] = merged.astype(BF16)

    over_images(len_ref, tokens, attend)

    w_o = unpack_weight(main_ref, 1, 1)
    for t in range(5):
        rows = pl.ds(t * tile, tile)
        x1 = patch_ref[rows, :].astype(F32) + mm(o_ref[rows, :], w_o)
        normal, _ = normed(x1)
        h2 = (normal * norms[2:3] + norms[3:4]).astype(BF16)
        h2_ref[rows, :] = h2
        logit[rows, :] = mm_nt(h2, phi)
        position = t * tile + lax.broadcasted_iota(jnp.int32, (tile, 1), 0)
        valid = position < total
        x1_ref[rows, :] = jnp.where(valid, x1, 0.0)
        gy_ref[rows, :] = jnp.where(valid, cot_ref[rows, :].astype(F32), 0.0).astype(BF16)

    position = lax.broadcasted_iota(jnp.int32, (tokens, columns), 0)
    member = (position >= starts) & (position < ends)
    present = ends > starts
    logits = logit[...]
    peak = jnp.max(jnp.where(member, logits, MASKED), axis=0, keepdims=True)
    peak = jnp.where(present, peak, 0.0)
    exponent = jnp.where(member, jnp.exp(jnp.where(member, logits - peak, 0.0)), 0.0)
    summed = jnp.sum(exponent, axis=0, keepdims=True) + jnp.where(present, 0.0, 1.0)
    dispatch = exponent / summed
    disp_ref[...] = dispatch
    slots = mm_tn(dispatch.astype(BF16), h2_ref[...])
    row_peak = jnp.max(logits, axis=-1, keepdims=True)
    exponent = jnp.exp(logits - row_peak)
    summed = jnp.sum(exponent, axis=-1, keepdims=True) * (1.0 / SLOT_ROWS)
    combine = jnp.where(member, exponent / summed, 0.0)
    comb_ref[...] = combine
    grad_result = mm_tn(combine.astype(BF16), gy_ref[...])
    for part, matrix in enumerate((slots, grad_result)):
        pack_rows(packf, matrix.reshape(experts, SLOT_ROWS, D))
        pack_ref[:, part * 16 : (part + 1) * 16, :] = packf[...].astype(BF16)


def pack_rows(packf, blocks):
    packf[...] = jnp.zeros_like(packf)
    for c in range(3):
        packf[:, c * IMAGES : (c + 1) * IMAGES, :] = blocks[:, :IMAGES, c * 128 : (c + 1) * 128]


def unpack_rows(packf, wide):
    wide[...] = jnp.zeros_like(wide)
    for c in range(3):
        wide[:, 0:IMAGES, c * 128 : (c + 1) * 128] = packf[:, c * IMAGES : (c + 1) * IMAGES, :]


def forward_local(lengths, patches, main, cotangent, experts):
    tokens = patches.shape[0]
    columns = experts * SLOT_ROWS
    shape = jax.ShapeDtypeStruct
    return pl.pallas_call(
        functools.partial(forward_kernel, experts),
        out_shape=(
            shape((9, tokens, 128), BF16),
            shape((tokens, D), BF16),
            shape((tokens, 128), F32),
            shape((tokens, D), F32),
            shape((tokens, D), BF16),
            shape((tokens, columns), F32),
            shape((tokens, columns), F32),
            shape((tokens, D), BF16),
            shape((experts, 32, 128), BF16),
        ),
        in_specs=[pl.BlockSpec(memory_space=pltpu.SMEM)] + whole(3),
        out_specs=tuple(whole(9)),
        scratch_shapes=[pltpu.VMEM((tokens, columns), F32), pltpu.VMEM((experts, 16, 128), F32)],
        compiler_params=pltpu.CompilerParams(vmem_limit_bytes=VMEM_BYTES),
        name="forward_local",
    )(lengths, patches, main, cotangent)


def expert_kernel(experts, pack_ref, in_ref, out_ref, result_ref, gslot_ref, gin_ref, gout_ref,
                  square_ref, inbox, partial, given, outbox, back, packf, wide, packe, widee,
                  send_one, recv_one, pair_send, pair_recv, send_two, recv_two, sum_sem):
    core = lax.axis_index("batch")
    chip = lax.axis_index("expert")
    barrier = pltpu.get_barrier_semaphore()

    @pl.loop(1, experts)
    def _(j):
        peer = lax.rem(chip + j, experts)
        pl.semaphore_signal(barrier, inc=1, device_id=(core, peer), device_id_type=MESH)

    pl.semaphore_signal(barrier, inc=1, device_id=(1 - core, chip), device_id_type=MESH)
    w_in = in_ref[0].astype(BF16)
    w_out = out_ref[0].astype(BF16)
    inbox[core, chip] = pack_ref[chip]
    pl.semaphore_wait(barrier, experts)

    def first(j, block, peer):
        return pltpu.make_async_remote_copy(
            src_ref=pack_ref.at[peer],
            dst_ref=inbox.at[core, block],
            send_sem=send_one.at[j],
            recv_sem=recv_one.at[j],
            device_id=(core, peer),
            device_id_type=MESH,
        )

    def to_pair(side, block):
        return pltpu.make_async_remote_copy(
            src_ref=inbox.at[side, block],
            dst_ref=inbox.at[side, block],
            send_sem=pair_send.at[block],
            recv_sem=pair_recv.at[block],
            device_id=(1 - core, chip),
            device_id_type=MESH,
        )

    def second(j, block, peer):
        return pltpu.make_async_remote_copy(
            src_ref=outbox.at[peer],
            dst_ref=back.at[block],
            send_sem=send_two.at[j],
            recv_sem=recv_two.at[j],
            device_id=(core, peer),
            device_id_type=MESH,
        )

    @pl.loop(1, experts)
    def _(j):
        first(j, chip, lax.rem(chip + j, experts)).start()

    to_pair(core, chip).start()

    @pl.loop(1, experts)
    def _(j):
        source = lax.rem(chip - j + experts, experts)
        first(j, source, source).wait_recv()
        to_pair(core, source).start()

    @pl.loop(0, experts)
    def _(block):
        to_pair(1 - core, block).wait_recv()

    def spread(side, part):
        packe[...] = inbox[side, :, part * 16 : (part + 1) * 16, :].astype(F32)
        unpack_rows(packe, widee)
        return widee[...].reshape(experts * SLOT_ROWS, D).astype(BF16)

    def run(side):
        slots = spread(side, 0)
        grads = spread(side, 1)
        hidden = mm(slots, w_in)
        root = math.sqrt(2.0 / math.pi)
        bent = jnp.tanh(root * (hidden + 0.044715 * (hidden * hidden * hidden)))
        half = 0.5 * (1.0 + bent)
        act = (hidden * half).astype(BF16)
        slope = half + 0.5 * hidden * (1.0 - bent * bent) * (
            root * (1.0 + 3.0 * 0.044715 * (hidden * hidden))
        )
        result = mm(act, w_out)
        grad_hidden = (mm_nt(grads, w_out) * slope).astype(BF16)
        grad_slots = mm_nt(grad_hidden, w_in)
        return slots, grads, act, grad_hidden, result, grad_slots

    theirs = run(1 - core)
    for part in range(2):
        pack_rows(packf, theirs[4 + part].reshape(experts, SLOT_ROWS, D))
        partial[:, part * 16 : (part + 1) * 16, :] = packf[...].astype(BF16)
    halves = pltpu.make_async_remote_copy(
        src_ref=partial,
        dst_ref=given,
        send_sem=sum_sem.at[0],
        recv_sem=sum_sem.at[1],
        device_id=(1 - core, chip),
        device_id_type=MESH,
    )
    halves.start()
    ours = run(core)
    halves.wait_recv()
    for part in range(2):
        block = slice(part * 16, (part + 1) * 16)
        pack_rows(packf, ours[4 + part].reshape(experts, SLOT_ROWS, D))
        outbox[:, block, :] = (packf[...] + given[:, block, :].astype(F32)).astype(BF16)

    @pl.loop(1, experts)
    def _(j):
        second(j, chip, lax.rem(chip + j, experts)).start()

    back[chip] = outbox[chip]
    grad_out = mm_tn(ours[2], ours[1]) + mm_tn(theirs[2], theirs[1])
    gout_ref[0] = grad_out
    grad_in = mm_tn(ours[0], ours[3]) + mm_tn(theirs[0], theirs[3])
    gin_ref[0] = grad_in
    squares = jnp.sum(grad_out * grad_out) + jnp.sum(grad_in * grad_in)
    square_ref[...] = jnp.full(square_ref.shape, squares, F32)

    @pl.loop(1, experts)
    def _(j):
        source = lax.rem(chip - j + experts, experts)
        second(j, source, source).wait_recv()

    for part, target in enumerate((result_ref, gslot_ref)):
        packe[...] = back[:, part * 16 : (part + 1) * 16, :].astype(F32)
        unpack_rows(packe, widee)
        target[...] = widee[...].reshape(experts * SLOT_ROWS, D).astype(BF16)

    halves.wait_send()

    @pl.loop(1, experts)
    def _(j):
        peer = lax.rem(chip + j, experts)
        first(j, chip, peer).wait_send()
        second(j, chip, peer).wait_send()

    @pl.loop(0, experts)
    def _(block):
        to_pair(core, block).wait_send()


def run_experts(packed, expert_in, expert_out, experts):
    shape = jax.ShapeDtypeStruct
    dma = pltpu.SemaphoreType.DMA
    return pl.pallas_call(
        functools.partial(expert_kernel, experts),
        out_shape=(
            shape((experts * SLOT_ROWS, D), BF16),
            shape((experts * SLOT_ROWS, D), BF16),
            shape(expert_in.shape, F32),
            shape(expert_out.shape, F32),
            shape((1, 128), F32),
        ),
        in_specs=whole(3),
        out_specs=tuple(whole(5)),
        scratch_shapes=[
            pltpu.VMEM((2, experts, 32, 128), BF16),
            pltpu.VMEM((experts, 32, 128), BF16),
            pltpu.VMEM((experts, 32, 128), BF16),
            pltpu.VMEM((experts, 32, 128), BF16),
            pltpu.VMEM((experts, 32, 128), BF16),
            pltpu.VMEM((experts, 16, 128), F32),
            pltpu.VMEM((experts, SLOT_ROWS, D), F32),
            pltpu.VMEM((experts, 16, 128), F32),
            pltpu.VMEM((experts, SLOT_ROWS, D), F32),
        ]
        + [dma((experts,))] * 6
        + [dma((2,))],
        compiler_params=pltpu.CompilerParams(
            collective_id=1, has_side_effects=True, vmem_limit_bytes=VMEM_BYTES
        ),
        name="run_experts",
    )(packed, expert_in, expert_out)


def backward_kernel(experts, len_ref, patch_ref, main_ref, qkv_ref, o_ref, lse_ref,
                    x1_ref, h2_ref, disp_ref, comb_ref, gy_ref, result_ref, gslot_ref, block_ref,
                    input_ref, gw_ref, gdisp, glog, gx1, branch, go, gqkv,
                    h1_all):
    tokens = patch_ref.shape[0]
    columns = experts * SLOT_ROWS
    tile = tokens // 5
    phi, norms = unpack_small(main_ref, experts)
    result = result_ref[...]
    gslots = gslot_ref[...]

    inner = jnp.zeros((1, columns), F32)
    for t in range(5):
        rows = pl.ds(t * tile, tile)
        grad_dispatch = mm_nt(h2_ref[rows, :], gslots)
        gdisp[rows, :] = grad_dispatch
        inner = inner + jnp.sum(disp_ref[rows, :] * grad_dispatch, axis=0, keepdims=True)

    w_o = unpack_weight(main_ref, 1, 1)
    gain_two = jnp.zeros((1, D), F32)
    bias_two = jnp.zeros((1, D), F32)
    for t in range(5):
        rows = pl.ds(t * tile, tile)
        dispatch, combine, gy = disp_ref[rows, :], comb_ref[rows, :], gy_ref[rows, :]
        x1 = x1_ref[rows, :]
        mixed = mm(combine.astype(BF16), result)
        block_ref[rows, :] = (x1 + mixed).astype(BF16)
        weighted = combine * mm_nt(gy, result)
        grad_logits = (
            weighted
            - combine * jnp.sum(weighted, axis=-1, keepdims=True)
            + dispatch * (gdisp[rows, :] - inner)
        ).astype(BF16)
        glog[rows, :] = grad_logits
        grad_h2 = mm(dispatch.astype(BF16), gslots) + mm(grad_logits, phi)
        normal, inverse = normed(x1)
        gain_two = gain_two + jnp.sum(grad_h2 * normal, axis=0, keepdims=True)
        bias_two = bias_two + jnp.sum(grad_h2, axis=0, keepdims=True)
        grad_x1 = gy.astype(F32) + norm_back(grad_h2, normal, inverse, norms[2:3])
        gx1[rows, :] = grad_x1
        grad_branch = grad_x1.astype(BF16)
        branch[rows, :] = grad_branch
        grad_o = mm_nt(grad_branch, w_o).astype(BF16)
        for c in range(PAIRS):
            go[c, rows, :] = grad_o[:, c * 128 : (c + 1) * 128]

    small_rows = gw_ref.shape[2] - 6 * GROUP_ROWS
    row = lax.broadcasted_iota(jnp.int32, (columns, small_rows), 0)
    column = lax.broadcasted_iota(jnp.int32, (columns, small_rows), 1)
    fold = jnp.where(column == row // SLOT_ROWS, 1.0, 0.0).astype(BF16)
    folded = mm(glog[...], fold).astype(BF16)
    gw_ref[0, :, 6 * GROUP_ROWS :, :] = pack_turned(mm_tn(folded, h2_ref[...]))

    def put(side, part, value):
        for g in range(3):
            place = (2 * g + part) * GROUP_ROWS
            gw_ref[side, :, place : place + GROUP_ROWS, :] = value[
                :, g * 128 : (g + 1) * 128
            ].reshape(GROUPS, GROUP_ROWS, 128)

    put(1, 1, mm_tn(o_ref[...], branch[...]))

    gqkv[...] = jnp.zeros_like(gqkv)
    low_lane = lax.broadcasted_iota(jnp.int32, (1, 128), 1) < HEAD_DIM
    lane = lax.broadcasted_iota(jnp.int32, (1, 128), 1)

    def attend(first, shift, full, window):
        bias, inside = window_masks(shift, full, window)
        rows = pl.ds(first, window)
        sums = lse_ref[rows, :]

        @pl.loop(0, PAIRS)
        def _(p):
            query_low = qkv_ref[p, rows, :]
            query = query_low.astype(F32) * SCORE_SCALE
            keys = qkv_ref[PAIRS + p, rows, :]
            values = qkv_ref[2 * PAIRS + p, rows, :]
            grads_low = go[p, rows, :]
            grads = grads_low.astype(F32)
            parts = []
            for h in range(2):
                mine = low_lane if h == 0 else jnp.logical_not(low_lane)
                scores = mm_nt(jnp.where(mine, query, 0.0).astype(BF16), keys) + bias
                summed = jnp.sum(jnp.where(lane == 2 * p + h, sums, 0.0), axis=-1, keepdims=True)
                probs = jnp.exp(scores - jnp.where(inside, summed, 1e30))
                grad_probs = mm_nt(jnp.where(mine, grads, 0.0).astype(BF16), values)
                dot = jnp.sum(probs * grad_probs, axis=-1, keepdims=True)
                grad_scores = (probs * (grad_probs - dot)).astype(BF16)
                parts.append(
                    (
                        mm(grad_scores, keys) * SCORE_SCALE,
                        mm_tn(grad_scores, query_low) * SCORE_SCALE,
                        mm_tn(probs.astype(BF16), grads_low),
                    )
                )
            for c in range(3):
                old = gqkv[c * PAIRS + p, rows, :].astype(F32)
                new = jnp.where(low_lane, parts[0][c], parts[1][c])
                gqkv[c * PAIRS + p, rows, :] = jnp.where(inside, new, old).astype(BF16)

    over_images(len_ref, tokens, attend)

    w_q, w_k = unpack_weight(main_ref, 0, 0), unpack_weight(main_ref, 0, 1)
    w_v = unpack_weight(main_ref, 1, 0)
    w_qkv = jnp.concatenate([w_q, w_k, w_v], axis=1)
    gain_one = jnp.zeros((1, D), F32)
    bias_one = jnp.zeros((1, D), F32)
    for t in range(5):
        rows = pl.ds(t * tile, tile)
        grad_qkv = jnp.concatenate([gqkv[c, rows, :] for c in range(9)], axis=1)
        grad_h1 = mm_nt(grad_qkv, w_qkv)
        normal, inverse = normed(patch_ref[rows, :].astype(F32))
        h1_all[rows, :] = (normal * norms[0:1] + norms[1:2]).astype(BF16)
        gain_one = gain_one + jnp.sum(grad_h1 * normal, axis=0, keepdims=True)
        bias_one = bias_one + jnp.sum(grad_h1, axis=0, keepdims=True)
        grad_x = gx1[rows, :] + norm_back(grad_h1, normal, inverse, norms[0:1])
        input_ref[rows, :] = grad_x.astype(BF16)
    for c, (side, part) in enumerate(((0, 0), (0, 1), (1, 0))):
        grad = jnp.concatenate([gqkv[c * PAIRS + p] for p in range(PAIRS)], axis=1)
        put(side, part, mm_tn(h1_all[...], grad))
    zeros = jnp.zeros((small_rows - 4, D), F32)
    turned = jnp.concatenate([gain_one, bias_one, gain_two, bias_two, zeros], axis=0)
    gw_ref[1, :, 6 * GROUP_ROWS :, :] = pack_turned(turned)


def backward_local(lengths, patches, main, saved, result, gslots, experts):
    tokens = patches.shape[0]
    columns = experts * SLOT_ROWS
    shape = jax.ShapeDtypeStruct
    return pl.pallas_call(
        functools.partial(backward_kernel, experts),
        out_shape=(
            shape((tokens, D), BF16),
            shape((tokens, D), BF16),
            shape((2,) + (GROUPS,) + main.shape[2:], F32),
        ),
        in_specs=[pl.BlockSpec(memory_space=pltpu.SMEM)] + whole(12),
        out_specs=tuple(whole(3)),
        scratch_shapes=[
            pltpu.VMEM((tokens, columns), F32),
            pltpu.VMEM((tokens, columns), BF16),
            pltpu.VMEM((tokens, D), F32),
            pltpu.VMEM((tokens, D), BF16),
            pltpu.VMEM((PAIRS, tokens, 128), BF16),
            pltpu.VMEM((9, tokens, 128), BF16),
            pltpu.VMEM((tokens, D), BF16),
        ],
        compiler_params=pltpu.CompilerParams(vmem_limit_bytes=VMEM_BYTES),
        name="backward_local",
    )(lengths, patches, main, *saved, result, gslots)


def reduce_kernel(experts, gw_ref, square_ref, attn_out, phi_out, norm_out, total_ref, own, pair_in,
                  box_one, in_one, box_two, in_two, box_z, in_z, final, scalars, load_sem, pair_send,
                  pair_recv, send_one, recv_one, send_two, recv_two, send_z, recv_z, swap_sem,
                  norm_send, norm_recv):
    core, chip, first, second = ring(experts)
    rows = attn_out.shape[0]
    layers = experts // 4
    layer = chip // 4
    column = lax.rem(chip, 4)
    barrier = pltpu.get_barrier_semaphore()

    @pl.loop(1, experts)
    def _(j):
        peer = lax.rem(chip + j, experts)
        pl.semaphore_signal(barrier, inc=1, device_id=(core, peer), device_id_type=MESH)

    pl.semaphore_signal(barrier, inc=1, device_id=(1 - core, chip), device_id_type=MESH)
    load = pltpu.make_async_copy(gw_ref.at[core], own, load_sem.at[0])
    load.start()
    pl.semaphore_wait(barrier, experts)

    def pair_copy(block):
        return pltpu.make_async_remote_copy(
            src_ref=gw_ref.at[1 - core, block],
            dst_ref=pair_in.at[block],
            send_sem=pair_send.at[block],
            recv_sem=pair_recv.at[block],
            device_id=(1 - core, chip),
            device_id_type=MESH,
        )

    def copy(source, target, sends, arrivals, index, device):
        return pltpu.make_async_remote_copy(
            src_ref=source.at[index],
            dst_ref=target.at[index],
            send_sem=sends.at[index],
            recv_sem=arrivals.at[index],
            device_id=device,
            device_id_type=MESH,
        )

    def to_first(index):
        return copy(box_one, in_one, send_one, recv_one, index, (core, first))

    def to_second(index):
        return copy(box_two, in_two, send_two, recv_two, index, (core, second))

    def layer_at(d):
        return lax.rem(layer + 1 + d, layers)

    far = 3 - column

    def block_at(d, place):
        return layer_at(d) * 4 + place

    both, one, two = far, lax.rem(first, 4), lax.rem(second, 4)

    for place in (both, two, one, column):

        @pl.loop(0, layers)
        def _(d):
            pair_copy(block_at(d, place)).start()

    load.wait()

    def summed(block):
        pair_copy(block).wait_recv()
        return own[block] + pair_in[block]

    for batch, place in ((0, both), (1, one)):

        @pl.loop(0, layers)
        def _(d):
            index = batch * layers + layer_at(d)
            box_one[index] = summed(block_at(d, place)).astype(BF16)
            to_first(index).start()

    @pl.loop(0, layers)
    def _(d):
        index = layer_at(d)
        total = summed(block_at(d, two))
        to_first(index).wait_recv()
        box_two[index] = (total + in_one[index].astype(F32)).astype(BF16)
        to_second(index).start()

    def to_layer(index):
        return pltpu.make_async_remote_copy(
            src_ref=box_z.at[index],
            dst_ref=in_z.at[layer],
            send_sem=send_z.at[index],
            recv_sem=recv_z.at[layer],
            device_id=(core, index * 4 + column),
            device_id_type=MESH,
        )

    def column_sum(index):
        total = summed(index * 4 + column)
        to_first(layers + index).wait_recv()
        total = total + in_one[layers + index].astype(F32)
        to_second(index).wait_recv()
        return total + in_two[index].astype(F32)

    @pl.loop(0, layers - 1)
    def _(d):
        index = layer_at(d)
        box_z[index] = column_sum(index).astype(BF16)
        to_layer(index).start()

    final[core] = column_sum(layer)

    @pl.loop(1, layers)
    def _(d):
        index = lax.rem(layer - d + layers, layers)
        pltpu.make_async_remote_copy(
            src_ref=box_z.at[index],
            dst_ref=in_z.at[index],
            send_sem=send_z.at[index],
            recv_sem=recv_z.at[index],
            device_id=(core, index * 4 + column),
            device_id_type=MESH,
        ).wait_recv()
        final[core] += in_z[index].astype(F32)

    def swap(side):
        return pltpu.make_async_remote_copy(
            src_ref=final.at[side],
            dst_ref=final.at[side],
            send_sem=swap_sem.at[0],
            recv_sem=swap_sem.at[1],
            device_id=(1 - core, chip),
            device_id_type=MESH,
        )

    mine = final[core]
    swap(core).start()

    scalars[experts + core] = square_ref[...] + jnp.sum(mine * mine)

    def norm_pair(side):
        return pltpu.make_async_remote_copy(
            src_ref=scalars.at[experts + side],
            dst_ref=scalars.at[experts + side],
            send_sem=swap_sem.at[2],
            recv_sem=swap_sem.at[3],
            device_id=(1 - core, chip),
            device_id_type=MESH,
        )

    norm_pair(core).start()
    norm_pair(1 - core).wait_recv()
    scalars[chip] = scalars[experts] + scalars[experts + 1]

    def norm_copy(j, block, peer):
        return pltpu.make_async_remote_copy(
            src_ref=scalars.at[block],
            dst_ref=scalars.at[block],
            send_sem=norm_send.at[j],
            recv_sem=norm_recv.at[j],
            device_id=(core, peer),
            device_id_type=MESH,
        )

    @pl.loop(1, experts)
    def _(j):
        norm_copy(j, chip, lax.rem(chip + j, experts)).start()

    swap(1 - core).wait_recv()
    for side in range(2):
        for part in range(2):
            for g in range(3):
                lanes = (side * 2 + part) * D + g * 128
                place = (2 * g + part) * rows
                attn_out[:, lanes : lanes + 128] = final[side, place : place + rows, :]
    phi_out[...] = final[0, 6 * rows : 6 * rows + experts, 0:rows]
    norm_out[...] = final[1, 6 * rows : 6 * rows + 4, 0:rows]

    @pl.loop(1, experts)
    def _(j):
        source = lax.rem(chip - j + experts, experts)
        norm_copy(j, source, source).wait_recv()

    total_ref[...] = jnp.sqrt(jnp.sum(scalars[0:experts], axis=0))
    swap(core).wait_send()
    norm_pair(core).wait_send()

    @pl.loop(0, experts)
    def _(block):
        pair_copy(block).wait_send()

    @pl.loop(0, 2 * layers)
    def _(index):
        to_first(index).wait_send()

    @pl.loop(0, layers)
    def _(index):
        to_second(index).wait_send()

    @pl.loop(1, layers)
    def _(d):
        to_layer(lax.rem(layer + d, layers)).wait_send()

    @pl.loop(1, experts)
    def _(j):
        norm_copy(j, chip, lax.rem(chip + j, experts)).wait_send()


def reduce_grads(grads, squares, experts):
    rows = D // experts
    layers = experts // 4
    block = grads.shape[2:]
    shape = jax.ShapeDtypeStruct
    dma = pltpu.SemaphoreType.DMA
    return pl.pallas_call(
        functools.partial(reduce_kernel, experts),
        out_shape=(
            shape((rows, 4 * D), F32),
            shape((experts, rows), F32),
            shape((4, rows), F32),
            shape((1, 128), F32),
        ),
        in_specs=[pl.BlockSpec(memory_space=pl.ANY)] + whole(1),
        out_specs=tuple(whole(4)),
        scratch_shapes=[
            pltpu.VMEM((experts,) + block, F32),
            pltpu.VMEM((experts,) + block, F32),
            pltpu.VMEM((2 * layers,) + block, BF16),
            pltpu.VMEM((2 * layers,) + block, BF16),
            pltpu.VMEM((layers,) + block, BF16),
            pltpu.VMEM((layers,) + block, BF16),
            pltpu.VMEM((layers,) + block, BF16),
            pltpu.VMEM((layers,) + block, BF16),
            pltpu.VMEM((2,) + block, F32),
            pltpu.VMEM((experts + 2, 1, 128), F32),
            dma((1,)),
            dma((experts,)),
            dma((experts,)),
            dma((2 * layers,)),
            dma((2 * layers,)),
            dma((layers,)),
            dma((layers,)),
            dma((layers,)),
            dma((layers,)),
            dma((4,)),
            dma((experts,)),
            dma((experts,)),
        ],
        compiler_params=pltpu.CompilerParams(
            collective_id=2, has_side_effects=True, vmem_limit_bytes=VMEM_BYTES
        ),
        name="reduce_grads",
    )(grads, squares)


def adam_update(weight, first_moment, second_moment, gradient, factor, learning_rate, decay_rate):
    clipped = gradient * factor
    first_new = BETA_FIRST * first_moment + (1.0 - BETA_FIRST) * clipped
    second_new = BETA_SECOND * second_moment + (1.0 - BETA_SECOND) * clipped * clipped
    first_hat = first_new / (1.0 - BETA_FIRST**STEP)
    second_hat = second_new / (1.0 - BETA_SECOND**STEP)
    weight_new = weight - learning_rate * (
        first_hat / (jnp.sqrt(second_hat) + ADAM_EPS) + decay_rate * weight
    )
    return (weight_new, first_new, second_new)


def pad_to(array, shape):
    return jnp.pad(array, [(0, full - size) for size, full in zip(array.shape, shape)])


def regroup_weights(blocks, experts):
    rows = D // experts
    if rows == GROUP_ROWS:
        return blocks
    main = blocks[:, :, : 6 * rows].reshape(experts, 2, 3, 2, rows, 128).transpose(1, 2, 3, 0, 4, 5)
    main = main.reshape(2, 3, 2, GROUPS, GROUP_ROWS, 128).transpose(3, 0, 1, 2, 4, 5)
    main = main.reshape(GROUPS, 2, 6 * GROUP_ROWS, 128)
    small_rows = max(experts, 16)
    small = blocks[:, :, 6 * rows :, :rows]
    small = pad_to(small[:, :, :small_rows], (experts, 2, small_rows, rows))
    small = small.transpose(1, 2, 0, 3).reshape(2, small_rows, GROUPS, GROUP_ROWS)
    small = pad_to(small.transpose(2, 0, 1, 3), (GROUPS, 2, small_rows, 128))
    return jnp.concatenate([main, small], axis=2)


def regroup_grads(groups, experts):
    rows = D // experts
    if rows == GROUP_ROWS:
        return groups
    main = groups[:, :, : 6 * GROUP_ROWS].reshape(2, GROUPS, 3, 2, GROUP_ROWS, 128)
    main = main.transpose(0, 2, 3, 1, 4, 5).reshape(2, 3, 2, experts, rows, 128)
    main = main.transpose(0, 3, 1, 2, 4, 5).reshape(2, experts, 6 * rows, 128)
    small = groups[:, :, 6 * GROUP_ROWS :, :GROUP_ROWS]
    small_rows = min(small.shape[2], block_rows(experts) - 6 * rows)
    small = small[:, :, :small_rows].transpose(0, 2, 1, 3).reshape(2, small_rows, experts, rows)
    small = pad_to(small.transpose(0, 2, 1, 3), (2, experts, small_rows, 128))
    both = jnp.concatenate([main, small], axis=2)
    return pad_to(both, (2, experts, block_rows(experts), 128))


def local(
    patches,
    slot_len,
    attn_weight,
    attn_first,
    attn_second,
    phi_weight,
    phi_first,
    phi_second,
    norm_params,
    norm_first,
    norm_second,
    expert_in,
    in_first,
    in_second,
    expert_out,
    out_first,
    out_second,
    cotangent,
):
    experts = lax.axis_size("expert")
    weights = gather_weights(attn_weight, phi_weight.T, norm_params, experts)
    weights = regroup_weights(weights, experts)
    *saved, packed = forward_local(slot_len, patches, weights, cotangent, experts)
    result, gslots, grad_in, grad_out, squares = run_experts(packed, expert_in, expert_out, experts)
    block_output, input_grad, grads = backward_local(
        slot_len, patches, weights, saved, result, gslots, experts
    )
    grads = regroup_grads(grads, experts)
    attn_part, phi_part, norm_part, norm_tile = reduce_grads(grads, squares, experts)
    phi_part = phi_part.T
    grad_norm = norm_tile[0, 0]
    factor = CLIP_NORM / jnp.maximum(grad_norm, CLIP_NORM)
    attn_new, attn_first_new, attn_second_new = adam_update(
        attn_weight, attn_first, attn_second, attn_part, factor, 1.0 / math.sqrt(D), WEIGHT_DECAY
    )
    phi_new, phi_first_new, phi_second_new = adam_update(
        phi_weight, phi_first, phi_second, phi_part, factor, 0.25 / math.sqrt(D), WEIGHT_DECAY
    )
    norm_new, norm_first_new, norm_second_new = adam_update(
        norm_params, norm_first, norm_second, norm_part, factor, 0.8, 0.0
    )
    in_new, in_first_new, in_second_new = adam_update(
        expert_in, in_first, in_second, grad_in, factor, 4.0 / math.sqrt(D), WEIGHT_DECAY
    )
    out_new, out_first_new, out_second_new = adam_update(
        expert_out, out_first, out_second, grad_out, factor, 8.0 / math.sqrt(FF), WEIGHT_DECAY
    )
    return (
        block_output,
        input_grad,
        grad_norm,
        attn_new,
        attn_first_new,
        attn_second_new,
        phi_new,
        phi_first_new,
        phi_second_new,
        norm_new,
        norm_first_new,
        norm_second_new,
        in_new,
        in_first_new,
        in_second_new,
        out_new,
        out_first_new,
        out_second_new,
    )


def solution(mesh):
    in_specs = (
        P(("batch", "expert"), None),
        P(("batch", "expert"), None),
        P("expert", None),
        P("expert", None),
        P("expert", None),
        P("expert", None),
        P("expert", None),
        P("expert", None),
        P(None, "expert"),
        P(None, "expert"),
        P(None, "expert"),
        P("expert", None, "batch"),
        P("expert", None, "batch"),
        P("expert", None, "batch"),
        P("expert", "batch", None),
        P("expert", "batch", None),
        P("expert", "batch", None),
        P(("batch", "expert"), None),
    )
    out_specs = (
        P(("batch", "expert"), None),
        P(("batch", "expert"), None),
        P(),
        P("expert", None),
        P("expert", None),
        P("expert", None),
        P("expert", None),
        P("expert", None),
        P("expert", None),
        P(None, "expert"),
        P(None, "expert"),
        P(None, "expert"),
        P("expert", None, "batch"),
        P("expert", None, "batch"),
        P("expert", None, "batch"),
        P("expert", "batch", None),
        P("expert", "batch", None),
        P("expert", "batch", None),
    )
    return jax.shard_map(local, mesh=mesh, in_specs=in_specs, out_specs=out_specs, check_vma=False)
```

time: 174 us -> 146 us (0.84)
  Pallas kernels: 155 us -> 129 us
  local copies, waits for them, and re-layouts: 8.81 us -> 3.52 us
    pallas_call x1, Pallas kernels: 49.8 us -> 28.4 us  [reduce_grads(): pl.pallas_call(functools.partial(reduce_kernel, experts), out_shape=(shap...]
    pallas_call x1, Pallas kernels: 38.5 us -> 25.1 us  [run_experts(): pl.pallas_call(functools.partial(expert_kernel, experts), out_shape=(shap...]
    pallas_call x1, Pallas kernels: 26.5 us -> 34.7 us  [backward_local(): pl.pallas_call(functools.partial(backward_kernel, experts), out_shape=(sh...]
    sub x5, other arithmetic: 7.28 us -> 11.1 us  [adam_update(): weight - learning_rate * (first_hat / (jnp.sqrt(second_hat) + ADAM_EPS) +...]
    pallas_call x1, Pallas kernels: 18.3 us -> 21.8 us  [forward_local(): pl.pallas_call(functools.partial(forward_kernel, experts), out_shape=(sha...]
    pallas_call x1, Pallas kernels: 21.5 us -> 19.1 us  [gather_weights(): pl.pallas_call(functools.partial(gather_kernel, experts), out_shape=jax.S...]
    slice x2 -> x0, local copies, waits for them, and re-layouts: 2.2 us -> none  [the longest x1 1.19 us: local(): grad_norm = norm_tile[0, 0]]
    unnamed x47 -> x40, local copies, waits for them, and re-layouts: 4.48 us -> 3.52 us
where the time goes in v2:
time: 146 us
  Pallas kernels  129 us (88%)
  other arithmetic  11.1 us (8%)
  local copies, waits for them, and re-layouts  3.52 us (2%)
  between operations  2.7 us (2%)
    pallas_call x1, Pallas kernels, backward_local(): pl.pallas_call(functools.partial(backward_kernel, experts), out_shape=(sh...  34.7 us
    pallas_call x1, Pallas kernels, reduce_grads(): pl.pallas_call(functools.partial(reduce_kernel, experts), out_shape=(shap...  28.4 us
    pallas_call x1, Pallas kernels, run_experts(): pl.pallas_call(functools.partial(expert_kernel, experts), out_shape=(shap...  25.1 us
    pallas_call x1, Pallas kernels, forward_local(): pl.pallas_call(functools.partial(forward_kernel, experts), out_shape=(sha...  21.8 us
    pallas_call x1, Pallas kernels, gather_weights(): pl.pallas_call(functools.partial(gather_kernel, experts), out_shape=jax.S...  19.1 us
    sub x5, other arithmetic, adam_update(): weight - learning_rate * (first_hat / (jnp.sqrt(second_hat) + ADAM_EPS) +...  11.1 us
    unnamed x40, local copies, waits for them, and re-layouts  3.52 us

profile of v2, /device:TPU:0, one launch (start us, length us, event | category | flops | bytes accessed | tf_op | source)
XLA Modules:
  0.0 146.4 jit_solution(16373496110622308734)
XLA Ops:
  0.7 0.0 copy-start.1
  0.7 0.9 copy-done.1
  1.6 0.0 copy-start.3
  1.6 0.7 copy-done.3
  2.3 0.0 copy-start.5
  2.3 0.7 copy-done.5
  2.9 19.1 %gather_weights.1.main_ref = bf16[16,2,160,128]{3,2,1,0:T(8,128)(2,1)S(1)} custom-call(f32[24,1536]{1,0:T(8,128)S(1)} %copy-done.1, f32[16,24]{1,0:T(8,128)S(1)} %bitcast.8, f32[4,24]{1,0:T(4,128)S(1)} %copy-done.5), custom_call_target="tpu_custom_call" | custom-call | tf_op jit(solution)/shard_map/gather_weights/pallas_call | solution.py:180
  22.0 0.0 copy-start
  22.1 1.2 copy-done
  23.2 21.8 %forward_local.1 = (bf16[9,1360,128]{2,1,0:T(8,128)(2,1)}, bf16[1360,384]{1,0:T(8,128)(2,1)}, f32[1360,128]{1,0:T(8,128)}, f32[1360,384]{1,0:T(8,128)}, bf16[136...) custom-call(s32[1,5]{1,0:T(1,128)} %len_ref.3, ...), custom_call_target="tpu_custom_call" | custom-call | tf_op jit(solution)/shard_map/forward_local/pallas_call | solution.py:390
  45.0 25.1 %run_experts.1 = (bf16[128,384]{1,0:T(8,128)(2,1)}, bf16[128,384]{1,0:T(8,128)(2,1)}, f32[1,384,768]{2,1,0:T(8,128)}, f32[1,768,384]{2,1,0:T(8,128)}, f32[1,128]{1,0:T(1,128)}) custom-call(bf16[16,32,128]{2,1,0:T(8,128)(2,1)} %get-tuple-element.47.pack_ref, f32[1,384,768]{2,1,0:T(8,128)} %in_ref.1, f32[1,768,384]{2,1,0:T(8,128)} %out_ref.1), custom_call_target="tpu_custom_call" | custom-call | tf_op jit(solution)/shard_map/run_experts/pallas_call | solution.py:554
  70.1 0.0 copy-start.17
  70.2 0.0 copy-start.18
  70.2 0.0 copy-start.15
  70.2 0.0 copy-start.16
  70.2 0.0 copy-start.14
  70.2 34.7 %backward_local.1 = (bf16[1360,384]{1,0:T(8,128)(2,1)}, bf16[1360,384]{1,0:T(8,128)(2,1)}, f32[2,16,160,128]{3,2,1,0:T(8,128)}) custom-call(s32[1,5]{1,0:T(1,128)} %len_ref.3, bf16[1360,384]{1,0:T(8,128)(2,1)} %patch_ref.3, bf16[16,2,160,128]{3,2,1,0:T(8,128)(2,1)} %copy-done, bf16[9,1360,128]{2,1,0:T(8,128)(2,1)} %get-tuple-element.39.qkv_ref, ...), custom_call_target="tpu_custom_call" | custom-call | tf_op jit(solution)/shard_map/backward_local/pallas_call | solution.py:714
  104.9 0.0 copy-start.6
  104.9 0.0 copy-start.2
  104.9 0.0 copy-start.13
  104.9 0.0 copy-start.7
  104.9 0.0 copy-start.9
  105.0 28.4 %reduce_grads.1 = (f32[24,1536]{1,0:T(8,128)}, f32[16,24]{1,0:T(8,128)}, f32[4,24]{1,0:T(4,128)}, f32[1,128]{1,0:T(1,128)}) custom-call(f32[2,16,160,128]{3,2,1,0:T(8,128)} %get-tuple-element.52.gw_ref, f32[1,128]{1,0:T(1,128)} %get-tuple-element.53.square_ref), custom_call_target="tpu_custom_call" | custom-call | tf_op jit(solution)/shard_map/reduce_grads/pallas_call | solution.py:949
  134.0 0.0 copy-done.17
  134.0 0.0 copy-done.18
  134.0 0.0 copy-done.6
  134.0 1.3 multiply_subtract_fusion.4
  135.3 0.0 copy-done.15
  135.3 0.0 copy-done.16
  135.3 0.0 copy-done.4
  135.3 1.3 multiply_subtract_fusion.3
  136.6 0.0 copy-done.14
  136.6 0.0 copy-done.2
  136.6 0.0 copy-done.13
  136.6 1.7 %multiply_subtract_fusion.2 = (f32[24,1536]{1,0:T(8,128)}, f32[24,1536]{1,0:T(8,128)}, f32[24,1536]{1,0:T(8,128)}) fusion(f32[24,1536]{1,0:T(8,128)S(1)} %copy-done.2, f32[24,1536]{1,0:T(8,128)} %get-tuple-element.55, f32[]{:T(128)S(6)} %div.48, f32[24,1536]{1,0:T(8,128)S(1)} %copy-done.13, f32[24,1536]{1,0:T(8,128)S(1)} %copy-done.14), kind=kLoop, calls=%fused_computation.11 | loop fusion | flops 552960 | bytes 1032196 | tf_op jit(solution)/shard_map/sub | solution.py:996
  138.4 0.0 copy-done.7
  138.4 0.0 copy-done.9
  138.4 0.0 copy-start.10
  138.4 0.0 copy-start.11
  138.4 0.0 copy-start.12
  138.4 4.3 %multiply_subtract_fusion = (f32[1,768,384]{2,1,0:T(8,128)}, f32[1,768,384]{2,1,0:T(8,128)}, f32[1,768,384]{2,1,0:T(8,128)}) fusion(f32[1,768,384]{2,1,0:T(8,128)S(1)} %copy-done.7, f32[1,768,384]{2,1,0:T(8,128)} %get-tuple-element.59, f32[]{:T(128)S(6)} %div.48, f32[1,768,384]{2,1,0:T(8,128)S(1)} %copy-done.9, f32[1,768,384]{2,1,0:T(8,128)} %param.34), kind=kLoop, calls=%fused_computation.6 | loop fusion | flops 4423680 | bytes 8257540 | tf_op jit(solution)/shard_map/sub | solution.py:996
  142.7 0.0 copy-done.8
  142.7 0.0 copy-done.10
  142.7 0.0 copy-done.11
  142.7 0.0 copy-done.12
  142.7 0.0 copy-start.19
  142.7 2.5 %multiply_subtract_fusion.1 = (f32[1,384,768]{2,1,0:T(8,128)}, f32[1,384,768]{2,1,0:T(8,128)}, f32[1,384,768]{2,1,0:T(8,128)}) fusion(f32[1,384,768]{2,1,0:T(8,128)S(1)} %copy-done.8, f32[1,384,768]{2,1,0:T(8,128)S(1)} %copy-done.12, f32[]{:T(128)S(6)} %div.48, f32[1,384,768]{2,1,0:T(8,128)S(1)} %copy-done.10, f32[1,384,768]{2,1,0:T(8,128)S(1)} %copy-done.11), kind=kLoop, calls=%fused_computation.7 | loop fusion | flops 4423680 | bytes 8257540 | tf_op jit(solution)/shard_map/sub | solution.py:996
  145.2 0.0 copy-done.19
  (2 shorter events, 0.0 us)
Async XLA Ops:
  0.7 0.9 copy-start.1
  1.6 0.7 copy-start.3
  2.3 0.7 copy-start.5
  22.0 1.2 copy-start
  70.1 63.8 %copy-start.17 = (f32[4,24]{1,0:T(4,128)S(1)}, f32[4,24]{1,0:T(4,128)}, u32[]{:S(2)}) copy-start(f32[4,24]{1,0:T(4,128)} %param.27) | copy-start | bytes 1156
  70.2 63.8 %copy-start.18 = (f32[4,24]{1,0:T(4,128)S(1)}, f32[4,24]{1,0:T(4,128)}, u32[]{:S(2)}) copy-start(f32[4,24]{1,0:T(4,128)} %param.28) | copy-start | bytes 1156
  70.2 65.1 %copy-start.15 = (f32[24,16]{0,1:T(8,128)S(1)}, f32[24,16]{0,1:T(8,128)}, u32[]{:S(2)}) copy-start(f32[24,16]{0,1:T(8,128)} %param.24) | copy-start | bytes 4612
  70.2 65.1 %copy-start.16 = (f32[24,16]{0,1:T(8,128)S(1)}, f32[24,16]{0,1:T(8,128)}, u32[]{:S(2)}) copy-start(f32[24,16]{0,1:T(8,128)} %param.25) | copy-start | bytes 4612
  70.2 66.4 %copy-start.14 = (f32[24,1536]{1,0:T(8,128)S(1)}, f32[24,1536]{1,0:T(8,128)}, u32[]{:S(2)}) copy-start(f32[24,1536]{1,0:T(8,128)} %param.22) | copy-start | bytes 442372
  104.9 29.1 %copy-start.6 = (f32[4,24]{1,0:T(4,128)S(1)}, f32[4,24]{1,0:T(4,128)}, u32[]{:S(2)}) copy-start(f32[4,24]{1,0:T(4,128)} %norm_ref.1) | copy-start | bytes 1156
  104.9 30.4 %copy-start.4 = (f32[24,16]{0,1:T(8,128)S(1)}, f32[24,16]{0,1:T(8,128)}, u32[]{:S(2)}) copy-start(f32[24,16]{0,1:T(8,128)} %param.23) | copy-start | bytes 4612
  104.9 31.7 %copy-start.2 = (f32[24,1536]{1,0:T(8,128)S(1)}, f32[24,1536]{1,0:T(8,128)}, u32[]{:S(2)}) copy-start(f32[24,1536]{1,0:T(8,128)} %attn_ref.1) | copy-start | bytes 442372
  104.9 31.7 %copy-start.13 = (f32[24,1536]{1,0:T(8,128)S(1)}, f32[24,1536]{1,0:T(8,128)}, u32[]{:S(2)}) copy-start(f32[24,1536]{1,0:T(8,128)} %param.21) | copy-start | bytes 442372
  104.9 33.5 %copy-start.7 = (f32[1,768,384]{2,1,0:T(8,128)S(1)}, f32[1,768,384]{2,1,0:T(8,128)}, u32[]{:S(2)}) copy-start(f32[1,768,384]{2,1,0:T(8,128)} %out_ref.1) | copy-start | bytes 3538948
  104.9 33.5 %copy-start.9 = (f32[1,768,384]{2,1,0:T(8,128)S(1)}, f32[1,768,384]{2,1,0:T(8,128)}, u32[]{:S(2)}) copy-start(f32[1,768,384]{2,1,0:T(8,128)} %param.33) | copy-start | bytes 3538948
  138.4 4.3 %copy-start.8 = (f32[1,384,768]{2,1,0:T(8,128)S(1)}, f32[1,384,768]{2,1,0:T(8,128)}, u32[]{:S(2)}) copy-start(f32[1,384,768]{2,1,0:T(8,128)} %in_ref.1) | copy-start | bytes 3538948
  138.4 4.3 %copy-start.10 = (f32[1,384,768]{2,1,0:T(8,128)S(1)}, f32[1,384,768]{2,1,0:T(8,128)}, u32[]{:S(2)}) copy-start(f32[1,384,768]{2,1,0:T(8,128)} %param.30) | copy-start | bytes 3538948
  138.4 4.3 %copy-start.11 = (f32[1,384,768]{2,1,0:T(8,128)S(1)}, f32[1,384,768]{2,1,0:T(8,128)}, u32[]{:S(2)}) copy-start(f32[1,384,768]{2,1,0:T(8,128)} %param.31) | copy-start | bytes 3538948
  138.4 4.3 %copy-start.12 = (f32[1,384,768]{2,1,0:T(8,128)S(1)}, f32[1,384,768]{2,1,0:T(8,128)}, u32[]{:S(2)}) copy-start(f32[1,384,768]{2,1,0:T(8,128)} %get-tuple-element.58) | copy-start | bytes 3538948
  142.7 2.5 %copy-start.19 = (f32[1,128]{1,0:T(1,128)S(1)}, f32[1,128]{1,0:T(1,128)}, u32[]{:S(2)}) copy-start(f32[1,128]{1,0:T(1,128)} %get-tuple-element.54) | copy-start | bytes 1540

commit v3 on v2

--- a/solution.py
+++ b/solution.py
@@ -20,6 +20,9 @@
 PAIRS = 3
 GROUPS = 16
 GROUP_ROWS = D // GROUPS
+LONG_WINDOW = 592
+LONG_SPAN = 640
+WINDOW_PAD = 48
 
 NORM_EPS = 1e-06
 CLIP_NORM = 1.0
@@ -33,7 +36,10 @@
 MESH = pl.DeviceIdType.MESH
 F32 = jnp.float32
 BF16 = jnp.bfloat16
-VMEM_BYTES = 58 * 1024 * 1024
+
+
+def vmem_bytes(experts, mebibytes):
+    return (mebibytes if experts <= 16 else 58) * 1024 * 1024
 
 
 def whole(count):
@@ -69,10 +75,18 @@
     return core, chip, first, second
 
 
-def gather_kernel(experts, attn_ref, phi_ref, norm_ref, out, stage, send_z, send_first,
-                  send_second, send_pair, recv, recv_pair):
+def gather_kernel(experts, attn_hbm, phi_hbm, norm_hbm, out, stage, attn_ref, phi_ref, norm_ref, load_sem,
+                  send_z, send_first, send_second, send_pair, recv, recv_pair):
     core, chip, first, second = ring(experts)
     rows = attn_ref.shape[0]
+    half = pl.multiple_of(core * (2 * D), 128)
+    loads = [
+        pltpu.make_async_copy(attn_hbm.at[:, pl.ds(half, 2 * D)], attn_ref, load_sem.at[0]),
+        pltpu.make_async_copy(phi_hbm, phi_ref, load_sem.at[1]),
+        pltpu.make_async_copy(norm_hbm, norm_ref, load_sem.at[2]),
+    ]
+    for load in loads:
+        load.start()
     column = lax.rem(chip, 4)
     layers = experts // 4
     layer = chip // 4
@@ -87,11 +101,13 @@
     pl.semaphore_signal(barrier, inc=1, device_id=(core, second), device_id_type=MESH)
     pl.semaphore_signal(barrier, inc=1, device_id=(1 - core, chip), device_id_type=MESH)
     stage[...] = jnp.zeros_like(stage)
+    for load in loads:
+        load.wait()
     for part in range(2):
         for g in range(3):
-            lanes = pl.multiple_of(core * (2 * D) + (part * D + g * 128), 128)
+            lanes = part * D + g * 128
             place = (2 * g + part) * rows
-            stage[place : place + rows, :] = attn_ref[:, pl.ds(lanes, 128)]
+            stage[place : place + rows, :] = attn_ref[:, lanes : lanes + 128]
 
     @pl.when(core == 0)
     def _():
@@ -180,12 +196,19 @@
     return pl.pallas_call(
         functools.partial(gather_kernel, experts),
         out_shape=jax.ShapeDtypeStruct((experts, 2, rows, 128), BF16),
-        in_specs=whole(3),
+        in_specs=[pl.BlockSpec(memory_space=pltpu.HBM)] * 3,
         out_specs=whole(1)[0],
-        scratch_shapes=[pltpu.VMEM((rows, 128), F32), dma((experts // 4,))]
+        scratch_shapes=[
+            pltpu.VMEM((rows, 128), F32),
+            pltpu.VMEM((attn_weight.shape[0], 2 * D), F32),
+            pltpu.VMEM(phi_turned.shape, F32),
+            pltpu.VMEM(norm_params.shape, F32),
+            dma((3,)),
+            dma((experts // 4,)),
+        ]
         + [dma((experts,))] * 5,
         compiler_params=pltpu.CompilerParams(
-            collective_id=0, has_side_effects=True, vmem_limit_bytes=16 * 1024 * 1024
+            collective_id=0, has_side_effects=True, vmem_limit_bytes=vmem_bytes(experts, 3)
         ),
         name="gather_weights",
     )(attn_weight, phi_turned, norm_params)
@@ -278,16 +301,21 @@
     lax.fori_loop(0, IMAGES, step, jnp.int32(0))
 
 
-def window_masks(shift, full, window):
-    column = lax.broadcasted_iota(jnp.int32, (1, window), 1)
-    row = lax.broadcasted_iota(jnp.int32, (window, 1), 0)
-    bias = jnp.where((column >= shift) & (column < shift + full), 0.0, MASKED)
-    inside = (row >= shift) & (row < shift + full)
-    return bias, inside
-
-
-def forward_kernel(experts, len_ref, patch_ref, main_ref, cot_ref, qkv_ref, o_ref, lse_ref, x1_ref,
-                   h2_ref, disp_ref, comb_ref, gy_ref, pack_ref, logit, packf):
+def rows_inside(shift, full, first, count):
+    row = first + lax.broadcasted_iota(jnp.int32, (count, 1), 0)
+    return (row >= shift) & (row < shift + full)
+
+
+def columns_inside(shift, full, count):
+    column = lax.broadcasted_iota(jnp.int32, (1, count), 1)
+    return (column >= shift) & (column < shift + full)
+
+
+def forward_kernel(experts, len_ref, patch_ref, main_ref, cot_hbm, qkv_ref, o_ref, lse_ref, x1_ref,
+                   h2_ref, disp_ref, comb_ref, gy_ref, pack_ref, logit, packf, scores,
+                   probs, peaks, cot_ref, load_sem):
+    load = pltpu.make_async_copy(cot_hbm, cot_ref, load_sem.at[0])
+    load.start()
     tokens = patch_ref.shape[0]
     columns = experts * SLOT_ROWS
     tile = tokens // 5
@@ -303,31 +331,42 @@
         qkv = mm(h1, w_qkv).astype(BF16)
         for c in range(9):
             qkv_ref[c, rows, :] = qkv[:, c * 128 : (c + 1) * 128]
+    qkv_ref[:, tokens:, :] = jnp.zeros((9, WINDOW_PAD, 128), BF16)
     o_ref[...] = jnp.zeros_like(o_ref)
     lse_ref[...] = jnp.zeros_like(lse_ref)
     low_lane = lax.broadcasted_iota(jnp.int32, (1, 128), 1) < HEAD_DIM
     lane = lax.broadcasted_iota(jnp.int32, (1, 128), 1)
 
     def attend(first, shift, full, window):
-        bias, inside = window_masks(shift, full, window)
+        span = round_up(window, 128)
+        bias = jnp.where(columns_inside(shift, full, span), 0.0, MASKED)
+        inside = rows_inside(shift, full, 0, window)
         rows = pl.ds(first, window)
+        wide = pl.ds(first, span)
 
         @pl.loop(0, PAIRS)
         def _(p):
             query = qkv_ref[p, rows, :].astype(F32) * SCORE_SCALE
-            keys = qkv_ref[PAIRS + p, rows, :]
-            values = qkv_ref[2 * PAIRS + p, rows, :]
+            keys = qkv_ref[PAIRS + p, wide, :]
+            ones = jnp.ones((span, 128), BF16)
+            values = jnp.concatenate([qkv_ref[2 * PAIRS + p, wide, :], ones], axis=1)
+            for h in range(2):
+                mine = low_lane if h == 0 else jnp.logical_not(low_lane)
+                scores[h, :window, :span] = mm_nt(jnp.where(mine, query, 0.0).astype(BF16), keys)
+            for h in range(2):
+                for r in range(0, window, 16):
+                    part = scores[h, r : r + 16, :span] + bias
+                    peak = jnp.max(part, axis=-1, keepdims=True)
+                    probs[h, r : r + 16, :span] = jnp.exp(part - peak).astype(BF16)
+                    peaks[h, r : r + 16, :] = jnp.broadcast_to(peak, (16, 128))
             outs = []
             sums = lse_ref[rows, :]
             for h in range(2):
-                mine = low_lane if h == 0 else jnp.logical_not(low_lane)
-                scores = mm_nt(jnp.where(mine, query, 0.0).astype(BF16), keys) + bias
-                peak = jnp.max(scores, axis=-1, keepdims=True)
-                exponent = jnp.exp(scores - peak)
-                summed = jnp.sum(exponent, axis=-1, keepdims=True)
-                probs = (exponent * (1.0 / summed)).astype(BF16)
-                outs.append(mm(probs, values))
-                sums = jnp.where(inside & (lane == 2 * p + h), peak + jnp.log(summed), sums)
+                both = mm(probs[h, :window, :span], values)
+                summed = both[:, 128:]
+                outs.append(both[:, :128] * (1.0 / summed))
+                logs = peaks[h, :window, :] + jnp.log(summed)
+                sums = jnp.where(inside & (lane == 2 * p + h), logs, sums)
             lse_ref[rows, :] = sums
             lanes = pl.ds(pl.multiple_of(p * 128, 128), 128)
             old = o_ref[rows, lanes].astype(F32)
@@ -336,6 +375,7 @@
 
     over_images(len_ref, tokens, attend)
 
+    load.wait()
     w_o = unpack_weight(main_ref, 1, 1)
     for t in range(5):
         rows = pl.ds(t * tile, tile)
@@ -390,9 +430,9 @@
     return pl.pallas_call(
         functools.partial(forward_kernel, experts),
         out_shape=(
-            shape((9, tokens, 128), BF16),
-            shape((tokens, D), BF16),
-            shape((tokens, 128), F32),
+            shape((9, tokens + WINDOW_PAD, 128), BF16),
+            shape((tokens + WINDOW_PAD, D), BF16),
+            shape((tokens + WINDOW_PAD, 128), F32),
             shape((tokens, D), F32),
             shape((tokens, D), BF16),
             shape((tokens, columns), F32),
@@ -400,10 +440,20 @@
             shape((tokens, D), BF16),
             shape((experts, 32, 128), BF16),
         ),
-        in_specs=[pl.BlockSpec(memory_space=pltpu.SMEM)] + whole(3),
+        in_specs=[pl.BlockSpec(memory_space=pltpu.SMEM)]
+        + whole(2)
+        + [pl.BlockSpec(memory_space=pltpu.HBM)],
         out_specs=tuple(whole(9)),
-        scratch_shapes=[pltpu.VMEM((tokens, columns), F32), pltpu.VMEM((experts, 16, 128), F32)],
-        compiler_params=pltpu.CompilerParams(vmem_limit_bytes=VMEM_BYTES),
+        scratch_shapes=[
+            pltpu.VMEM((tokens, columns), F32),
+            pltpu.VMEM((experts, 16, 128), F32),
+            pltpu.VMEM((2, LONG_WINDOW, LONG_SPAN), F32),
+            pltpu.VMEM((2, LONG_WINDOW, LONG_SPAN), BF16),
+            pltpu.VMEM((2, LONG_WINDOW, 128), F32),
+            pltpu.VMEM((tokens, D), BF16),
+            pltpu.SemaphoreType.DMA((1,)),
+        ],
+        compiler_params=pltpu.CompilerParams(vmem_limit_bytes=vmem_bytes(experts, 22)),
         name="forward_local",
     )(lengths, patches, main, cotangent)
 
@@ -576,7 +626,7 @@
         + [dma((experts,))] * 6
         + [dma((2,))],
         compiler_params=pltpu.CompilerParams(
-            collective_id=1, has_side_effects=True, vmem_limit_bytes=VMEM_BYTES
+            collective_id=1, has_side_effects=True, vmem_limit_bytes=vmem_bytes(experts, 8)
         ),
         name="run_experts",
     )(packed, expert_in, expert_out)
@@ -585,7 +635,7 @@
 def backward_kernel(experts, len_ref, patch_ref, main_ref, qkv_ref, o_ref, lse_ref,
                     x1_ref, h2_ref, disp_ref, comb_ref, gy_ref, result_ref, gslot_ref, block_ref,
                     input_ref, gw_ref, gdisp, glog, gx1, branch, go, gqkv,
-                    h1_all):
+                    h1_all, scores, grad_probs, probs, grad_scores, sums):
     tokens = patch_ref.shape[0]
     columns = experts * SLOT_ROWS
     tile = tokens // 5
@@ -642,39 +692,60 @@
                 :, g * 128 : (g + 1) * 128
             ].reshape(GROUPS, GROUP_ROWS, 128)
 
-    put(1, 1, mm_tn(o_ref[...], branch[...]))
+    put(1, 1, mm_tn(o_ref[0:tokens, :], branch[...]))
 
     gqkv[...] = jnp.zeros_like(gqkv)
+    go[:, tokens:, :] = jnp.zeros((PAIRS, WINDOW_PAD, 128), BF16)
     low_lane = lax.broadcasted_iota(jnp.int32, (1, 128), 1) < HEAD_DIM
-    lane = lax.broadcasted_iota(jnp.int32, (1, 128), 1)
+
+    head_row = lax.broadcasted_iota(jnp.int32, (8, 128), 0)
+    head_lane = lax.broadcasted_iota(jnp.int32, (8, 128), 1)
+    heads = jnp.where(head_row == head_lane // HEAD_DIM, 1.0, 0.0).astype(BF16)
 
     def attend(first, shift, full, window):
-        bias, inside = window_masks(shift, full, window)
+        span = round_up(window, 128)
+        inside = rows_inside(shift, full, 0, window)
+        queries_inside = columns_inside(shift, full, span)
         rows = pl.ds(first, window)
-        sums = lse_ref[rows, :]
+        wide = pl.ds(first, span)
+        sums[:, :span] = jnp.transpose(lse_ref[wide, :])
 
         @pl.loop(0, PAIRS)
         def _(p):
-            query_low = qkv_ref[p, rows, :]
-            query = query_low.astype(F32) * SCORE_SCALE
-            keys = qkv_ref[PAIRS + p, rows, :]
-            values = qkv_ref[2 * PAIRS + p, rows, :]
-            grads_low = go[p, rows, :]
-            grads = grads_low.astype(F32)
+            lanes = pl.ds(pl.multiple_of(p * 128, 128), 128)
+            query = qkv_ref[p, wide, :]
+            keys_low = qkv_ref[PAIRS + p, rows, :]
+            keys = keys_low.astype(F32) * SCORE_SCALE
+            values = qkv_ref[2 * PAIRS + p, rows, :].astype(F32)
+            grads = go[p, wide, :]
+            product = grads.astype(F32) * o_ref[wide, lanes].astype(F32)
+            upper = product.astype(BF16)
+            lower = (product - upper.astype(F32)).astype(BF16)
+            inner_rows = mm_nt(heads, upper) + mm_nt(heads, lower)
+            for h in range(2):
+                mine = low_lane if h == 0 else jnp.logical_not(low_lane)
+                scores[h, :window, :span] = mm_nt(jnp.where(mine, keys, 0.0).astype(BF16), query)
+                grad_probs[h, :window, :span] = mm_nt(
+                    jnp.where(mine, values, 0.0).astype(BF16), grads
+                )
+            for h in range(2):
+                logs = jnp.where(queries_inside, sums[pl.ds(2 * p + h, 1), :span], 1e30)
+                inner_row = inner_rows[h : h + 1]
+                for r in range(0, window, 16):
+                    part = jnp.exp(scores[h, r : r + 16, :span] - logs)
+                    if r == 0 or r + 16 > full:
+                        part = jnp.where(rows_inside(shift, full, r, 16), part, 0.0)
+                    probs[h, r : r + 16, :span] = part.astype(BF16)
+                    slope = part * (grad_probs[h, r : r + 16, :span] - inner_row)
+                    grad_scores[h, r : r + 16, :span] = slope.astype(BF16)
             parts = []
             for h in range(2):
-                mine = low_lane if h == 0 else jnp.logical_not(low_lane)
-                scores = mm_nt(jnp.where(mine, query, 0.0).astype(BF16), keys) + bias
-                summed = jnp.sum(jnp.where(lane == 2 * p + h, sums, 0.0), axis=-1, keepdims=True)
-                probs = jnp.exp(scores - jnp.where(inside, summed, 1e30))
-                grad_probs = mm_nt(jnp.where(mine, grads, 0.0).astype(BF16), values)
-                dot = jnp.sum(probs * grad_probs, axis=-1, keepdims=True)
-                grad_scores = (probs * (grad_probs - dot)).astype(BF16)
+                slopes = grad_scores[h, :window, :span]
                 parts.append(
                     (
-                        mm(grad_scores, keys) * SCORE_SCALE,
-                        mm_tn(grad_scores, query_low) * SCORE_SCALE,
-                        mm_tn(probs.astype(BF16), grads_low),
+                        mm_tn(slopes, keys_low)[:window] * SCORE_SCALE,
+                        mm(slopes, query) * SCORE_SCALE,
+                        mm(probs[h, :window, :span], grads),
                     )
                 )
             for c in range(3):
@@ -725,11 +796,16 @@
             pltpu.VMEM((tokens, columns), BF16),
             pltpu.VMEM((tokens, D), F32),
             pltpu.VMEM((tokens, D), BF16),
-            pltpu.VMEM((PAIRS, tokens, 128), BF16),
+            pltpu.VMEM((PAIRS, tokens + WINDOW_PAD, 128), BF16),
             pltpu.VMEM((9, tokens, 128), BF16),
             pltpu.VMEM((tokens, D), BF16),
+            pltpu.VMEM((2, LONG_WINDOW, LONG_SPAN), F32),
+            pltpu.VMEM((2, LONG_WINDOW, LONG_SPAN), F32),
+            pltpu.VMEM((2, LONG_WINDOW, LONG_SPAN), BF16),
+            pltpu.VMEM((2, LONG_WINDOW, LONG_SPAN), BF16),
+            pltpu.VMEM((128, LONG_SPAN), F32),
         ],
-        compiler_params=pltpu.CompilerParams(vmem_limit_bytes=VMEM_BYTES),
+        compiler_params=pltpu.CompilerParams(vmem_limit_bytes=vmem_bytes(experts, 28)),
         name="backward_local",
     )(lengths, patches, main, *saved, result, gslots)
 
@@ -981,7 +1057,7 @@
             dma((experts,)),
         ],
         compiler_params=pltpu.CompilerParams(
-            collective_id=2, has_side_effects=True, vmem_limit_bytes=VMEM_BYTES
+            collective_id=2, has_side_effects=True, vmem_limit_bytes=vmem_bytes(experts, 8)
         ),
         name="reduce_grads",
     )(grads, squares)
@@ -997,6 +1073,56 @@
         first_hat / (jnp.sqrt(second_hat) + ADAM_EPS) + decay_rate * weight
     )
     return (weight_new, first_new, second_new)
+
+
+RATES = (
+    (1.0 / math.sqrt(D), WEIGHT_DECAY),
+    (0.25 / math.sqrt(D), WEIGHT_DECAY),
+    (0.8, 0.0),
+    (4.0 / math.sqrt(D), WEIGHT_DECAY),
+    (8.0 / math.sqrt(FF), WEIGHT_DECAY),
+)
+UPDATE_STEPS = 4
+
+
+def update_kernel(norm_ref, *refs):
+    grad_norm = norm_ref[...]
+    factor = CLIP_NORM / jnp.maximum(grad_norm, CLIP_NORM)
+    factor = factor[0:1, 0:1]
+    inputs, outputs = refs[:20], refs[20:]
+    for k, (rate, decay) in enumerate(RATES):
+        weight, first, second, grad = (ref[...] for ref in inputs[4 * k : 4 * k + 4])
+        by = factor.reshape((1,) * grad.ndim)
+        news = adam_update(weight, first, second, grad, by, rate, decay)
+        for ref, new in zip(outputs[3 * k : 3 * k + 3], news):
+            ref[...] = new
+
+
+def update(norm_tile, groups):
+    def spec(k, shape):
+        if k == 0:
+            return pl.BlockSpec((shape[0], shape[1] // UPDATE_STEPS), lambda i: (0, i))
+        if k < 3:
+            return pl.BlockSpec(shape, lambda i: (0, 0))
+        return pl.BlockSpec((1, shape[1] // UPDATE_STEPS, shape[2]), lambda i: (0, i, 0))
+
+    specs = [spec(k, group[0].shape) for k, group in enumerate(groups)]
+    return pl.pallas_call(
+        update_kernel,
+        grid=(UPDATE_STEPS,),
+        out_shape=tuple(
+            jax.ShapeDtypeStruct(group[0].shape, F32) for group in groups for _ in range(3)
+        ),
+        in_specs=[pl.BlockSpec((1, 128), lambda i: (0, 0))]
+        + [one for one in specs for _ in range(4)],
+        out_specs=tuple(one for one in specs for _ in range(3)),
+        compiler_params=pltpu.CompilerParams(vmem_limit_bytes=24 * 1024 * 1024),
+        name="update",
+    )(norm_tile, *[array for group in groups for array in group])
+
+
+def in_hbm(array):
+    return pltpu.with_memory_space_constraint(array, pltpu.HBM)
 
 
 def pad_to(array, shape):
@@ -1054,33 +1180,35 @@
     cotangent,
 ):
     experts = lax.axis_size("expert")
-    weights = gather_weights(attn_weight, phi_weight.T, norm_params, experts)
+    weights = gather_weights(
+        in_hbm(attn_weight), in_hbm(phi_weight.T), in_hbm(norm_params), experts
+    )
     weights = regroup_weights(weights, experts)
-    *saved, packed = forward_local(slot_len, patches, weights, cotangent, experts)
+    *saved, packed = forward_local(
+        slot_len, patches, weights, in_hbm(cotangent), experts
+    )
     result, gslots, grad_in, grad_out, squares = run_experts(packed, expert_in, expert_out, experts)
     block_output, input_grad, grads = backward_local(
         slot_len, patches, weights, saved, result, gslots, experts
     )
     grads = regroup_grads(grads, experts)
     attn_part, phi_part, norm_part, norm_tile = reduce_grads(grads, squares, experts)
-    phi_part = phi_part.T
+    news = update(
+        norm_tile,
+        (
+            (attn_weight, attn_first, attn_second, attn_part),
+            (phi_weight.T, phi_first.T, phi_second.T, phi_part),
+            (norm_params, norm_first, norm_second, norm_part),
+            (expert_in, in_first, in_second, grad_in),
+            (expert_out, out_first, out_second, grad_out),
+        ),
+    )
+    attn_new, attn_first_new, attn_second_new = news[0:3]
+    phi_new, phi_first_new, phi_second_new = (new.T for new in news[3:6])
+    norm_new, norm_first_new, norm_second_new = news[6:9]
+    in_new, in_first_new, in_second_new = news[9:12]
+    out_new, out_first_new, out_second_new = news[12:15]
     grad_norm = norm_tile[0, 0]
-    factor = CLIP_NORM / jnp.maximum(grad_norm, CLIP_NORM)
-    attn_new, attn_first_new, attn_second_new = adam_update(
-        attn_weight, attn_first, attn_second, attn_part, factor, 1.0 / math.sqrt(D), WEIGHT_DECAY
-    )
-    phi_new, phi_first_new, phi_second_new = adam_update(
-        phi_weight, phi_first, phi_second, phi_part, factor, 0.25 / math.sqrt(D), WEIGHT_DECAY
-    )
-    norm_new, norm_first_new, norm_second_new = adam_update(
-        norm_params, norm_first, norm_second, norm_part, factor, 0.8, 0.0
-    )
-    in_new, in_first_new, in_second_new = adam_update(
-        expert_in, in_first, in_second, grad_in, factor, 4.0 / math.sqrt(D), WEIGHT_DECAY
-    )
-    out_new, out_first_new, out_second_new = adam_update(
-        expert_out, out_first, out_second, grad_out, factor, 8.0 / math.sqrt(FF), WEIGHT_DECAY
-    )
     return (
         block_output,
         input_grad,

time: 146 us -> 111 us (0.76)
  Pallas kernels: 129 us -> 108 us
  other arithmetic: 11.1 us -> 0 us
  local copies, waits for them, and re-layouts: 3.52 us -> 0.1 us
    sub x5 -> x0, other arithmetic: 11.1 us -> none  [adam_update(): weight - learning_rate * (first_hat / (jnp.sqrt(second_hat) + ADAM_EPS) +...]
    pallas_call x1, Pallas kernels: 34.7 us -> 24.9 us  [backward_local(): pl.pallas_call(functools.partial(backward_kernel, experts), out_shape=(sh...]
    pallas_call x1, Pallas kernels: 21.8 us -> 14.9 us  [forward_local(): pl.pallas_call(functools.partial(forward_kernel, experts), out_shape=(sha...]
    pallas_call x1, Pallas kernels: 25.1 us -> 19.6 us  [run_experts(): pl.pallas_call(functools.partial(expert_kernel, experts), out_shape=(shap...]
    pallas_call x0 -> x1, Pallas kernels: none -> 4.9 us  [update(): pl.pallas_call(update_kernel, grid=(UPDATE_STEPS,), out_shape=tuple((jax....]
    pallas_call x1, Pallas kernels: 28.4 us -> 24.7 us  [reduce_grads(): pl.pallas_call(functools.partial(reduce_kernel, experts), out_shape=(shap...]
    unnamed x40 -> x34, local copies, waits for them, and re-layouts: 3.52 us -> 0.1 us
where the time goes in v3:
time: 111 us; the launch traced here: 110 us
  Pallas kernels  108 us (97%)
  between operations  2.13 us (2%)
    pallas_call x1, Pallas kernels, backward_local(): pl.pallas_call(functools.partial(backward_kernel, experts), out_shape=(sh...  24.9 us
    pallas_call x1, Pallas kernels, reduce_grads(): pl.pallas_call(functools.partial(reduce_kernel, experts), out_shape=(shap...  24.7 us
    pallas_call x1, Pallas kernels, run_experts(): pl.pallas_call(functools.partial(expert_kernel, experts), out_shape=(shap...  19.6 us
    pallas_call x1, Pallas kernels, gather_weights(): pl.pallas_call(functools.partial(gather_kernel, experts), out_shape=jax.S...  19.2 us
    pallas_call x1, Pallas kernels, forward_local(): pl.pallas_call(functools.partial(forward_kernel, experts), out_shape=(sha...  14.9 us
    pallas_call x1, Pallas kernels, update(): pl.pallas_call(update_kernel, grid=(UPDATE_STEPS,), out_shape=tuple((jax....  4.9 us

profile of v3, /device:TPU:0, one launch (start us, length us, event | category | flops | bytes accessed | tf_op | source)
XLA Modules:
  0.0 110.4 jit_solution(16679834616650083020)
XLA Ops:
  0.7 0.0 copy-start.16
  0.7 0.0 copy-start.2
  0.7 19.2 %gather_weights.1.main_ref = bf16[16,2,160,128]{3,2,1,0:T(8,128)(2,1)S(1)} custom-call(f32[24,1536]{1,0:T(8,128)} %refs_0_.1, f32[16,24]{1,0:T(8,128)} %bitcast.8, f32[4,24]{1,0:T(4,128)} %refs_8_.1), custom_call_target="tpu_custom_call" | custom-call | tf_op jit(solution)/shard_map/gather_weights/pallas_call | solution.py:196
  19.8 0.0 copy-done.16
  19.9 0.0 copy-done.2
  19.9 0.0 copy-start
  19.9 0.0 copy-start.1
  19.9 14.9 %forward_local.1 = (bf16[9,1408,128]{2,1,0:T(8,128)(2,1)S(1)}, bf16[1408,384]{1,0:T(8,128)(2,1)S(1)}, f32[1408,128]{1,0:T(8,128)S(1)}, f32[1360,384]{1,0:T(8,128...) custom-call(s32[1,5]{1,0:T(1,128)S(1)} %copy-done.16, ...), custom_call_target="tpu_custom_call" | custom-call | tf_op jit(solution)/shard_map/forward_local/pallas_call | solution.py:430
  34.8 0.0 copy-done
  34.8 0.0 copy-done.1
  34.8 19.6 %run_experts.1 = (bf16[128,384]{1,0:T(8,128)(2,1)S(1)}, bf16[128,384]{1,0:T(8,128)(2,1)S(1)}, f32[1,384,768]{2,1,0:T(8,128)S(1)}, f32[1,768,384]{2,1,0:T(8,128)S(1)}, f32[1,128]{1,0:T(1,128)S(1)}) custom-call(bf16[16,32,128]{2,1,0:T(8,128)(2,1)S(1)} %get-tuple-element.62.pack_ref, f32[1,384,768]{2,1,0:T(8,128)S(1)} %copy-done, f32[1,768,384]{2,1,0:T(8,128)S(1)} %copy-done.1), custom_call_target="tpu_custom_call" | custom-call | tf_op jit(solution)/shard_map/run_experts/pallas_call | solution.py:604
  54.4 0.0 copy-start.5
  54.5 0.0 copy-start.6
  54.5 0.0 copy-start.8
  54.5 0.0 copy-start.9
  54.5 24.9 %backward_local.1 = (bf16[1360,384]{1,0:T(8,128)(2,1)}, bf16[1360,384]{1,0:T(8,128)(2,1)}, f32[2,16,160,128]{3,2,1,0:T(8,128)S(1)}) custom-call(s32[1,5]{1,0:T(1,128)S(1)} %copy-done.16, bf16[1360,384]{1,0:T(8,128)(2,1)S(1)} %copy-done.2, bf16[16,2,160,128]{3,2,1,0:T(8,128)(2,1)S(1)} %gather_weights.1.main_ref, ...), custom_call_target="tpu_custom_call" | custom-call | tf_op jit(solution)/shard_map/backward_local/pallas_call | solution.py:785
  79.4 0.0 copy-start.3
  79.4 0.0 copy-start.4
  79.4 0.0 copy-start.7
  79.4 0.0 copy-start.10
  79.5 0.0 copy-start.11
  79.5 0.0 copy-start.12
  79.5 0.0 copy-start.13
  79.5 0.0 copy-start.14
  79.5 0.0 copy-start.15
  79.5 24.7 %reduce_grads.1 = (f32[24,1536]{1,0:T(8,128)S(1)}, f32[16,24]{1,0:T(8,128)S(1)}, f32[4,24]{1,0:T(4,128)S(1)}, f32[1,128]{1,0:T(1,128)S(1)}) custom-call(f32[2,16,160,128]{3,2,1,0:T(8,128)S(1)} %get-tuple-element.67.gw_ref, f32[1,128]{1,0:T(1,128)S(1)} %get-tuple-element.68.square_ref), custom_call_target="tpu_custom_call" | custom-call | tf_op jit(solution)/shard_map/reduce_grads/pallas_call | solution.py:1025
  104.2 0.0 copy-done.5
  104.2 0.0 copy-done.6
  104.3 0.0 copy-done.8
  104.3 0.0 copy-done.9
  104.3 0.0 copy-done.3
  104.3 0.0 copy-done.4
  104.3 0.0 copy-done.7
  104.3 0.0 copy-done.10
  104.3 0.0 copy-done.11
  104.3 0.0 copy-done.12
  104.3 0.0 copy-done.13
  104.3 0.0 copy-done.14
  104.4 0.0 copy-done.15
  104.4 4.9 %update.1 = (f32[24,1536]{1,0:T(8,128)}, f32[24,1536]{1,0:T(8,128)}, f32[24,1536]{1,0:T(8,128)}, f32[16,24]{1,0:T(8,128)}, f32[16,24]{1,0:T(8,128)}, /*index=5*/...) custom-call(f32[1,128]{1,0:T(1,128)S(1)} %get-tuple-element.69.norm_, ...), custom_call_target="tpu_custom_call" | custom-call | tf_op jit(solution)/shard_map/update/pallas_call | solution.py:1110
Async XLA Ops:
  0.7 19.2 %copy-start.16 = (s32[1,5]{1,0:T(1,128)S(1)}, s32[1,5]{1,0:T(1,128)}, u32[]{:S(2)}) copy-start(s32[1,5]{1,0:T(1,128)} %len_ref.3) | copy-start | bytes 64
  0.7 19.2 %copy-start.2 = (bf16[1360,384]{1,0:T(8,128)(2,1)S(1)}, bf16[1360,384]{1,0:T(8,128)(2,1)}, u32[]{:S(2)}) copy-start(bf16[1360,384]{1,0:T(8,128)(2,1)} %patch_ref.3) | copy-start | bytes 3133444
  19.9 14.9 %copy-start = (f32[1,384,768]{2,1,0:T(8,128)S(1)}, f32[1,384,768]{2,1,0:T(8,128)}, u32[]{:S(2)}) copy-start(f32[1,384,768]{2,1,0:T(8,128)} %refs_12_.1) | copy-start | bytes 3538948
  19.9 14.9 %copy-start.1 = (f32[1,768,384]{2,1,0:T(8,128)S(1)}, f32[1,768,384]{2,1,0:T(8,128)}, u32[]{:S(2)}) copy-start(f32[1,768,384]{2,1,0:T(8,128)} %refs_16_.1) | copy-start | bytes 3538948
  54.4 49.8 %copy-start.5 = (f32[1,768,384]{2,1,0:T(8,128)S(1)}, f32[1,768,384]{2,1,0:T(8,128)}, u32[]{:S(2)}) copy-start(f32[1,768,384]{2,1,0:T(8,128)} %refs_17_.1) | copy-start | bytes 3538948
  54.5 49.8 %copy-start.6 = (f32[1,768,384]{2,1,0:T(8,128)S(1)}, f32[1,768,384]{2,1,0:T(8,128)}, u32[]{:S(2)}) copy-start(f32[1,768,384]{2,1,0:T(8,128)} %refs_18_.1) | copy-start | bytes 3538948
  54.5 49.8 %copy-start.8 = (f32[24,1536]{1,0:T(8,128)S(1)}, f32[24,1536]{1,0:T(8,128)}, u32[]{:S(2)}) copy-start(f32[24,1536]{1,0:T(8,128)} %refs_1_.1) | copy-start | bytes 442372
  54.5 49.8 %copy-start.9 = (f32[24,1536]{1,0:T(8,128)S(1)}, f32[24,1536]{1,0:T(8,128)}, u32[]{:S(2)}) copy-start(f32[24,1536]{1,0:T(8,128)} %refs_2_.1) | copy-start | bytes 442372
  79.4 24.9 %copy-start.3 = (f32[1,384,768]{2,1,0:T(8,128)S(1)}, f32[1,384,768]{2,1,0:T(8,128)}, u32[]{:S(2)}) copy-start(f32[1,384,768]{2,1,0:T(8,128)} %refs_13_.1) | copy-start | bytes 3538948
  79.4 24.9 %copy-start.4 = (f32[1,384,768]{2,1,0:T(8,128)S(1)}, f32[1,384,768]{2,1,0:T(8,128)}, u32[]{:S(2)}) copy-start(f32[1,384,768]{2,1,0:T(8,128)} %refs_14_.1) | copy-start | bytes 3538948
  79.4 24.9 %copy-start.7 = (f32[24,1536]{1,0:T(8,128)S(1)}, f32[24,1536]{1,0:T(8,128)}, u32[]{:S(2)}) copy-start(f32[24,1536]{1,0:T(8,128)} %refs_0_.1) | copy-start | bytes 442372
  79.4 24.9 %copy-start.10 = (f32[24,16]{0,1:T(8,128)S(1)}, f32[24,16]{0,1:T(8,128)}, u32[]{:S(2)}) copy-start(f32[24,16]{0,1:T(8,128)} %param.23) | copy-start | bytes 4612
  79.5 24.9 %copy-start.11 = (f32[4,24]{1,0:T(4,128)S(1)}, f32[4,24]{1,0:T(4,128)}, u32[]{:S(2)}) copy-start(f32[4,24]{1,0:T(4,128)} %refs_8_.1) | copy-start | bytes 1156
  79.5 24.9 %copy-start.12 = (f32[24,16]{0,1:T(8,128)S(1)}, f32[24,16]{0,1:T(8,128)}, u32[]{:S(2)}) copy-start(f32[24,16]{0,1:T(8,128)} %param.24) | copy-start | bytes 4612
  79.5 24.9 %copy-start.13 = (f32[24,16]{0,1:T(8,128)S(1)}, f32[24,16]{0,1:T(8,128)}, u32[]{:S(2)}) copy-start(f32[24,16]{0,1:T(8,128)} %param.25) | copy-start | bytes 4612
  79.5 24.9 %copy-start.14 = (f32[4,24]{1,0:T(4,128)S(1)}, f32[4,24]{1,0:T(4,128)}, u32[]{:S(2)}) copy-start(f32[4,24]{1,0:T(4,128)} %refs_9_.1) | copy-start | bytes 1156
  79.5 24.9 %copy-start.15 = (f32[4,24]{1,0:T(4,128)S(1)}, f32[4,24]{1,0:T(4,128)}, u32[]{:S(2)}) copy-start(f32[4,24]{1,0:T(4,128)} %refs_10_.1) | copy-start | bytes 1156

commit v4 on v3

--- a/solution.py
+++ b/solution.py
@@ -20,6 +20,7 @@
 PAIRS = 3
 GROUPS = 16
 GROUP_ROWS = D // GROUPS
+CHUNK = 112
 LONG_WINDOW = 592
 LONG_SPAN = 640
 WINDOW_PAD = 48
@@ -39,7 +40,7 @@
 
 
 def vmem_bytes(experts, mebibytes):
-    return (mebibytes if experts <= 16 else 58) * 1024 * 1024
+    return (mebibytes if experts <= 16 else 60) * 1024 * 1024
 
 
 def whole(count):
@@ -76,7 +77,7 @@
 
 
 def gather_kernel(experts, attn_hbm, phi_hbm, norm_hbm, out, stage, attn_ref, phi_ref, norm_ref, load_sem,
-                  send_z, send_first, send_second, send_pair, recv, recv_pair):
+                  sent, recv):
     core, chip, first, second = ring(experts)
     rows = attn_ref.shape[0]
     half = pl.multiple_of(core * (2 * D), 128)
@@ -120,74 +121,57 @@
     out[chip, core] = stage[...].astype(BF16)
     pl.semaphore_wait(barrier, layers + 2)
 
-    def copy(block, side, sems, sem, arrivals, device):
+    def copy(source, target, send_sem, recv_sem, device):
         return pltpu.make_async_remote_copy(
-            src_ref=out.at[block, side],
-            dst_ref=out.at[block, side],
-            send_sem=sems.at[sem],
-            recv_sem=arrivals.at[block],
+            src_ref=source,
+            dst_ref=target,
+            send_sem=send_sem,
+            recv_sem=recv_sem,
             device_id=device,
             device_id_type=MESH,
         )
 
-    def along_z(d):
-        peer = lax.rem(layer + d, layers) * 4 + column
-        return copy(chip, core, send_z, d, recv, (core, peer))
-
-    def to_first(block):
-        return copy(block, core, send_first, block, recv, (core, first))
-
-    def to_second(block):
-        return copy(block, core, send_second, block, recv, (core, second))
+    def along(block, peer):
+        mine = out.at[block, core]
+        return copy(mine, mine, sent.at[0], recv.at[block], (core, peer))
 
     def to_pair(block):
-        return copy(block, core, send_pair, block, recv_pair, (1 - core, chip))
+        mine = out.at[block, core]
+        return copy(mine, mine, sent.at[1], sent.at[2], (1 - core, chip))
 
     @pl.loop(1, layers)
     def _(d):
-        along_z(d).start()
-
-    to_first(chip).start()
-    to_second(chip).start()
+        along(chip, lax.rem(layer + d, layers) * 4 + column).start()
+
+    along(chip, first).start()
+    along(chip, second).start()
     to_pair(chip).start()
 
     @pl.loop(1, layers)
     def _(d):
         block = lax.rem(layer - d + layers, layers) * 4 + column
-        to_first(block).wait_recv()
-        to_first(block).start()
-        to_second(block).start()
+        along(block, first).wait_recv()
+        along(block, first).start()
+        along(block, second).start()
         to_pair(block).start()
 
     @pl.loop(0, layers)
     def _(d):
         block = lax.rem(layer - d + layers, layers) * 4 + lax.rem(first, 4)
-        to_first(block).wait_recv()
-        to_second(block).start()
+        along(block, first).wait_recv()
+        along(block, second).start()
         to_pair(block).start()
 
     @pl.loop(0, 2 * layers)
     def _(d):
         other = jnp.where(lax.rem(d, 2) == 0, lax.rem(second, 4), lax.rem(3 - column, 4))
         block = lax.rem(layer - d // 2 + layers, layers) * 4 + other
-        to_first(block).wait_recv()
+        along(block, first).wait_recv()
         to_pair(block).start()
 
-    @pl.loop(1, layers)
-    def _(d):
-        along_z(d).wait_send()
-
-    @pl.loop(0, layers)
-    def _(d):
-        block = d * 4 + column
-        to_first(block).wait_send()
-        to_second(block).wait_send()
-        to_second(d * 4 + lax.rem(first, 4)).wait_send()
-
-    @pl.loop(0, experts)
-    def _(block):
-        to_pair(block).wait_send()
-        copy(block, 1 - core, send_pair, block, recv_pair, (1 - core, chip)).wait_recv()
+    sides = out.at[pl.ds(0, experts - 1), core]
+    copy(sides, sides, sent.at[0], sent.at[0], (1 - core, chip)).wait_send()
+    copy(out.at[:, core], out.at[:, 1 - core], sent.at[1], sent.at[2], (1 - core, chip)).wait()
 
 
 def gather_weights(attn_weight, phi_turned, norm_params, experts):
@@ -204,9 +188,9 @@
             pltpu.VMEM(phi_turned.shape, F32),
             pltpu.VMEM(norm_params.shape, F32),
             dma((3,)),
-            dma((experts // 4,)),
-        ]
-        + [dma((experts,))] * 5,
+            dma((3,)),
+            dma((experts,)),
+        ],
         compiler_params=pltpu.CompilerParams(
             collective_id=0, has_side_effects=True, vmem_limit_bytes=vmem_bytes(experts, 3)
         ),
@@ -285,6 +269,16 @@
     )
 
 
+def over_rows(start, stop, carry, body):
+    for at in range(start, stop, CHUNK):
+        carry = body(at, min(CHUNK, stop - at), carry)
+    return carry
+
+
+def fold_rows(values):
+    return jnp.sum(values.reshape(values.shape[0] // 8, 8, values.shape[1]), axis=0)
+
+
 def over_images(len_ref, tokens, body):
     def step(k, start):
         length = len_ref[0, k]
@@ -313,7 +307,7 @@
 
 def forward_kernel(experts, len_ref, patch_ref, main_ref, cot_hbm, qkv_ref, o_ref, lse_ref, x1_ref,
                    h2_ref, disp_ref, comb_ref, gy_ref, pack_ref, logit, packf, scores,
-                   probs, peaks, cot_ref, load_sem):
+                   probs, peaks, cot_ref, h1_all, load_sem):
     load = pltpu.make_async_copy(cot_hbm, cot_ref, load_sem.at[0])
     load.start()
     tokens = patch_ref.shape[0]
@@ -324,11 +318,17 @@
     w_q, w_k = unpack_weight(main_ref, 0, 0), unpack_weight(main_ref, 0, 1)
     w_v = unpack_weight(main_ref, 1, 0)
     w_qkv = jnp.concatenate([w_q, w_k, w_v], axis=1)
+
+    def first_norm(at, count, carry):
+        rows = pl.ds(at, count)
+        normal, _ = normed(patch_ref[rows, :].astype(F32))
+        h1_all[rows, :] = (normal * norms[0:1] + norms[1:2]).astype(BF16)
+        return carry
+
+    over_rows(0, tokens, 0, first_norm)
     for t in range(5):
         rows = pl.ds(t * tile, tile)
-        normal, _ = normed(patch_ref[rows, :].astype(F32))
-        h1 = (normal * norms[0:1] + norms[1:2]).astype(BF16)
-        qkv = mm(h1, w_qkv).astype(BF16)
+        qkv = mm(h1_all[rows, :], w_qkv).astype(BF16)
         for c in range(9):
             qkv_ref[c, rows, :] = qkv[:, c * 128 : (c + 1) * 128]
     qkv_ref[:, tokens:, :] = jnp.zeros((9, WINDOW_PAD, 128), BF16)
@@ -344,34 +344,37 @@
         rows = pl.ds(first, window)
         wide = pl.ds(first, span)
 
-        @pl.loop(0, PAIRS)
-        def _(p):
-            query = qkv_ref[p, rows, :].astype(F32) * SCORE_SCALE
+        ones = jnp.ones((span, 128), BF16)
+
+        def score(n):
+            p, h = divmod(n, 2)
+            mine = low_lane if h == 0 else jnp.logical_not(low_lane)
+            query = jnp.where(mine, qkv_ref[p, rows, :].astype(F32) * SCORE_SCALE, 0.0)
             keys = qkv_ref[PAIRS + p, wide, :]
-            ones = jnp.ones((span, 128), BF16)
+            scores[h, :window, :span] = mm_nt(query.astype(BF16), keys)
+
+        score(0)
+        outs = []
+        for n in range(HEADS):
+            p, h = divmod(n, 2)
+            if n + 1 < HEADS:
+                score(n + 1)
+            for r in range(0, window, 16):
+                part = scores[h, r : r + 16, :span] + bias
+                peak = jnp.max(part, axis=-1, keepdims=True)
+                probs[h, r : r + 16, :span] = jnp.exp(part - peak).astype(BF16)
+                peaks[h, r : r + 16, :] = jnp.broadcast_to(peak, (16, 128))
             values = jnp.concatenate([qkv_ref[2 * PAIRS + p, wide, :], ones], axis=1)
-            for h in range(2):
-                mine = low_lane if h == 0 else jnp.logical_not(low_lane)
-                scores[h, :window, :span] = mm_nt(jnp.where(mine, query, 0.0).astype(BF16), keys)
-            for h in range(2):
-                for r in range(0, window, 16):
-                    part = scores[h, r : r + 16, :span] + bias
-                    peak = jnp.max(part, axis=-1, keepdims=True)
-                    probs[h, r : r + 16, :span] = jnp.exp(part - peak).astype(BF16)
-                    peaks[h, r : r + 16, :] = jnp.broadcast_to(peak, (16, 128))
-            outs = []
-            sums = lse_ref[rows, :]
-            for h in range(2):
-                both = mm(probs[h, :window, :span], values)
-                summed = both[:, 128:]
-                outs.append(both[:, :128] * (1.0 / summed))
-                logs = peaks[h, :window, :] + jnp.log(summed)
-                sums = jnp.where(inside & (lane == 2 * p + h), logs, sums)
-            lse_ref[rows, :] = sums
-            lanes = pl.ds(pl.multiple_of(p * 128, 128), 128)
-            old = o_ref[rows, lanes].astype(F32)
-            merged = jnp.where(inside, jnp.where(low_lane, outs[0], outs[1]), old)
-            o_ref[rows, lanes] = merged.astype(BF16)
+            both = mm(probs[h, :window, :span], values)
+            summed = both[:, 128:]
+            outs.append(both[:, :128] * (1.0 / summed))
+            logs = peaks[h, :window, :] + jnp.log(summed)
+            lse_ref[rows, :] = jnp.where(inside & (lane == n), logs, lse_ref[rows, :])
+            if h == 1:
+                lanes = slice(p * 128, (p + 1) * 128)
+                old = o_ref[rows, lanes].astype(F32)
+                merged = jnp.where(inside, jnp.where(low_lane, outs[n - 1], outs[n]), old)
+                o_ref[rows, lanes] = merged.astype(BF16)
 
     over_images(len_ref, tokens, attend)
 
@@ -379,33 +382,53 @@
     w_o = unpack_weight(main_ref, 1, 1)
     for t in range(5):
         rows = pl.ds(t * tile, tile)
-        x1 = patch_ref[rows, :].astype(F32) + mm(o_ref[rows, :], w_o)
+        x1_ref[rows, :] = mm(o_ref[rows, :], w_o)
+
+    def second_norm(at, count, carry):
+        rows = pl.ds(at, count)
+        x1 = patch_ref[rows, :].astype(F32) + x1_ref[rows, :]
         normal, _ = normed(x1)
-        h2 = (normal * norms[2:3] + norms[3:4]).astype(BF16)
-        h2_ref[rows, :] = h2
-        logit[rows, :] = mm_nt(h2, phi)
-        position = t * tile + lax.broadcasted_iota(jnp.int32, (tile, 1), 0)
-        valid = position < total
+        h2_ref[rows, :] = (normal * norms[2:3] + norms[3:4]).astype(BF16)
+        valid = at + lax.broadcasted_iota(jnp.int32, (count, 1), 0) < total
         x1_ref[rows, :] = jnp.where(valid, x1, 0.0)
         gy_ref[rows, :] = jnp.where(valid, cot_ref[rows, :].astype(F32), 0.0).astype(BF16)
-
-    position = lax.broadcasted_iota(jnp.int32, (tokens, columns), 0)
-    member = (position >= starts) & (position < ends)
+        return carry
+
+    over_rows(0, tokens, 0, second_norm)
+    logit[...] = mm_nt(h2_ref[...], phi)
+
+    def members(at, count):
+        position = at + lax.broadcasted_iota(jnp.int32, (count, columns), 0)
+        return (position >= starts) & (position < ends)
+
+    def mixing(at, count, peak):
+        rows = pl.ds(at, count)
+        logits = logit[rows, :]
+        member = members(at, count)
+        exponent = jnp.exp(logits - jnp.max(logits, axis=-1, keepdims=True))
+        summed = jnp.sum(exponent, axis=-1, keepdims=True) * (1.0 / SLOT_ROWS)
+        comb_ref[rows, :] = jnp.where(member, exponent * (1.0 / summed), 0.0)
+        inside = jnp.where(member, logits, MASKED)
+        return jnp.maximum(peak, jnp.max(inside.reshape(count // 8, 8, columns), axis=0))
+
+    peak = over_rows(0, tokens, jnp.full((8, columns), MASKED, F32), mixing)
     present = ends > starts
-    logits = logit[...]
-    peak = jnp.max(jnp.where(member, logits, MASKED), axis=0, keepdims=True)
-    peak = jnp.where(present, peak, 0.0)
-    exponent = jnp.where(member, jnp.exp(jnp.where(member, logits - peak, 0.0)), 0.0)
-    summed = jnp.sum(exponent, axis=0, keepdims=True) + jnp.where(present, 0.0, 1.0)
-    dispatch = exponent / summed
+    peak = jnp.where(present, jnp.max(peak, axis=0, keepdims=True), 0.0)
+
+    def exponents(at, count, summed):
+        rows = pl.ds(at, count)
+        member = members(at, count)
+        exponent = jnp.exp(jnp.where(member, logit[rows, :] - peak, 0.0))
+        exponent = jnp.where(member, exponent, 0.0)
+        disp_ref[rows, :] = exponent
+        return summed + fold_rows(exponent)
+
+    summed = over_rows(0, tokens, jnp.zeros((8, columns), F32), exponents)
+    summed = jnp.sum(summed, axis=0, keepdims=True) + jnp.where(present, 0.0, 1.0)
+    dispatch = disp_ref[...] * (1.0 / summed)
     disp_ref[...] = dispatch
     slots = mm_tn(dispatch.astype(BF16), h2_ref[...])
-    row_peak = jnp.max(logits, axis=-1, keepdims=True)
-    exponent = jnp.exp(logits - row_peak)
-    summed = jnp.sum(exponent, axis=-1, keepdims=True) * (1.0 / SLOT_ROWS)
-    combine = jnp.where(member, exponent / summed, 0.0)
-    comb_ref[...] = combine
-    grad_result = mm_tn(combine.astype(BF16), gy_ref[...])
+    grad_result = mm_tn(comb_ref[...].astype(BF16), gy_ref[...])
     for part, matrix in enumerate((slots, grad_result)):
         pack_rows(packf, matrix.reshape(experts, SLOT_ROWS, D))
         pack_ref[:, part * 16 : (part + 1) * 16, :] = packf[...].astype(BF16)
@@ -451,16 +474,17 @@
             pltpu.VMEM((2, LONG_WINDOW, LONG_SPAN), BF16),
             pltpu.VMEM((2, LONG_WINDOW, 128), F32),
             pltpu.VMEM((tokens, D), BF16),
+            pltpu.VMEM((tokens, D), BF16),
             pltpu.SemaphoreType.DMA((1,)),
         ],
-        compiler_params=pltpu.CompilerParams(vmem_limit_bytes=vmem_bytes(experts, 22)),
+        compiler_params=pltpu.CompilerParams(vmem_limit_bytes=vmem_bytes(experts, 24)),
         name="forward_local",
     )(lengths, patches, main, cotangent)
 
 
 def expert_kernel(experts, pack_ref, in_ref, out_ref, result_ref, gslot_ref, gin_ref, gout_ref,
                   square_ref, inbox, partial, given, outbox, back, packf, wide, packe, widee,
-                  send_one, recv_one, pair_send, pair_recv, send_two, recv_two, sum_sem):
+                  sems):
     core = lax.axis_index("batch")
     chip = lax.axis_index("expert")
     barrier = pltpu.get_barrier_semaphore()
@@ -476,51 +500,27 @@
     inbox[core, chip] = pack_ref[chip]
     pl.semaphore_wait(barrier, experts)
 
-    def first(j, block, peer):
+    def copy(source, target, sem, device):
         return pltpu.make_async_remote_copy(
-            src_ref=pack_ref.at[peer],
-            dst_ref=inbox.at[core, block],
-            send_sem=send_one.at[j],
-            recv_sem=recv_one.at[j],
-            device_id=(core, peer),
+            src_ref=source,
+            dst_ref=target,
+            send_sem=sems.at[sem],
+            recv_sem=sems.at[sem + 1],
+            device_id=device,
             device_id_type=MESH,
         )
 
-    def to_pair(side, block):
-        return pltpu.make_async_remote_copy(
-            src_ref=inbox.at[side, block],
-            dst_ref=inbox.at[side, block],
-            send_sem=pair_send.at[block],
-            recv_sem=pair_recv.at[block],
-            device_id=(1 - core, chip),
-            device_id_type=MESH,
-        )
-
-    def second(j, block, peer):
-        return pltpu.make_async_remote_copy(
-            src_ref=outbox.at[peer],
-            dst_ref=back.at[block],
-            send_sem=send_two.at[j],
-            recv_sem=recv_two.at[j],
-            device_id=(core, peer),
-            device_id_type=MESH,
-        )
-
     @pl.loop(1, experts)
     def _(j):
-        first(j, chip, lax.rem(chip + j, experts)).start()
-
-    to_pair(core, chip).start()
-
-    @pl.loop(1, experts)
-    def _(j):
-        source = lax.rem(chip - j + experts, experts)
-        first(j, source, source).wait_recv()
-        to_pair(core, source).start()
-
-    @pl.loop(0, experts)
-    def _(block):
-        to_pair(1 - core, block).wait_recv()
+        peer = lax.rem(chip + j, experts)
+        copy(pack_ref.at[peer], inbox.at[core, chip], 0, (core, peer)).start()
+
+    others = pl.ds(0, experts - 1)
+    first = copy(pack_ref.at[others], inbox.at[core, others], 0, (core, chip))
+    first.wait_recv()
+    pair = copy(inbox.at[core], inbox.at[core], 2, (1 - core, chip))
+    pair.start()
+    pair.wait_recv()
 
     def spread(side, part):
         packe[...] = inbox[side, :, part * 16 : (part + 1) * 16, :].astype(F32)
@@ -547,14 +547,7 @@
     for part in range(2):
         pack_rows(packf, theirs[4 + part].reshape(experts, SLOT_ROWS, D))
         partial[:, part * 16 : (part + 1) * 16, :] = packf[...].astype(BF16)
-    halves = pltpu.make_async_remote_copy(
-        src_ref=partial,
-        dst_ref=given,
-        send_sem=sum_sem.at[0],
-        recv_sem=sum_sem.at[1],
-        device_id=(1 - core, chip),
-        device_id_type=MESH,
-    )
+    halves = copy(partial, given, 4, (1 - core, chip))
     halves.start()
     ours = run(core)
     halves.wait_recv()
@@ -565,42 +558,36 @@
 
     @pl.loop(1, experts)
     def _(j):
-        second(j, chip, lax.rem(chip + j, experts)).start()
+        peer = lax.rem(chip + j, experts)
+        copy(outbox.at[peer], back.at[chip], 6, (core, peer)).start()
 
     back[chip] = outbox[chip]
     grad_out = mm_tn(ours[2], ours[1]) + mm_tn(theirs[2], theirs[1])
     gout_ref[0] = grad_out
     grad_in = mm_tn(ours[0], ours[3]) + mm_tn(theirs[0], theirs[3])
     gin_ref[0] = grad_in
-    squares = jnp.sum(grad_out * grad_out) + jnp.sum(grad_in * grad_in)
-    square_ref[...] = jnp.full(square_ref.shape, squares, F32)
-
-    @pl.loop(1, experts)
-    def _(j):
-        source = lax.rem(chip - j + experts, experts)
-        second(j, source, source).wait_recv()
-
+    squares = jnp.zeros((1, 128), F32)
+    for grad in (grad_out, grad_in):
+        columns = jnp.sum(grad * grad, axis=0, keepdims=True)
+        for c in range(0, grad.shape[1], 128):
+            squares = squares + columns[:, c : c + 128]
+    square_ref[...] = squares
+
+    second = copy(outbox.at[others], back.at[others], 6, (core, chip))
+    second.wait_recv()
     for part, target in enumerate((result_ref, gslot_ref)):
         packe[...] = back[:, part * 16 : (part + 1) * 16, :].astype(F32)
         unpack_rows(packe, widee)
         target[...] = widee[...].reshape(experts * SLOT_ROWS, D).astype(BF16)
 
+    first.wait_send()
+    pair.wait_send()
     halves.wait_send()
-
-    @pl.loop(1, experts)
-    def _(j):
-        peer = lax.rem(chip + j, experts)
-        first(j, chip, peer).wait_send()
-        second(j, chip, peer).wait_send()
-
-    @pl.loop(0, experts)
-    def _(block):
-        to_pair(core, block).wait_send()
+    second.wait_send()
 
 
 def run_experts(packed, expert_in, expert_out, experts):
     shape = jax.ShapeDtypeStruct
-    dma = pltpu.SemaphoreType.DMA
     return pl.pallas_call(
         functools.partial(expert_kernel, experts),
         out_shape=(
@@ -623,8 +610,7 @@
             pltpu.VMEM((experts, 16, 128), F32),
             pltpu.VMEM((experts, SLOT_ROWS, D), F32),
         ]
-        + [dma((experts,))] * 6
-        + [dma((2,))],
+        + [pltpu.SemaphoreType.DMA((8,))],
         compiler_params=pltpu.CompilerParams(
             collective_id=1, has_side_effects=True, vmem_limit_bytes=vmem_bytes(experts, 8)
         ),
@@ -635,7 +621,8 @@
 def backward_kernel(experts, len_ref, patch_ref, main_ref, qkv_ref, o_ref, lse_ref,
                     x1_ref, h2_ref, disp_ref, comb_ref, gy_ref, result_ref, gslot_ref, block_ref,
                     input_ref, gw_ref, gdisp, glog, gx1, branch, go, gqkv,
-                    h1_all, scores, grad_probs, probs, grad_scores, sums):
+                    h1_all, scores, grad_probs, probs, grad_scores, sums, gcomb,
+                    wide_rows):
     tokens = patch_ref.shape[0]
     columns = experts * SLOT_ROWS
     tile = tokens // 5
@@ -643,38 +630,63 @@
     result = result_ref[...]
     gslots = gslot_ref[...]
 
-    inner = jnp.zeros((1, columns), F32)
+    kept = gdisp.shape[0] == tokens
+
+    def place(at):
+        return at if kept else at % tile
+
+    inner = jnp.zeros((8, columns), F32)
     for t in range(5):
         rows = pl.ds(t * tile, tile)
-        grad_dispatch = mm_nt(h2_ref[rows, :], gslots)
-        gdisp[rows, :] = grad_dispatch
-        inner = inner + jnp.sum(disp_ref[rows, :] * grad_dispatch, axis=0, keepdims=True)
-
-    w_o = unpack_weight(main_ref, 1, 1)
-    gain_two = jnp.zeros((1, D), F32)
-    bias_two = jnp.zeros((1, D), F32)
+        gdisp[pl.ds(place(t * tile), tile), :] = mm_nt(h2_ref[rows, :], gslots)
+
+        def dispatch_inner(at, count, inner):
+            products = disp_ref[pl.ds(at, count), :] * gdisp[pl.ds(place(at), count), :]
+            return inner + fold_rows(products)
+
+        inner = over_rows(t * tile, (t + 1) * tile, inner, dispatch_inner)
+    inner = jnp.sum(inner, axis=0, keepdims=True)
     for t in range(5):
         rows = pl.ds(t * tile, tile)
-        dispatch, combine, gy = disp_ref[rows, :], comb_ref[rows, :], gy_ref[rows, :]
-        x1 = x1_ref[rows, :]
-        mixed = mm(combine.astype(BF16), result)
-        block_ref[rows, :] = (x1 + mixed).astype(BF16)
-        weighted = combine * mm_nt(gy, result)
-        grad_logits = (
-            weighted
-            - combine * jnp.sum(weighted, axis=-1, keepdims=True)
-            + dispatch * (gdisp[rows, :] - inner)
-        ).astype(BF16)
-        glog[rows, :] = grad_logits
-        grad_h2 = mm(dispatch.astype(BF16), gslots) + mm(grad_logits, phi)
-        normal, inverse = normed(x1)
-        gain_two = gain_two + jnp.sum(grad_h2 * normal, axis=0, keepdims=True)
-        bias_two = bias_two + jnp.sum(grad_h2, axis=0, keepdims=True)
-        grad_x1 = gy.astype(F32) + norm_back(grad_h2, normal, inverse, norms[2:3])
+        here = pl.ds(place(t * tile), tile)
+        gx1[rows, :] = mm(comb_ref[rows, :].astype(BF16), result)
+        gcomb[here, :] = mm_nt(gy_ref[rows, :], result)
+        if not kept:
+            gdisp[here, :] = mm_nt(h2_ref[rows, :], gslots)
+
+        def logit_grads(at, count, carry):
+            rows, here = pl.ds(at, count), pl.ds(place(at), count)
+            block_ref[rows, :] = (x1_ref[rows, :] + gx1[rows, :]).astype(BF16)
+            combine = comb_ref[rows, :]
+            weighted = combine * gcomb[here, :]
+            glog[rows, :] = (
+                weighted
+                - combine * jnp.sum(weighted, axis=-1, keepdims=True)
+                + disp_ref[rows, :] * (gdisp[here, :] - inner)
+            ).astype(BF16)
+            return carry
+
+        over_rows(t * tile, (t + 1) * tile, 0, logit_grads)
+    for t in range(5):
+        rows = pl.ds(t * tile, tile)
+        gx1[rows, :] = mm(disp_ref[rows, :].astype(BF16), gslots) + mm(glog[rows, :], phi)
+
+    def second_norm(at, count, carry):
+        gain, bias = carry
+        rows = pl.ds(at, count)
+        grad_h2 = gx1[rows, :]
+        normal, inverse = normed(x1_ref[rows, :])
+        grad_x1 = gy_ref[rows, :].astype(F32) + norm_back(grad_h2, normal, inverse, norms[2:3])
         gx1[rows, :] = grad_x1
-        grad_branch = grad_x1.astype(BF16)
-        branch[rows, :] = grad_branch
-        grad_o = mm_nt(grad_branch, w_o).astype(BF16)
+        branch[rows, :] = grad_x1.astype(BF16)
+        return gain + fold_rows(grad_h2 * normal), bias + fold_rows(grad_h2)
+
+    zero = jnp.zeros((8, D), F32)
+    gain_two, bias_two = over_rows(0, tokens, (zero, zero), second_norm)
+    w_o = unpack_weight(main_ref, 1, 1)
+    for t in range(5):
+        rows = pl.ds(t * tile, tile)
+        grad_o = mm_nt(branch[rows, :], w_o).astype(BF16)
         for c in range(PAIRS):
             go[c, rows, :] = grad_o[:, c * 128 : (c + 1) * 128]
 
@@ -710,77 +722,88 @@
         wide = pl.ds(first, span)
         sums[:, :span] = jnp.transpose(lse_ref[wide, :])
 
-        @pl.loop(0, PAIRS)
-        def _(p):
-            lanes = pl.ds(pl.multiple_of(p * 128, 128), 128)
-            query = qkv_ref[p, wide, :]
-            keys_low = qkv_ref[PAIRS + p, rows, :]
-            keys = keys_low.astype(F32) * SCORE_SCALE
-            values = qkv_ref[2 * PAIRS + p, rows, :].astype(F32)
-            grads = go[p, wide, :]
-            product = grads.astype(F32) * o_ref[wide, lanes].astype(F32)
-            upper = product.astype(BF16)
-            lower = (product - upper.astype(F32)).astype(BF16)
-            inner_rows = mm_nt(heads, upper) + mm_nt(heads, lower)
-            for h in range(2):
-                mine = low_lane if h == 0 else jnp.logical_not(low_lane)
-                scores[h, :window, :span] = mm_nt(jnp.where(mine, keys, 0.0).astype(BF16), query)
-                grad_probs[h, :window, :span] = mm_nt(
-                    jnp.where(mine, values, 0.0).astype(BF16), grads
+        def score(n):
+            p, h = divmod(n, 2)
+            mine = low_lane if h == 0 else jnp.logical_not(low_lane)
+            keys = jnp.where(mine, qkv_ref[PAIRS + p, rows, :].astype(F32) * SCORE_SCALE, 0.0)
+            values = jnp.where(mine, qkv_ref[2 * PAIRS + p, rows, :].astype(F32), 0.0)
+            scores[h, :window, :span] = mm_nt(keys.astype(BF16), qkv_ref[p, wide, :])
+            grad_probs[h, :window, :span] = mm_nt(values.astype(BF16), go[p, wide, :])
+
+        def split(values):
+            low = values.astype(F32)
+            halves = (jnp.where(low_lane, low, 0.0), jnp.where(low_lane, 0.0, low))
+            return jnp.concatenate(halves, axis=0).astype(BF16)
+
+        score(0)
+        for n in range(HEADS):
+            p, h = divmod(n, 2)
+            if n + 1 < HEADS:
+                score(n + 1)
+            if h == 0:
+                lanes = slice(p * 128, (p + 1) * 128)
+                product = go[p, wide, :].astype(F32) * o_ref[wide, lanes].astype(F32)
+                upper = product.astype(BF16)
+                lower = (product - upper.astype(F32)).astype(BF16)
+                inner_rows = mm_nt(heads, upper) + mm_nt(heads, lower)
+            logs = jnp.where(queries_inside, sums[n : n + 1, :span], 1e30)
+            inner_row = inner_rows[h : h + 1]
+            for r in range(0, window, 16):
+                part = jnp.exp(scores[h, r : r + 16, :span] - logs)
+                if r == 0 or r + 16 > full:
+                    part = jnp.where(rows_inside(shift, full, r, 16), part, 0.0)
+                probs[h, r : r + 16, :span] = part.astype(BF16)
+                slope = part * (grad_probs[h, r : r + 16, :span] - inner_row)
+                grad_scores[h, r : r + 16, :span] = slope.astype(BF16)
+            if h == 1:
+                slopes = [grad_scores[g, :window, :span] for g in range(2)]
+                weights = [probs[g, :window, :span] for g in range(2)]
+                keys = split(qkv_ref[PAIRS + p, rows, :])
+                news = (
+                    jnp.transpose(mm_tn(keys, jnp.concatenate(slopes, axis=0)))[:window] * SCORE_SCALE,
+                    mm(jnp.concatenate(slopes, axis=1), split(qkv_ref[p, wide, :])) * SCORE_SCALE,
+                    mm(jnp.concatenate(weights, axis=1), split(go[p, wide, :])),
                 )
-            for h in range(2):
-                logs = jnp.where(queries_inside, sums[pl.ds(2 * p + h, 1), :span], 1e30)
-                inner_row = inner_rows[h : h + 1]
-                for r in range(0, window, 16):
-                    part = jnp.exp(scores[h, r : r + 16, :span] - logs)
-                    if r == 0 or r + 16 > full:
-                        part = jnp.where(rows_inside(shift, full, r, 16), part, 0.0)
-                    probs[h, r : r + 16, :span] = part.astype(BF16)
-                    slope = part * (grad_probs[h, r : r + 16, :span] - inner_row)
-                    grad_scores[h, r : r + 16, :span] = slope.astype(BF16)
-            parts = []
-            for h in range(2):
-                slopes = grad_scores[h, :window, :span]
-                parts.append(
-                    (
-                        mm_tn(slopes, keys_low)[:window] * SCORE_SCALE,
-                        mm(slopes, query) * SCORE_SCALE,
-                        mm(probs[h, :window, :span], grads),
-                    )
-                )
-            for c in range(3):
-                old = gqkv[c * PAIRS + p, rows, :].astype(F32)
-                new = jnp.where(low_lane, parts[0][c], parts[1][c])
-                gqkv[c * PAIRS + p, rows, :] = jnp.where(inside, new, old).astype(BF16)
+                for c in range(3):
+                    old = gqkv[c * PAIRS + p, rows, :].astype(F32)
+                    gqkv[c * PAIRS + p, rows, :] = jnp.where(inside, news[c], old).astype(BF16)
 
     over_images(len_ref, tokens, attend)
 
     w_q, w_k = unpack_weight(main_ref, 0, 0), unpack_weight(main_ref, 0, 1)
     w_v = unpack_weight(main_ref, 1, 0)
     w_qkv = jnp.concatenate([w_q, w_k, w_v], axis=1)
-    gain_one = jnp.zeros((1, D), F32)
-    bias_one = jnp.zeros((1, D), F32)
+    sums_one = (zero, zero)
     for t in range(5):
         rows = pl.ds(t * tile, tile)
         grad_qkv = jnp.concatenate([gqkv[c, rows, :] for c in range(9)], axis=1)
-        grad_h1 = mm_nt(grad_qkv, w_qkv)
-        normal, inverse = normed(patch_ref[rows, :].astype(F32))
-        h1_all[rows, :] = (normal * norms[0:1] + norms[1:2]).astype(BF16)
-        gain_one = gain_one + jnp.sum(grad_h1 * normal, axis=0, keepdims=True)
-        bias_one = bias_one + jnp.sum(grad_h1, axis=0, keepdims=True)
-        grad_x = gx1[rows, :] + norm_back(grad_h1, normal, inverse, norms[0:1])
-        input_ref[rows, :] = grad_x.astype(BF16)
+        wide_rows[pl.ds(place(t * tile), tile), :] = mm_nt(grad_qkv, w_qkv)
+
+        def first_norm(at, count, carry):
+            gain, bias = carry
+            rows = pl.ds(at, count)
+            grad_h1 = wide_rows[pl.ds(place(at), count), :]
+            normal, inverse = normed(patch_ref[rows, :].astype(F32))
+            h1_all[rows, :] = (normal * norms[0:1] + norms[1:2]).astype(BF16)
+            grad_x = gx1[rows, :] + norm_back(grad_h1, normal, inverse, norms[0:1])
+            input_ref[rows, :] = grad_x.astype(BF16)
+            return gain + fold_rows(grad_h1 * normal), bias + fold_rows(grad_h1)
+
+        sums_one = over_rows(t * tile, (t + 1) * tile, sums_one, first_norm)
+    gain_one, bias_one = sums_one
+    grad = mm_tn(h1_all[...], jnp.concatenate([gqkv[c] for c in range(9)], axis=1))
     for c, (side, part) in enumerate(((0, 0), (0, 1), (1, 0))):
-        grad = jnp.concatenate([gqkv[c * PAIRS + p] for p in range(PAIRS)], axis=1)
-        put(side, part, mm_tn(h1_all[...], grad))
+        put(side, part, grad[:, c * D : (c + 1) * D])
     zeros = jnp.zeros((small_rows - 4, D), F32)
-    turned = jnp.concatenate([gain_one, bias_one, gain_two, bias_two, zeros], axis=0)
+    turned = [jnp.sum(one, axis=0, keepdims=True) for one in (gain_one, bias_one, gain_two, bias_two)]
+    turned = jnp.concatenate(turned + [zeros], axis=0)
     gw_ref[1, :, 6 * GROUP_ROWS :, :] = pack_turned(turned)
 
 
 def backward_local(lengths, patches, main, saved, result, gslots, experts):
     tokens = patches.shape[0]
     columns = experts * SLOT_ROWS
+    kept = tokens if experts <= 16 else tokens // 5
     shape = jax.ShapeDtypeStruct
     return pl.pallas_call(
         functools.partial(backward_kernel, experts),
@@ -792,7 +815,7 @@
         in_specs=[pl.BlockSpec(memory_space=pltpu.SMEM)] + whole(12),
         out_specs=tuple(whole(3)),
         scratch_shapes=[
-            pltpu.VMEM((tokens, columns), F32),
+            pltpu.VMEM((kept, columns), F32),
             pltpu.VMEM((tokens, columns), BF16),
             pltpu.VMEM((tokens, D), F32),
             pltpu.VMEM((tokens, D), BF16),
@@ -804,16 +827,17 @@
             pltpu.VMEM((2, LONG_WINDOW, LONG_SPAN), BF16),
             pltpu.VMEM((2, LONG_WINDOW, LONG_SPAN), BF16),
             pltpu.VMEM((128, LONG_SPAN), F32),
+            pltpu.VMEM((kept, columns), F32),
+            pltpu.VMEM((kept, D), F32),
         ],
-        compiler_params=pltpu.CompilerParams(vmem_limit_bytes=vmem_bytes(experts, 28)),
+        compiler_params=pltpu.CompilerParams(vmem_limit_bytes=vmem_bytes(experts, 34)),
         name="backward_local",
     )(lengths, patches, main, *saved, result, gslots)
 
 
 def reduce_kernel(experts, gw_ref, square_ref, attn_out, phi_out, norm_out, total_ref, own, pair_in,
-                  box_one, in_one, box_two, in_two, box_z, in_z, final, scalars, load_sem, pair_send,
-                  pair_recv, send_one, recv_one, send_two, recv_two, send_z, recv_z, swap_sem,
-                  norm_send, norm_recv):
+                  box_one, in_one, box_two, in_two, box_z, in_z, final, scalars, load_sem, sent,
+                  pair_recv, recv_one, recv_two, recv_z, swap_sem, norm_recv):
     core, chip, first, second = ring(experts)
     rows = attn_out.shape[0]
     layers = experts // 4
@@ -831,82 +855,72 @@
     load.start()
     pl.semaphore_wait(barrier, experts)
 
-    def pair_copy(block):
+    def send(source, target, send_sem, recv_sem, device):
         return pltpu.make_async_remote_copy(
-            src_ref=gw_ref.at[1 - core, block],
-            dst_ref=pair_in.at[block],
-            send_sem=pair_send.at[block],
-            recv_sem=pair_recv.at[block],
-            device_id=(1 - core, chip),
-            device_id_type=MESH,
-        )
-
-    def copy(source, target, sends, arrivals, index, device):
-        return pltpu.make_async_remote_copy(
-            src_ref=source.at[index],
-            dst_ref=target.at[index],
-            send_sem=sends.at[index],
-            recv_sem=arrivals.at[index],
+            src_ref=source,
+            dst_ref=target,
+            send_sem=send_sem,
+            recv_sem=recv_sem,
             device_id=device,
             device_id_type=MESH,
         )
 
+    def pair_copy(place):
+        return send(
+            gw_ref.at[1 - core, :, place],
+            pair_in.at[:, place],
+            sent.at[0],
+            pair_recv.at[place],
+            (1 - core, chip),
+        )
+
     def to_first(index):
-        return copy(box_one, in_one, send_one, recv_one, index, (core, first))
+        return send(box_one.at[index], in_one.at[index], sent.at[1], recv_one.at[index], (core, first))
 
     def to_second(index):
-        return copy(box_two, in_two, send_two, recv_two, index, (core, second))
+        return send(box_two.at[index], in_two.at[index], sent.at[2], recv_two.at[index], (core, second))
 
     def layer_at(d):
         return lax.rem(layer + 1 + d, layers)
 
     far = 3 - column
 
-    def block_at(d, place):
-        return layer_at(d) * 4 + place
-
     both, one, two = far, lax.rem(first, 4), lax.rem(second, 4)
 
     for place in (both, two, one, column):
-
-        @pl.loop(0, layers)
-        def _(d):
-            pair_copy(block_at(d, place)).start()
+        pair_copy(place).start()
 
     load.wait()
 
-    def summed(block):
-        pair_copy(block).wait_recv()
-        return own[block] + pair_in[block]
-
     for batch, place in ((0, both), (1, one)):
+        pair_copy(place).wait_recv()
 
         @pl.loop(0, layers)
         def _(d):
             index = batch * layers + layer_at(d)
-            box_one[index] = summed(block_at(d, place)).astype(BF16)
+            total = own[layer_at(d), place] + pair_in[layer_at(d), place]
+            box_one[index] = total.astype(BF16)
             to_first(index).start()
+
+    pair_copy(two).wait_recv()
 
     @pl.loop(0, layers)
     def _(d):
         index = layer_at(d)
-        total = summed(block_at(d, two))
+        total = own[index, two] + pair_in[index, two]
         to_first(index).wait_recv()
         box_two[index] = (total + in_one[index].astype(F32)).astype(BF16)
         to_second(index).start()
 
+    pair_copy(column).wait_recv()
+
     def to_layer(index):
-        return pltpu.make_async_remote_copy(
-            src_ref=box_z.at[index],
-            dst_ref=in_z.at[layer],
-            send_sem=send_z.at[index],
-            recv_sem=recv_z.at[layer],
-            device_id=(core, index * 4 + column),
-            device_id_type=MESH,
+        return send(
+            box_z.at[index], in_z.at[layer], sent.at[3], recv_z.at[layer], (core, index * 4 + column)
         )
 
     def column_sum(index):
-        total = summed(index * 4 + column)
+        total = own[index, column] + pair_in[index, column]
         to_first(layers + index).wait_recv()
         total = total + in_one[layers + index].astype(F32)
         to_second(index).wait_recv()
@@ -923,58 +937,31 @@
     @pl.loop(1, layers)
     def _(d):
         index = lax.rem(layer - d + layers, layers)
-        pltpu.make_async_remote_copy(
-            src_ref=box_z.at[index],
-            dst_ref=in_z.at[index],
-            send_sem=send_z.at[index],
-            recv_sem=recv_z.at[index],
-            device_id=(core, index * 4 + column),
-            device_id_type=MESH,
+        send(
+            box_z.at[index], in_z.at[index], sent.at[3], recv_z.at[index], (core, index * 4 + column)
         ).wait_recv()
         final[core] += in_z[index].astype(F32)
 
     def swap(side):
-        return pltpu.make_async_remote_copy(
-            src_ref=final.at[side],
-            dst_ref=final.at[side],
-            send_sem=swap_sem.at[0],
-            recv_sem=swap_sem.at[1],
-            device_id=(1 - core, chip),
-            device_id_type=MESH,
-        )
+        return send(final.at[side], final.at[side], swap_sem.at[0], swap_sem.at[1], (1 - core, chip))
 
     mine = final[core]
     swap(core).start()
 
-    scalars[experts + core] = square_ref[...] + jnp.sum(mine * mine)
+    scalars[experts + core] = square_ref[...] + jnp.sum(mine * mine, axis=0, keepdims=True)
 
     def norm_pair(side):
-        return pltpu.make_async_remote_copy(
-            src_ref=scalars.at[experts + side],
-            dst_ref=scalars.at[experts + side],
-            send_sem=swap_sem.at[2],
-            recv_sem=swap_sem.at[3],
-            device_id=(1 - core, chip),
-            device_id_type=MESH,
-        )
+        mine = scalars.at[experts + side]
+        return send(mine, mine, swap_sem.at[2], swap_sem.at[3], (1 - core, chip))
 
     norm_pair(core).start()
     norm_pair(1 - core).wait_recv()
     scalars[chip] = scalars[experts] + scalars[experts + 1]
 
-    def norm_copy(j, block, peer):
-        return pltpu.make_async_remote_copy(
-            src_ref=scalars.at[block],
-            dst_ref=scalars.at[block],
-            send_sem=norm_send.at[j],
-            recv_sem=norm_recv.at[j],
-            device_id=(core, peer),
-            device_id_type=MESH,
-        )
-
     @pl.loop(1, experts)
     def _(j):
-        norm_copy(j, chip, lax.rem(chip + j, experts)).start()
+        mine = scalars.at[chip]
+        send(mine, mine, sent.at[4], norm_recv.at[0], (core, lax.rem(chip + j, experts))).start()
 
     swap(1 - core).wait_recv()
     for side in range(2):
@@ -986,34 +973,23 @@
     phi_out[...] = final[0, 6 * rows : 6 * rows + experts, 0:rows]
     norm_out[...] = final[1, 6 * rows : 6 * rows + 4, 0:rows]
 
-    @pl.loop(1, experts)
-    def _(j):
-        source = lax.rem(chip - j + experts, experts)
-        norm_copy(j, source, source).wait_recv()
-
-    total_ref[...] = jnp.sqrt(jnp.sum(scalars[0:experts], axis=0))
+    others = scalars.at[pl.ds(0, experts - 1)]
+    norms = send(others, others, sent.at[4], norm_recv.at[0], (1 - core, chip))
+    norms.wait_recv()
+    lanes = jnp.sum(scalars[0:experts], axis=0)
+    total = jnp.sqrt(jnp.sum(lanes, axis=-1, keepdims=True))
+    total_ref[...] = jnp.broadcast_to(total, (1, 128))
     swap(core).wait_send()
     norm_pair(core).wait_send()
 
-    @pl.loop(0, experts)
-    def _(block):
-        pair_copy(block).wait_send()
-
-    @pl.loop(0, 2 * layers)
-    def _(index):
-        to_first(index).wait_send()
-
-    @pl.loop(0, layers)
-    def _(index):
-        to_second(index).wait_send()
-
-    @pl.loop(1, layers)
-    def _(d):
-        to_layer(lax.rem(layer + d, layers)).wait_send()
-
-    @pl.loop(1, experts)
-    def _(j):
-        norm_copy(j, chip, lax.rem(chip + j, experts)).wait_send()
+    for source, sem in (
+        (gw_ref.at[1 - core], 0),
+        (box_one, 1),
+        (box_two, 2),
+        (box_z.at[pl.ds(0, layers - 1)], 3),
+    ):
+        send(source, source, sent.at[sem], sent.at[sem], (1 - core, chip)).wait_send()
+    norms.wait_send()
 
 
 def reduce_grads(grads, squares, experts):
@@ -1033,8 +1009,8 @@
         in_specs=[pl.BlockSpec(memory_space=pl.ANY)] + whole(1),
         out_specs=tuple(whole(4)),
         scratch_shapes=[
-            pltpu.VMEM((experts,) + block, F32),
-            pltpu.VMEM((experts,) + block, F32),
+            pltpu.VMEM((layers, 4) + block, F32),
+            pltpu.VMEM((layers, 4) + block, F32),
             pltpu.VMEM((2 * layers,) + block, BF16),
             pltpu.VMEM((2 * layers,) + block, BF16),
             pltpu.VMEM((layers,) + block, BF16),
@@ -1044,33 +1020,29 @@
             pltpu.VMEM((2,) + block, F32),
             pltpu.VMEM((experts + 2, 1, 128), F32),
             dma((1,)),
-            dma((experts,)),
-            dma((experts,)),
-            dma((2 * layers,)),
+            dma((5,)),
+            dma((4,)),
             dma((2 * layers,)),
             dma((layers,)),
             dma((layers,)),
-            dma((layers,)),
-            dma((layers,)),
             dma((4,)),
-            dma((experts,)),
-            dma((experts,)),
+            dma((1,)),
         ],
         compiler_params=pltpu.CompilerParams(
             collective_id=2, has_side_effects=True, vmem_limit_bytes=vmem_bytes(experts, 8)
         ),
         name="reduce_grads",
-    )(grads, squares)
+    )(grads.reshape((2, layers, 4) + block), squares)
 
 
 def adam_update(weight, first_moment, second_moment, gradient, factor, learning_rate, decay_rate):
     clipped = gradient * factor
     first_new = BETA_FIRST * first_moment + (1.0 - BETA_FIRST) * clipped
     second_new = BETA_SECOND * second_moment + (1.0 - BETA_SECOND) * clipped * clipped
-    first_hat = first_new / (1.0 - BETA_FIRST**STEP)
-    second_hat = second_new / (1.0 - BETA_SECOND**STEP)
-    weight_new = weight - learning_rate * (
-        first_hat / (jnp.sqrt(second_hat) + ADAM_EPS) + decay_rate * weight
+    step_rate = learning_rate / (1.0 - BETA_FIRST**STEP)
+    root = jnp.sqrt(second_new * (1.0 / (1.0 - BETA_SECOND**STEP)))
+    weight_new = weight * (1.0 - learning_rate * decay_rate) - step_rate * (
+        first_new / (root + ADAM_EPS)
     )
     return (weight_new, first_new, second_new)
 

time: 111 us -> 98.6 us (0.89)
  Pallas kernels: 108 us -> 96.5 us
    pallas_call x1, Pallas kernels: 24.7 us -> 21.4 us  [reduce_grads(): pl.pallas_call(functools.partial(reduce_kernel, experts), out_shape=(shap...]
    pallas_call x1, Pallas kernels: 24.9 us -> 21.8 us  [backward_local(): pl.pallas_call(functools.partial(backward_kernel, experts), out_shape=(sh...]
    pallas_call x1, Pallas kernels: 19.6 us -> 17 us  [run_experts(): pl.pallas_call(functools.partial(expert_kernel, experts), out_shape=(shap...]
    pallas_call x1, Pallas kernels: 14.9 us -> 13.1 us  [forward_local(): pl.pallas_call(functools.partial(forward_kernel, experts), out_shape=(sha...]
where the time goes in v4:
time: 98.6 us; the launch traced here: 98.7 us
  Pallas kernels  96.5 us (98%)
  between operations  2.13 us (2%)
    pallas_call x1, Pallas kernels, backward_local(): pl.pallas_call(functools.partial(backward_kernel, experts), out_shape=(sh...  21.8 us
    pallas_call x1, Pallas kernels, reduce_grads(): pl.pallas_call(functools.partial(reduce_kernel, experts), out_shape=(shap...  21.4 us
    pallas_call x1, Pallas kernels, gather_weights(): pl.pallas_call(functools.partial(gather_kernel, experts), out_shape=jax.S...  18.5 us
    pallas_call x1, Pallas kernels, run_experts(): pl.pallas_call(functools.partial(expert_kernel, experts), out_shape=(shap...  17 us
    pallas_call x1, Pallas kernels, forward_local(): pl.pallas_call(functools.partial(forward_kernel, experts), out_shape=(sha...  13.1 us
    pallas_call x1, Pallas kernels, update(): pl.pallas_call(update_kernel, grid=(UPDATE_STEPS,), out_shape=tuple((jax....  4.57 us

profile of v4, /device:TPU:0, one launch (start us, length us, event | category | flops | bytes accessed | tf_op | source)
XLA Modules:
  0.0 98.7 jit_solution(7637135552394503492)
XLA Ops:
  0.7 0.0 copy-start.16
  0.7 0.0 copy-start.2
  0.7 18.5 %gather_weights.1.main_ref = bf16[16,2,160,128]{3,2,1,0:T(8,128)(2,1)S(1)} custom-call(f32[24,1536]{1,0:T(8,128)} %refs_0_.1, f32[16,24]{1,0:T(8,128)} %bitcast.10, f32[4,24]{1,0:T(4,128)} %refs_8_.1), custom_call_target="tpu_custom_call" | custom-call | tf_op jit(solution)/shard_map/gather_weights/pallas_call | solution.py:180
  19.2 0.0 copy-done.16
  19.2 0.0 copy-done.2
  19.3 0.0 copy-start
  19.3 0.0 copy-start.1
  19.3 13.1 %forward_local.1 = (bf16[9,1408,128]{2,1,0:T(8,128)(2,1)S(1)}, bf16[1408,384]{1,0:T(8,128)(2,1)S(1)}, f32[1408,128]{1,0:T(8,128)S(1)}, f32[1360,384]{1,0:T(8,128...) custom-call(s32[1,5]{1,0:T(1,128)S(1)} %copy-done.16, ...), custom_call_target="tpu_custom_call" | custom-call | tf_op jit(solution)/shard_map/forward_local/pallas_call | solution.py:453
  32.4 0.0 copy-done
  32.4 0.0 copy-done.1
  32.4 17.0 %run_experts.1 = (bf16[128,384]{1,0:T(8,128)(2,1)S(1)}, bf16[128,384]{1,0:T(8,128)(2,1)S(1)}, f32[1,384,768]{2,1,0:T(8,128)S(1)}, f32[1,768,384]{2,1,0:T(8,128)S(1)}, f32[1,128]{1,0:T(1,128)S(1)}) custom-call(bf16[16,32,128]{2,1,0:T(8,128)(2,1)S(1)} %get-tuple-element.62.pack_ref, f32[1,384,768]{2,1,0:T(8,128)S(1)} %copy-done, f32[1,768,384]{2,1,0:T(8,128)S(1)} %copy-done.1), custom_call_target="tpu_custom_call" | custom-call | tf_op jit(solution)/shard_map/run_experts/pallas_call | solution.py:591
  49.5 0.0 copy-start.5
  49.5 0.0 copy-start.6
  49.5 0.0 copy-start.8
  49.5 0.0 copy-start.9
  49.5 21.8 %backward_local.1 = (bf16[1360,384]{1,0:T(8,128)(2,1)}, bf16[1360,384]{1,0:T(8,128)(2,1)}, f32[2,16,160,128]{3,2,1,0:T(8,128)S(1)}) custom-call(s32[1,5]{1,0:T(1,128)S(1)} %copy-done.16, bf16[1360,384]{1,0:T(8,128)(2,1)S(1)} %copy-done.2, bf16[16,2,160,128]{3,2,1,0:T(8,128)(2,1)S(1)} %gather_weights.1.main_ref, ...), custom_call_target="tpu_custom_call" | custom-call | tf_op jit(solution)/shard_map/backward_local/pallas_call | solution.py:808
  71.3 0.0 copy-start.3
  71.3 0.0 copy-start.4
  71.3 0.0 copy-start.7
  71.3 0.0 copy-start.10
  71.4 0.0 copy-start.11
  71.4 0.0 copy-start.12
  71.4 0.0 copy-start.13
  71.4 0.0 copy-start.14
  71.4 0.0 copy-start.15
  71.4 21.4 %reduce_grads.1 = (f32[24,1536]{1,0:T(8,128)S(1)}, f32[16,24]{1,0:T(8,128)S(1)}, f32[4,24]{1,0:T(4,128)S(1)}, f32[1,128]{1,0:T(1,128)S(1)}) custom-call(f32[2,4,4,160,128]{4,3,2,1,0:T(8,128)S(1)} %bitcast.9, f32[1,128]{1,0:T(1,128)S(1)} %get-tuple-element.68.square_ref), custom_call_target="tpu_custom_call" | custom-call | tf_op jit(solution)/shard_map/reduce_grads/pallas_call | solution.py:1001
  92.8 0.0 copy-done.5
  92.8 0.0 copy-done.6
  92.8 0.0 copy-done.8
  92.8 0.0 copy-done.9
  92.9 0.0 copy-done.3
  92.9 0.0 copy-done.4
  92.9 0.0 copy-done.7
  92.9 0.0 copy-done.10
  92.9 0.0 copy-done.11
  92.9 0.0 copy-done.12
  92.9 0.0 copy-done.13
  92.9 0.0 copy-done.14
  92.9 0.0 copy-done.15
  92.9 4.6 %update.1 = (f32[24,1536]{1,0:T(8,128)}, f32[24,1536]{1,0:T(8,128)}, f32[24,1536]{1,0:T(8,128)}, f32[16,24]{1,0:T(8,128)}, f32[16,24]{1,0:T(8,128)}, /*index=5*/...) custom-call(f32[1,128]{1,0:T(1,128)S(1)} %get-tuple-element.69.norm_, ...), custom_call_target="tpu_custom_call" | custom-call | tf_op jit(solution)/shard_map/update/pallas_call | solution.py:1082
Async XLA Ops:
  0.7 18.6 %copy-start.16 = (s32[1,5]{1,0:T(1,128)S(1)}, s32[1,5]{1,0:T(1,128)}, u32[]{:S(2)}) copy-start(s32[1,5]{1,0:T(1,128)} %len_ref.3) | copy-start | bytes 64
  0.7 18.6 %copy-start.2 = (bf16[1360,384]{1,0:T(8,128)(2,1)S(1)}, bf16[1360,384]{1,0:T(8,128)(2,1)}, u32[]{:S(2)}) copy-start(bf16[1360,384]{1,0:T(8,128)(2,1)} %patch_ref.3) | copy-start | bytes 3133444
  19.3 13.2 %copy-start = (f32[1,384,768]{2,1,0:T(8,128)S(1)}, f32[1,384,768]{2,1,0:T(8,128)}, u32[]{:S(2)}) copy-start(f32[1,384,768]{2,1,0:T(8,128)} %refs_12_.1) | copy-start | bytes 3538948
  19.3 13.2 %copy-start.1 = (f32[1,768,384]{2,1,0:T(8,128)S(1)}, f32[1,768,384]{2,1,0:T(8,128)}, u32[]{:S(2)}) copy-start(f32[1,768,384]{2,1,0:T(8,128)} %refs_16_.1) | copy-start | bytes 3538948
  49.5 43.4 %copy-start.5 = (f32[1,768,384]{2,1,0:T(8,128)S(1)}, f32[1,768,384]{2,1,0:T(8,128)}, u32[]{:S(2)}) copy-start(f32[1,768,384]{2,1,0:T(8,128)} %refs_17_.1) | copy-start | bytes 3538948
  49.5 43.3 %copy-start.6 = (f32[1,768,384]{2,1,0:T(8,128)S(1)}, f32[1,768,384]{2,1,0:T(8,128)}, u32[]{:S(2)}) copy-start(f32[1,768,384]{2,1,0:T(8,128)} %refs_18_.1) | copy-start | bytes 3538948
  49.5 43.3 %copy-start.8 = (f32[24,1536]{1,0:T(8,128)S(1)}, f32[24,1536]{1,0:T(8,128)}, u32[]{:S(2)}) copy-start(f32[24,1536]{1,0:T(8,128)} %refs_1_.1) | copy-start | bytes 442372
  49.5 43.3 %copy-start.9 = (f32[24,1536]{1,0:T(8,128)S(1)}, f32[24,1536]{1,0:T(8,128)}, u32[]{:S(2)}) copy-start(f32[24,1536]{1,0:T(8,128)} %refs_2_.1) | copy-start | bytes 442372
  71.3 21.5 %copy-start.3 = (f32[1,384,768]{2,1,0:T(8,128)S(1)}, f32[1,384,768]{2,1,0:T(8,128)}, u32[]{:S(2)}) copy-start(f32[1,384,768]{2,1,0:T(8,128)} %refs_13_.1) | copy-start | bytes 3538948
  71.3 21.5 %copy-start.4 = (f32[1,384,768]{2,1,0:T(8,128)S(1)}, f32[1,384,768]{2,1,0:T(8,128)}, u32[]{:S(2)}) copy-start(f32[1,384,768]{2,1,0:T(8,128)} %refs_14_.1) | copy-start | bytes 3538948
  71.3 21.5 %copy-start.7 = (f32[24,1536]{1,0:T(8,128)S(1)}, f32[24,1536]{1,0:T(8,128)}, u32[]{:S(2)}) copy-start(f32[24,1536]{1,0:T(8,128)} %refs_0_.1) | copy-start | bytes 442372
  71.3 21.5 %copy-start.10 = (f32[24,16]{0,1:T(8,128)S(1)}, f32[24,16]{0,1:T(8,128)}, u32[]{:S(2)}) copy-start(f32[24,16]{0,1:T(8,128)} %param.23) | copy-start | bytes 4612
  71.4 21.5 %copy-start.11 = (f32[4,24]{1,0:T(4,128)S(1)}, f32[4,24]{1,0:T(4,128)}, u32[]{:S(2)}) copy-start(f32[4,24]{1,0:T(4,128)} %refs_8_.1) | copy-start | bytes 1156
  71.4 21.5 %copy-start.12 = (f32[24,16]{0,1:T(8,128)S(1)}, f32[24,16]{0,1:T(8,128)}, u32[]{:S(2)}) copy-start(f32[24,16]{0,1:T(8,128)} %param.24) | copy-start | bytes 4612
  71.4 21.5 %copy-start.13 = (f32[24,16]{0,1:T(8,128)S(1)}, f32[24,16]{0,1:T(8,128)}, u32[]{:S(2)}) copy-start(f32[24,16]{0,1:T(8,128)} %param.25) | copy-start | bytes 4612
  71.4 21.5 %copy-start.14 = (f32[4,24]{1,0:T(4,128)S(1)}, f32[4,24]{1,0:T(4,128)}, u32[]{:S(2)}) copy-start(f32[4,24]{1,0:T(4,128)} %refs_9_.1) | copy-start | bytes 1156
  71.4 21.5 %copy-start.15 = (f32[4,24]{1,0:T(4,128)S(1)}, f32[4,24]{1,0:T(4,128)}, u32[]{:S(2)}) copy-start(f32[4,24]{1,0:T(4,128)} %refs_10_.1) | copy-start | bytes 1156

commit v5 on v4

--- a/solution.py
+++ b/solution.py
@@ -76,7 +76,7 @@
     return core, chip, first, second
 
 
-def gather_kernel(experts, attn_hbm, phi_hbm, norm_hbm, out, stage, attn_ref, phi_ref, norm_ref, load_sem,
+def gather_kernel(experts, attn_hbm, phi_hbm, norm_hbm, patch_hbm, out, normal_ref, inverse_ref, patch_ref, stage, attn_ref, phi_ref, norm_ref, load_sem,
                   sent, recv):
     core, chip, first, second = ring(experts)
     rows = attn_ref.shape[0]
@@ -88,6 +88,8 @@
     ]
     for load in loads:
         load.start()
+    load_patches = pltpu.make_async_copy(patch_hbm, patch_ref, load_sem.at[3])
+    load_patches.start()
     column = lax.rem(chip, 4)
     layers = experts // 4
     layer = chip // 4
@@ -147,6 +149,17 @@
     along(chip, second).start()
     to_pair(chip).start()
 
+    load_patches.wait()
+
+    def statistics(at, count, carry):
+        rows = pl.ds(at, count)
+        normal, inverse = normed(patch_ref[rows, :].astype(F32))
+        normal_ref[rows, :] = normal
+        inverse_ref[rows, :] = jnp.broadcast_to(inverse, (count, 128))
+        return carry
+
+    over_rows(0, patch_ref.shape[0], 0, statistics)
+
     @pl.loop(1, layers)
     def _(d):
         block = lax.rem(layer - d + layers, layers) * 4 + column
@@ -174,28 +187,34 @@
     copy(out.at[:, core], out.at[:, 1 - core], sent.at[1], sent.at[2], (1 - core, chip)).wait()
 
 
-def gather_weights(attn_weight, phi_turned, norm_params, experts):
+def gather_weights(attn_weight, phi_turned, norm_params, patches, experts):
     rows = block_rows(experts)
+    tokens = patches.shape[0]
     dma = pltpu.SemaphoreType.DMA
     return pl.pallas_call(
         functools.partial(gather_kernel, experts),
-        out_shape=jax.ShapeDtypeStruct((experts, 2, rows, 128), BF16),
-        in_specs=[pl.BlockSpec(memory_space=pltpu.HBM)] * 3,
-        out_specs=whole(1)[0],
+        out_shape=(
+            jax.ShapeDtypeStruct((experts, 2, rows, 128), BF16),
+            jax.ShapeDtypeStruct((tokens, D), F32),
+            jax.ShapeDtypeStruct((tokens, 128), F32),
+        ),
+        in_specs=[pl.BlockSpec(memory_space=pltpu.HBM)] * 4,
+        out_specs=tuple(whole(3)),
         scratch_shapes=[
+            pltpu.VMEM((tokens, D), BF16),
             pltpu.VMEM((rows, 128), F32),
             pltpu.VMEM((attn_weight.shape[0], 2 * D), F32),
             pltpu.VMEM(phi_turned.shape, F32),
             pltpu.VMEM(norm_params.shape, F32),
-            dma((3,)),
+            dma((4,)),
             dma((3,)),
             dma((experts,)),
         ],
         compiler_params=pltpu.CompilerParams(
-            collective_id=0, has_side_effects=True, vmem_limit_bytes=vmem_bytes(experts, 3)
+            collective_id=0, has_side_effects=True, vmem_limit_bytes=vmem_bytes(experts, 10)
         ),
         name="gather_weights",
-    )(attn_weight, phi_turned, norm_params)
+    )(attn_weight, phi_turned, norm_params, patches)
 
 
 def unpack_weight(main_ref, side, part):
@@ -275,6 +294,10 @@
     return carry
 
 
+def thrice(values):
+    return jnp.concatenate([values] * 3, axis=1)
+
+
 def fold_rows(values):
     return jnp.sum(values.reshape(values.shape[0] // 8, 8, values.shape[1]), axis=0)
 
@@ -305,9 +328,10 @@
     return (column >= shift) & (column < shift + full)
 
 
-def forward_kernel(experts, len_ref, patch_ref, main_ref, cot_hbm, qkv_ref, o_ref, lse_ref, x1_ref,
-                   h2_ref, disp_ref, comb_ref, gy_ref, pack_ref, logit, packf, scores,
-                   probs, peaks, cot_ref, h1_all, load_sem):
+def forward_kernel(experts, len_ref, patch_ref, main_ref, norm_ref, cot_hbm, w_ref, phi_ref, norms_ref,
+                   normal_ref, inverse_ref, h1_all, qkv_ref, o_ref, lse_ref, x1_ref, h2_ref, disp_ref,
+                   comb_ref, gy_ref, pack_ref, logit, packf, scores,
+                   probs, peaks, cot_ref, load_sem):
     load = pltpu.make_async_copy(cot_hbm, cot_ref, load_sem.at[0])
     load.start()
     tokens = patch_ref.shape[0]
@@ -315,14 +339,15 @@
     tile = tokens // 5
     phi, norms = unpack_small(main_ref, experts)
     starts, ends, total = slot_bounds(len_ref, columns)
-    w_q, w_k = unpack_weight(main_ref, 0, 0), unpack_weight(main_ref, 0, 1)
-    w_v = unpack_weight(main_ref, 1, 0)
-    w_qkv = jnp.concatenate([w_q, w_k, w_v], axis=1)
+    norms_ref[...] = norms
+    phi_ref[...] = phi
+    for k in range(4):
+        w_ref[:, k * D : (k + 1) * D] = unpack_weight(main_ref, k // 2, k % 2)
+    w_qkv = w_ref[:, : 3 * D]
 
     def first_norm(at, count, carry):
         rows = pl.ds(at, count)
-        normal, _ = normed(patch_ref[rows, :].astype(F32))
-        h1_all[rows, :] = (normal * norms[0:1] + norms[1:2]).astype(BF16)
+        h1_all[rows, :] = (norm_ref[rows, :] * norms[0:1] + norms[1:2]).astype(BF16)
         return carry
 
     over_rows(0, tokens, 0, first_norm)
@@ -379,7 +404,7 @@
     over_images(len_ref, tokens, attend)
 
     load.wait()
-    w_o = unpack_weight(main_ref, 1, 1)
+    w_o = w_ref[:, 3 * D :]
     for t in range(5):
         rows = pl.ds(t * tile, tile)
         x1_ref[rows, :] = mm(o_ref[rows, :], w_o)
@@ -387,7 +412,9 @@
     def second_norm(at, count, carry):
         rows = pl.ds(at, count)
         x1 = patch_ref[rows, :].astype(F32) + x1_ref[rows, :]
-        normal, _ = normed(x1)
+        normal, inverse = normed(x1)
+        normal_ref[rows, :] = normal
+        inverse_ref[rows, :] = jnp.broadcast_to(inverse, (count, 128))
         h2_ref[rows, :] = (normal * norms[2:3] + norms[3:4]).astype(BF16)
         valid = at + lax.broadcasted_iota(jnp.int32, (count, 1), 0) < total
         x1_ref[rows, :] = jnp.where(valid, x1, 0.0)
@@ -446,13 +473,19 @@
         wide[:, 0:IMAGES, c * 128 : (c + 1) * 128] = packf[:, c * IMAGES : (c + 1) * IMAGES, :]
 
 
-def forward_local(lengths, patches, main, cotangent, experts):
+def forward_local(lengths, patches, main, normal, cotangent, experts):
     tokens = patches.shape[0]
     columns = experts * SLOT_ROWS
     shape = jax.ShapeDtypeStruct
     return pl.pallas_call(
         functools.partial(forward_kernel, experts),
         out_shape=(
+            shape((D, 4 * D), BF16),
+            shape((columns, D), BF16),
+            shape((8, D), F32),
+            shape((tokens, D), F32),
+            shape((tokens, 128), F32),
+            shape((tokens, D), BF16),
             shape((9, tokens + WINDOW_PAD, 128), BF16),
             shape((tokens + WINDOW_PAD, D), BF16),
             shape((tokens + WINDOW_PAD, 128), F32),
@@ -464,9 +497,9 @@
             shape((experts, 32, 128), BF16),
         ),
         in_specs=[pl.BlockSpec(memory_space=pltpu.SMEM)]
-        + whole(2)
+        + whole(3)
         + [pl.BlockSpec(memory_space=pltpu.HBM)],
-        out_specs=tuple(whole(9)),
+        out_specs=tuple(whole(15)),
         scratch_shapes=[
             pltpu.VMEM((tokens, columns), F32),
             pltpu.VMEM((experts, 16, 128), F32),
@@ -474,17 +507,15 @@
             pltpu.VMEM((2, LONG_WINDOW, LONG_SPAN), BF16),
             pltpu.VMEM((2, LONG_WINDOW, 128), F32),
             pltpu.VMEM((tokens, D), BF16),
-            pltpu.VMEM((tokens, D), BF16),
             pltpu.SemaphoreType.DMA((1,)),
         ],
         compiler_params=pltpu.CompilerParams(vmem_limit_bytes=vmem_bytes(experts, 24)),
         name="forward_local",
-    )(lengths, patches, main, cotangent)
+    )(lengths, patches, main, normal, cotangent)
 
 
 def expert_kernel(experts, pack_ref, in_ref, out_ref, result_ref, gslot_ref, gin_ref, gout_ref,
-                  square_ref, inbox, partial, given, outbox, back, packf, wide, packe, widee,
-                  sems):
+                  square_ref, inbox, partial, given, outbox, back, packf, packe, widee, sems):
     core = lax.axis_index("batch")
     chip = lax.axis_index("expert")
     barrier = pltpu.get_barrier_semaphore()
@@ -497,7 +528,8 @@
     pl.semaphore_signal(barrier, inc=1, device_id=(1 - core, chip), device_id_type=MESH)
     w_in = in_ref[0].astype(BF16)
     w_out = out_ref[0].astype(BF16)
-    inbox[core, chip] = pack_ref[chip]
+    for part in range(2):
+        inbox[part, core, chip] = pack_ref[chip, part * 16 : (part + 1) * 16, :]
     pl.semaphore_wait(barrier, experts)
 
     def copy(source, target, sem, device):
@@ -510,61 +542,85 @@
             device_id_type=MESH,
         )
 
-    @pl.loop(1, experts)
-    def _(j):
-        peer = lax.rem(chip + j, experts)
-        copy(pack_ref.at[peer], inbox.at[core, chip], 0, (core, peer)).start()
-
     others = pl.ds(0, experts - 1)
-    first = copy(pack_ref.at[others], inbox.at[core, others], 0, (core, chip))
-    first.wait_recv()
-    pair = copy(inbox.at[core], inbox.at[core], 2, (1 - core, chip))
-    pair.start()
-    pair.wait_recv()
-
-    def spread(side, part):
-        packe[...] = inbox[side, :, part * 16 : (part + 1) * 16, :].astype(F32)
+    firsts, pairs, halves, seconds = [], [], [], []
+    for part in range(2):
+        block = pl.ds(part * 16, 16)
+
+        @pl.loop(1, experts)
+        def _(j):
+            peer = lax.rem(chip + j, experts)
+            copy(
+                pack_ref.at[peer, block], inbox.at[part, core, chip], 2 * part, (core, peer)
+            ).start()
+
+        firsts.append(
+            copy(pack_ref.at[others, block], inbox.at[part, core, others], 2 * part, (core, chip))
+        )
+        mine = inbox.at[part, core]
+        pairs.append(copy(mine, mine, 4 + 2 * part, (1 - core, chip)))
+        halves.append(copy(partial.at[part], given.at[part], 8 + 2 * part, (1 - core, chip)))
+        seconds.append(
+            copy(outbox.at[part, others], back.at[part, others], 12 + 2 * part, (core, chip))
+        )
+
+    def spread(part, side):
+        packe[...] = inbox[part, side].astype(F32)
         unpack_rows(packe, widee)
         return widee[...].reshape(experts * SLOT_ROWS, D).astype(BF16)
 
-    def run(side):
-        slots = spread(side, 0)
-        grads = spread(side, 1)
+    root = math.sqrt(2.0 / math.pi)
+
+    def forward(side):
+        slots = spread(0, side)
         hidden = mm(slots, w_in)
-        root = math.sqrt(2.0 / math.pi)
         bent = jnp.tanh(root * (hidden + 0.044715 * (hidden * hidden * hidden)))
         half = 0.5 * (1.0 + bent)
         act = (hidden * half).astype(BF16)
         slope = half + 0.5 * hidden * (1.0 - bent * bent) * (
             root * (1.0 + 3.0 * 0.044715 * (hidden * hidden))
         )
-        result = mm(act, w_out)
+        return slots, act, slope, mm(act, w_out)
+
+    def backward(side, slope):
+        grads = spread(1, side)
         grad_hidden = (mm_nt(grads, w_out) * slope).astype(BF16)
-        grad_slots = mm_nt(grad_hidden, w_in)
-        return slots, grads, act, grad_hidden, result, grad_slots
-
-    theirs = run(1 - core)
-    for part in range(2):
-        pack_rows(packf, theirs[4 + part].reshape(experts, SLOT_ROWS, D))
-        partial[:, part * 16 : (part + 1) * 16, :] = packf[...].astype(BF16)
-    halves = copy(partial, given, 4, (1 - core, chip))
-    halves.start()
-    ours = run(core)
-    halves.wait_recv()
-    for part in range(2):
-        block = slice(part * 16, (part + 1) * 16)
-        pack_rows(packf, ours[4 + part].reshape(experts, SLOT_ROWS, D))
-        outbox[:, block, :] = (packf[...] + given[:, block, :].astype(F32)).astype(BF16)
-
-    @pl.loop(1, experts)
-    def _(j):
-        peer = lax.rem(chip + j, experts)
-        copy(outbox.at[peer], back.at[chip], 6, (core, peer)).start()
-
-    back[chip] = outbox[chip]
-    grad_out = mm_tn(ours[2], ours[1]) + mm_tn(theirs[2], theirs[1])
+        return grads, grad_hidden, mm_nt(grad_hidden, w_in)
+
+    def give_half(part, values):
+        pack_rows(packf, values.reshape(experts, SLOT_ROWS, D))
+        partial[part] = packf[...].astype(BF16)
+        halves[part].start()
+
+    def send_back(part, values):
+        pack_rows(packf, values.reshape(experts, SLOT_ROWS, D))
+        halves[part].wait_recv()
+        outbox[part] = (packf[...] + given[part].astype(F32)).astype(BF16)
+
+        @pl.loop(1, experts)
+        def _(j):
+            peer = lax.rem(chip + j, experts)
+            copy(outbox.at[part, peer], back.at[part, chip], 12 + 2 * part, (core, peer)).start()
+
+        back[part, chip] = outbox[part, chip]
+
+    firsts[0].wait_recv()
+    pairs[0].start()
+    pairs[0].wait_recv()
+    their_slots, their_act, their_slope, their_result = forward(1 - core)
+    give_half(0, their_result)
+    firsts[1].wait_recv()
+    pairs[1].start()
+    our_slots, our_act, our_slope, our_result = forward(core)
+    send_back(0, our_result)
+    pairs[1].wait_recv()
+    their_grads, their_hidden, their_back = backward(1 - core, their_slope)
+    give_half(1, their_back)
+    our_grads, our_hidden, our_back = backward(core, our_slope)
+    send_back(1, our_back)
+    grad_out = mm_tn(our_act, our_grads) + mm_tn(their_act, their_grads)
     gout_ref[0] = grad_out
-    grad_in = mm_tn(ours[0], ours[3]) + mm_tn(theirs[0], theirs[3])
+    grad_in = mm_tn(our_slots, our_hidden) + mm_tn(their_slots, their_hidden)
     gin_ref[0] = grad_in
     squares = jnp.zeros((1, 128), F32)
     for grad in (grad_out, grad_in):
@@ -572,18 +628,13 @@
         for c in range(0, grad.shape[1], 128):
             squares = squares + columns[:, c : c + 128]
     square_ref[...] = squares
-
-    second = copy(outbox.at[others], back.at[others], 6, (core, chip))
-    second.wait_recv()
     for part, target in enumerate((result_ref, gslot_ref)):
-        packe[...] = back[:, part * 16 : (part + 1) * 16, :].astype(F32)
+        seconds[part].wait_recv()
+        packe[...] = back[part].astype(F32)
         unpack_rows(packe, widee)
         target[...] = widee[...].reshape(experts * SLOT_ROWS, D).astype(BF16)
-
-    first.wait_send()
-    pair.wait_send()
-    halves.wait_send()
-    second.wait_send()
+    for sent in firsts + pairs + halves + seconds:
+        sent.wait_send()
 
 
 def run_experts(packed, expert_in, expert_out, experts):
@@ -600,17 +651,16 @@
         in_specs=whole(3),
         out_specs=tuple(whole(5)),
         scratch_shapes=[
-            pltpu.VMEM((2, experts, 32, 128), BF16),
-            pltpu.VMEM((experts, 32, 128), BF16),
-            pltpu.VMEM((experts, 32, 128), BF16),
-            pltpu.VMEM((experts, 32, 128), BF16),
-            pltpu.VMEM((experts, 32, 128), BF16),
+            pltpu.VMEM((2, 2, experts, 16, 128), BF16),
+            pltpu.VMEM((2, experts, 16, 128), BF16),
+            pltpu.VMEM((2, experts, 16, 128), BF16),
+            pltpu.VMEM((2, experts, 16, 128), BF16),
+            pltpu.VMEM((2, experts, 16, 128), BF16),
+            pltpu.VMEM((experts, 16, 128), F32),
             pltpu.VMEM((experts, 16, 128), F32),
             pltpu.VMEM((experts, SLOT_ROWS, D), F32),
-            pltpu.VMEM((experts, 16, 128), F32),
-            pltpu.VMEM((experts, SLOT_ROWS, D), F32),
-        ]
-        + [pltpu.SemaphoreType.DMA((8,))],
+            pltpu.SemaphoreType.DMA((16,)),
+        ],
         compiler_params=pltpu.CompilerParams(
             collective_id=1, has_side_effects=True, vmem_limit_bytes=vmem_bytes(experts, 8)
         ),
@@ -618,15 +668,14 @@
     )(packed, expert_in, expert_out)
 
 
-def backward_kernel(experts, len_ref, patch_ref, main_ref, qkv_ref, o_ref, lse_ref,
-                    x1_ref, h2_ref, disp_ref, comb_ref, gy_ref, result_ref, gslot_ref, block_ref,
-                    input_ref, gw_ref, gdisp, glog, gx1, branch, go, gqkv,
-                    h1_all, scores, grad_probs, probs, grad_scores, sums, gcomb,
-                    wide_rows):
-    tokens = patch_ref.shape[0]
+def backward_kernel(experts, len_ref, normal_one, inverse_one, w_ref, phi_ref, norms_ref, normal_two,
+                    inverse_two, h1_all, qkv_ref, o_ref, lse_ref, h2_ref, disp_ref, comb_ref, gy_ref,
+                    result_ref, gslot_ref, input_ref, gw_ref, gdisp, glog, gx1, branch, go, gqkv,
+                    scores, grad_probs, probs, grad_scores, sums, gcomb, wide_rows):
+    tokens = h2_ref.shape[0]
     columns = experts * SLOT_ROWS
     tile = tokens // 5
-    phi, norms = unpack_small(main_ref, experts)
+    phi, norms = phi_ref[...], norms_ref[...]
     result = result_ref[...]
     gslots = gslot_ref[...]
 
@@ -649,14 +698,12 @@
     for t in range(5):
         rows = pl.ds(t * tile, tile)
         here = pl.ds(place(t * tile), tile)
-        gx1[rows, :] = mm(comb_ref[rows, :].astype(BF16), result)
         gcomb[here, :] = mm_nt(gy_ref[rows, :], result)
         if not kept:
             gdisp[here, :] = mm_nt(h2_ref[rows, :], gslots)
 
         def logit_grads(at, count, carry):
             rows, here = pl.ds(at, count), pl.ds(place(at), count)
-            block_ref[rows, :] = (x1_ref[rows, :] + gx1[rows, :]).astype(BF16)
             combine = comb_ref[rows, :]
             weighted = combine * gcomb[here, :]
             glog[rows, :] = (
@@ -675,7 +722,7 @@
         gain, bias = carry
         rows = pl.ds(at, count)
         grad_h2 = gx1[rows, :]
-        normal, inverse = normed(x1_ref[rows, :])
+        normal, inverse = normal_two[rows, :], thrice(inverse_two[rows, :])
         grad_x1 = gy_ref[rows, :].astype(F32) + norm_back(grad_h2, normal, inverse, norms[2:3])
         gx1[rows, :] = grad_x1
         branch[rows, :] = grad_x1.astype(BF16)
@@ -683,7 +730,7 @@
 
     zero = jnp.zeros((8, D), F32)
     gain_two, bias_two = over_rows(0, tokens, (zero, zero), second_norm)
-    w_o = unpack_weight(main_ref, 1, 1)
+    w_o = w_ref[:, 3 * D :]
     for t in range(5):
         rows = pl.ds(t * tile, tile)
         grad_o = mm_nt(branch[rows, :], w_o).astype(BF16)
@@ -734,6 +781,19 @@
             low = values.astype(F32)
             halves = (jnp.where(low_lane, low, 0.0), jnp.where(low_lane, 0.0, low))
             return jnp.concatenate(halves, axis=0).astype(BF16)
+
+        def finish(p):
+            slopes = [grad_scores[(2 * p + g) % 4, :window, :span] for g in range(2)]
+            weights = [probs[(2 * p + g) % 4, :window, :span] for g in range(2)]
+            keys = split(qkv_ref[PAIRS + p, rows, :])
+            news = (
+                jnp.transpose(mm_tn(keys, jnp.concatenate(slopes, axis=0)))[:window] * SCORE_SCALE,
+                mm(jnp.concatenate(slopes, axis=1), split(qkv_ref[p, wide, :])) * SCORE_SCALE,
+                mm(jnp.concatenate(weights, axis=1), split(go[p, wide, :])),
+            )
+            for c in range(3):
+                old = gqkv[c * PAIRS + p, rows, :].astype(F32)
+                gqkv[c * PAIRS + p, rows, :] = jnp.where(inside, news[c], old).astype(BF16)
 
         score(0)
         for n in range(HEADS):
@@ -752,27 +812,16 @@
                 part = jnp.exp(scores[h, r : r + 16, :span] - logs)
                 if r == 0 or r + 16 > full:
                     part = jnp.where(rows_inside(shift, full, r, 16), part, 0.0)
-                probs[h, r : r + 16, :span] = part.astype(BF16)
+                probs[n % 4, r : r + 16, :span] = part.astype(BF16)
                 slope = part * (grad_probs[h, r : r + 16, :span] - inner_row)
-                grad_scores[h, r : r + 16, :span] = slope.astype(BF16)
-            if h == 1:
-                slopes = [grad_scores[g, :window, :span] for g in range(2)]
-                weights = [probs[g, :window, :span] for g in range(2)]
-                keys = split(qkv_ref[PAIRS + p, rows, :])
-                news = (
-                    jnp.transpose(mm_tn(keys, jnp.concatenate(slopes, axis=0)))[:window] * SCORE_SCALE,
-                    mm(jnp.concatenate(slopes, axis=1), split(qkv_ref[p, wide, :])) * SCORE_SCALE,
-                    mm(jnp.concatenate(weights, axis=1), split(go[p, wide, :])),
-                )
-                for c in range(3):
-                    old = gqkv[c * PAIRS + p, rows, :].astype(F32)
-                    gqkv[c * PAIRS + p, rows, :] = jnp.where(inside, news[c], old).astype(BF16)
+                grad_scores[n % 4, r : r + 16, :span] = slope.astype(BF16)
+            if n in (2, 4):
+                finish(n // 2 - 1)
+        finish(PAIRS - 1)
 
     over_images(len_ref, tokens, attend)
 
-    w_q, w_k = unpack_weight(main_ref, 0, 0), unpack_weight(main_ref, 0, 1)
-    w_v = unpack_weight(main_ref, 1, 0)
-    w_qkv = jnp.concatenate([w_q, w_k, w_v], axis=1)
+    w_qkv = w_ref[:, : 3 * D]
     sums_one = (zero, zero)
     for t in range(5):
         rows = pl.ds(t * tile, tile)
@@ -783,8 +832,7 @@
             gain, bias = carry
             rows = pl.ds(at, count)
             grad_h1 = wide_rows[pl.ds(place(at), count), :]
-            normal, inverse = normed(patch_ref[rows, :].astype(F32))
-            h1_all[rows, :] = (normal * norms[0:1] + norms[1:2]).astype(BF16)
+            normal, inverse = normal_one[rows, :], thrice(inverse_one[rows, :])
             grad_x = gx1[rows, :] + norm_back(grad_h1, normal, inverse, norms[0:1])
             input_ref[rows, :] = grad_x.astype(BF16)
             return gain + fold_rows(grad_h1 * normal), bias + fold_rows(grad_h1)
@@ -800,8 +848,8 @@
     gw_ref[1, :, 6 * GROUP_ROWS :, :] = pack_turned(turned)
 
 
-def backward_local(lengths, patches, main, saved, result, gslots, experts):
-    tokens = patches.shape[0]
+def backward_local(lengths, first_norm, saved, result, gslots, block, experts):
+    tokens = first_norm[0].shape[0]
     columns = experts * SLOT_ROWS
     kept = tokens if experts <= 16 else tokens // 5
     shape = jax.ShapeDtypeStruct
@@ -809,11 +857,10 @@
         functools.partial(backward_kernel, experts),
         out_shape=(
             shape((tokens, D), BF16),
-            shape((tokens, D), BF16),
-            shape((2,) + (GROUPS,) + main.shape[2:], F32),
+            shape((2, GROUPS) + block, F32),
         ),
-        in_specs=[pl.BlockSpec(memory_space=pltpu.SMEM)] + whole(12),
-        out_specs=tuple(whole(3)),
+        in_specs=[pl.BlockSpec(memory_space=pltpu.SMEM)] + whole(17),
+        out_specs=tuple(whole(2)),
         scratch_shapes=[
             pltpu.VMEM((kept, columns), F32),
             pltpu.VMEM((tokens, columns), BF16),
@@ -821,21 +868,20 @@
             pltpu.VMEM((tokens, D), BF16),
             pltpu.VMEM((PAIRS, tokens + WINDOW_PAD, 128), BF16),
             pltpu.VMEM((9, tokens, 128), BF16),
-            pltpu.VMEM((tokens, D), BF16),
             pltpu.VMEM((2, LONG_WINDOW, LONG_SPAN), F32),
             pltpu.VMEM((2, LONG_WINDOW, LONG_SPAN), F32),
-            pltpu.VMEM((2, LONG_WINDOW, LONG_SPAN), BF16),
-            pltpu.VMEM((2, LONG_WINDOW, LONG_SPAN), BF16),
+            pltpu.VMEM((4, LONG_WINDOW, LONG_SPAN), BF16),
+            pltpu.VMEM((4, LONG_WINDOW, LONG_SPAN), BF16),
             pltpu.VMEM((128, LONG_SPAN), F32),
             pltpu.VMEM((kept, columns), F32),
             pltpu.VMEM((kept, D), F32),
         ],
-        compiler_params=pltpu.CompilerParams(vmem_limit_bytes=vmem_bytes(experts, 34)),
+        compiler_params=pltpu.CompilerParams(vmem_limit_bytes=vmem_bytes(experts, 28)),
         name="backward_local",
-    )(lengths, patches, main, *saved, result, gslots)
-
-
-def reduce_kernel(experts, gw_ref, square_ref, attn_out, phi_out, norm_out, total_ref, own, pair_in,
+    )(lengths, *first_norm, *saved, result, gslots)
+
+
+def reduce_kernel(experts, gw_ref, square_ref, x1_ref, comb_ref, result_ref, attn_out, phi_out, norm_out, total_ref, block_ref, own, pair_in,
                   box_one, in_one, box_two, in_two, box_z, in_z, final, scalars, load_sem, sent,
                   pair_recv, recv_one, recv_two, recv_z, swap_sem, norm_recv):
     core, chip, first, second = ring(experts)
@@ -902,6 +948,11 @@
             box_one[index] = total.astype(BF16)
             to_first(index).start()
 
+    tile = x1_ref.shape[0] // 5
+    for t in range(5):
+        part = pl.ds(t * tile, tile)
+        mixed = mm(comb_ref[part, :].astype(BF16), result_ref[...])
+        block_ref[part, :] = (x1_ref[part, :] + mixed).astype(BF16)
     pair_copy(two).wait_recv()
 
     @pl.loop(0, layers)
@@ -992,7 +1043,7 @@
     norms.wait_send()
 
 
-def reduce_grads(grads, squares, experts):
+def reduce_grads(grads, squares, x1, combine, result, experts):
     rows = D // experts
     layers = experts // 4
     block = grads.shape[2:]
@@ -1005,9 +1056,10 @@
             shape((experts, rows), F32),
             shape((4, rows), F32),
             shape((1, 128), F32),
+            shape(x1.shape, BF16),
         ),
-        in_specs=[pl.BlockSpec(memory_space=pl.ANY)] + whole(1),
-        out_specs=tuple(whole(4)),
+        in_specs=[pl.BlockSpec(memory_space=pl.ANY)] + whole(4),
+        out_specs=tuple(whole(5)),
         scratch_shapes=[
             pltpu.VMEM((layers, 4) + block, F32),
             pltpu.VMEM((layers, 4) + block, F32),
@@ -1029,10 +1081,10 @@
             dma((1,)),
         ],
         compiler_params=pltpu.CompilerParams(
-            collective_id=2, has_side_effects=True, vmem_limit_bytes=vmem_bytes(experts, 8)
+            collective_id=2, has_side_effects=True, vmem_limit_bytes=vmem_bytes(experts, 16)
         ),
         name="reduce_grads",
-    )(grads.reshape((2, layers, 4) + block), squares)
+    )(grads.reshape((2, layers, 4) + block), squares, x1, combine, result)
 
 
 def adam_update(weight, first_moment, second_moment, gradient, factor, learning_rate, decay_rate):
@@ -1057,40 +1109,52 @@
 UPDATE_STEPS = 4
 
 
-def update_kernel(norm_ref, *refs):
+def update_kernel(block_ref, norm_ref, *refs):
+    inputs, block_out, outputs, news, sems = refs[:20], refs[20], refs[21:36], refs[36:51], refs[51]
     grad_norm = norm_ref[...]
-    factor = CLIP_NORM / jnp.maximum(grad_norm, CLIP_NORM)
-    factor = factor[0:1, 0:1]
-    inputs, outputs = refs[:20], refs[20:]
-    for k, (rate, decay) in enumerate(RATES):
+    factor = (CLIP_NORM / jnp.maximum(grad_norm, CLIP_NORM))[0:1, 0:1]
+    copies = []
+
+    def start(source, target):
+        copies.append(pltpu.make_async_copy(source, target, sems.at[len(copies)]))
+        copies[-1].start()
+
+    for t in range(UPDATE_STEPS):
+        for k in (3, 4):
+            rate, decay = RATES[k]
+            rows = inputs[4 * k].shape[1] // UPDATE_STEPS
+            part = (0, pl.ds(t * rows, rows))
+            weight, first, second, grad = (ref[part] for ref in inputs[4 * k : 4 * k + 4])
+            made = adam_update(weight, first, second, grad, factor, rate, decay)
+            for c in range(3):
+                news[3 * k + c][part] = made[c]
+                start(news[3 * k + c].at[part], outputs[3 * k + c].at[part])
+        if t == 0:
+            start(block_ref, block_out)
+    for k in range(3):
+        rate, decay = RATES[k]
         weight, first, second, grad = (ref[...] for ref in inputs[4 * k : 4 * k + 4])
-        by = factor.reshape((1,) * grad.ndim)
-        news = adam_update(weight, first, second, grad, by, rate, decay)
-        for ref, new in zip(outputs[3 * k : 3 * k + 3], news):
-            ref[...] = new
-
-
-def update(norm_tile, groups):
-    def spec(k, shape):
-        if k == 0:
-            return pl.BlockSpec((shape[0], shape[1] // UPDATE_STEPS), lambda i: (0, i))
-        if k < 3:
-            return pl.BlockSpec(shape, lambda i: (0, 0))
-        return pl.BlockSpec((1, shape[1] // UPDATE_STEPS, shape[2]), lambda i: (0, i, 0))
-
-    specs = [spec(k, group[0].shape) for k, group in enumerate(groups)]
+        made = adam_update(weight, first, second, grad, factor, rate, decay)
+        for c in range(3):
+            news[3 * k + c][...] = made[c]
+            start(news[3 * k + c], outputs[3 * k + c])
+    for copy in copies:
+        copy.wait()
+
+
+def update(block_output, norm_tile, groups):
+    shapes = [group[0].shape for group in groups for _ in range(3)]
+    block_shape = jax.ShapeDtypeStruct(block_output.shape, BF16)
     return pl.pallas_call(
         update_kernel,
-        grid=(UPDATE_STEPS,),
-        out_shape=tuple(
-            jax.ShapeDtypeStruct(group[0].shape, F32) for group in groups for _ in range(3)
-        ),
-        in_specs=[pl.BlockSpec((1, 128), lambda i: (0, 0))]
-        + [one for one in specs for _ in range(4)],
-        out_specs=tuple(one for one in specs for _ in range(3)),
+        out_shape=(block_shape,) + tuple(jax.ShapeDtypeStruct(shape, F32) for shape in shapes),
+        in_specs=whole(22),
+        out_specs=(pl.BlockSpec(memory_space=pl.ANY),) * 16,
+        scratch_shapes=[pltpu.VMEM(shape, F32) for shape in shapes]
+        + [pltpu.SemaphoreType.DMA((10 + 6 * UPDATE_STEPS,))],
         compiler_params=pltpu.CompilerParams(vmem_limit_bytes=24 * 1024 * 1024),
         name="update",
-    )(norm_tile, *[array for group in groups for array in group])
+    )(block_output, norm_tile, *[array for group in groups for array in group])
 
 
 def in_hbm(array):
@@ -1152,20 +1216,24 @@
     cotangent,
 ):
     experts = lax.axis_size("expert")
-    weights = gather_weights(
-        in_hbm(attn_weight), in_hbm(phi_weight.T), in_hbm(norm_params), experts
+    weights, *first_norm = gather_weights(
+        in_hbm(attn_weight), in_hbm(phi_weight.T), in_hbm(norm_params), in_hbm(patches), experts
     )
     weights = regroup_weights(weights, experts)
     *saved, packed = forward_local(
-        slot_len, patches, weights, in_hbm(cotangent), experts
+        slot_len, patches, weights, first_norm[0], in_hbm(cotangent), experts
     )
+    x1, combine = saved.pop(9), saved[11]
     result, gslots, grad_in, grad_out, squares = run_experts(packed, expert_in, expert_out, experts)
-    block_output, input_grad, grads = backward_local(
-        slot_len, patches, weights, saved, result, gslots, experts
+    input_grad, grads = backward_local(
+        slot_len, first_norm, saved, result, gslots, weights.shape[2:], experts
     )
     grads = regroup_grads(grads, experts)
-    attn_part, phi_part, norm_part, norm_tile = reduce_grads(grads, squares, experts)
-    news = update(
+    attn_part, phi_part, norm_part, norm_tile, block_output = reduce_grads(
+        grads, squares, x1, combine, result, experts
+    )
+    block_output, *news = update(
+        block_output,
         norm_tile,
         (
             (attn_weight, attn_first, attn_second, attn_part),

time: 98.6 us -> 96.2 us (0.976)
  Pallas kernels: 96.5 us -> 93.9 us
    pallas_call x1, Pallas kernels: 21.8 us -> 14.9 us  [backward_local(): pl.pallas_call(functools.partial(backward_kernel, experts), out_shape=(sh...]
    pallas_call x1, Pallas kernels: 21.4 us -> 25.9 us  [reduce_grads(): pl.pallas_call(functools.partial(reduce_kernel, experts), out_shape=(shap...]
    pallas_call x1, Pallas kernels: 13.1 us -> 10.3 us  [forward_local(): pl.pallas_call(functools.partial(forward_kernel, experts), out_shape=(sha...]
    pallas_call x1, Pallas kernels: 17 us -> 19.7 us  [run_experts(): pl.pallas_call(functools.partial(expert_kernel, experts), out_shape=(shap...]
where the time goes in v5:
time: 96.2 us; the launch traced here: 96.1 us
  Pallas kernels  93.9 us (98%)
  between operations  2.13 us (2%)
    pallas_call x1, Pallas kernels, reduce_grads(): pl.pallas_call(functools.partial(reduce_kernel, experts), out_shape=(shap...  25.9 us
    pallas_call x1, Pallas kernels, run_experts(): pl.pallas_call(functools.partial(expert_kernel, experts), out_shape=(shap...  19.7 us
    pallas_call x1, Pallas kernels, gather_weights(): pl.pallas_call(functools.partial(gather_kernel, experts), out_shape=(jax....  18.6 us
    pallas_call x1, Pallas kernels, backward_local(): pl.pallas_call(functools.partial(backward_kernel, experts), out_shape=(sh...  14.9 us
    pallas_call x1, Pallas kernels, forward_local(): pl.pallas_call(functools.partial(forward_kernel, experts), out_shape=(sha...  10.3 us
    pallas_call x1, Pallas kernels, update(): pl.pallas_call(update_kernel, out_shape=(block_shape,) + tuple((jax.Shape...  4.44 us

profile of v5, /device:TPU:0, one launch (start us, length us, event | category | flops | bytes accessed | tf_op | source)
XLA Modules:
  0.0 96.1 jit_solution(448222593710541583)
XLA Ops:
  0.7 0.0 copy-start.14
  0.7 0.0 copy-start.2
  0.7 18.6 %gather_weights.1 = (bf16[16,2,160,128]{3,2,1,0:T(8,128)(2,1)S(1)}, f32[1360,384]{1,0:T(8,128)S(1)}, f32[1360,128]{1,0:T(8,128)S(1)}) custom-call(f32[24,1536]{1,0:T(8,128)} %refs_0_.1, f32[16,24]{1,0:T(8,128)} %bitcast.10, f32[4,24]{1,0:T(4,128)} %refs_8_.1, bf16[1360,384]{1,0:T(8,128)(2,1)} %patch_ref.1), custom_call_target="tpu_custom_call" | custom-call | tf_op jit(solution)/shard_map/gather_weights/pallas_call | solution.py:194
  19.2 0.0 copy-done.14
  19.3 0.0 copy-done.2
  19.3 0.0 copy-start
  19.3 0.0 copy-start.1
  19.3 10.3 %forward_local.1 = (bf16[384,1536]{1,0:T(8,128)(2,1)S(1)}, bf16[128,384]{1,0:T(8,128)(2,1)S(1)}, f32[8,384]{1,0:T(8,128)S(1)}, f32[1360,384]{1,0:T(8,128)S(1)}, ...) custom-call(s32[1,5]{1,0:T(1,128)S(1)} %copy-done.14, ...), custom_call_target="tpu_custom_call" | custom-call | tf_op jit(solution)/shard_map/forward_local/pallas_call | solution.py:480
  29.6 0.0 copy-done
  29.6 0.0 copy-done.1
  29.7 19.7 %run_experts.1 = (bf16[128,384]{1,0:T(8,128)(2,1)S(1)}, bf16[128,384]{1,0:T(8,128)(2,1)S(1)}, f32[1,384,768]{2,1,0:T(8,128)S(1)}, f32[1,768,384]{2,1,0:T(8,128)S(1)}, f32[1,128]{1,0:T(1,128)S(1)}) custom-call(bf16[16,32,128]{2,1,0:T(8,128)(2,1)S(1)} %get-tuple-element.80.pack_ref, f32[1,384,768]{2,1,0:T(8,128)S(1)} %copy-done, f32[1,768,384]{2,1,0:T(8,128)S(1)} %copy-done.1), custom_call_target="tpu_custom_call" | custom-call | tf_op jit(solution)/shard_map/run_experts/pallas_call | solution.py:642
  49.4 14.9 %backward_local.1 = (bf16[1360,384]{1,0:T(8,128)(2,1)}, f32[2,16,160,128]{3,2,1,0:T(8,128)S(1)}) custom-call(s32[1,5]{1,0:T(1,128)S(1)} %copy-done.14, f32[1360,384]{1,0:T(8,128)S(1)} %get-tuple-element.64.norm_ref.normal_one, f32[1360,128]{1,0:T(8,128)S(1)} %get-tuple-element.65.inverse_one, bf16[384,1536]{1,0:T(8,128)(2,1)S(1)} %get-tuple-element.67.w_ref, ...), custom_call_target="tpu_custom_call" | custom-call | tf_op jit(solution)/shard_map/backward_local/pallas_call | solution.py:856
  64.3 0.0 copy-start.3
  64.3 0.0 copy-start.4
  64.4 0.0 copy-start.5
  64.4 0.0 copy-start.6
  64.4 0.0 copy-start.7
  64.4 0.0 copy-start.8
  64.4 0.0 copy-start.9
  64.4 0.0 copy-start.10
  64.4 0.0 copy-start.11
  64.4 0.0 copy-start.12
  64.5 0.0 copy-start.13
  64.5 0.0 copy-start.15
  64.5 0.0 copy-start.16
  64.5 25.9 %reduce_grads.1 = (f32[24,1536]{1,0:T(8,128)S(1)}, f32[16,24]{1,0:T(8,128)S(1)}, f32[4,24]{1,0:T(4,128)S(1)}, f32[1,128]{1,0:T(1,128)S(1)}, bf16[1360,384]{1,0:T(8,128)(2,1)S(1)}) custom-call(f32[2,4,4,160,128]{4,3,2,1,0:T(8,128)S(1)} %bitcast.9, f32[1,128]{1,0:T(1,128)S(1)} %get-tuple-element.84.square_ref, f32[1360,384]{1,0:T(8,128)S(1)} %get-tuple-element.85.x1_ref, ...), custom_call_target="tpu_custom_call" | custom-call | tf_op jit(solution)/shard_map/reduce_grads/pallas_call | solution.py:1052
  90.4 0.0 copy-done.3
  90.4 0.0 copy-done.4
  90.4 0.0 copy-done.5
  90.4 0.0 copy-done.6
  90.4 0.0 copy-done.7
  90.4 0.0 copy-done.8
  90.5 0.0 copy-done.9
  90.5 0.0 copy-done.10
  90.5 0.0 copy-done.11
  90.5 0.0 copy-done.12
  90.5 0.0 copy-done.13
  90.5 0.0 copy-done.15
  90.5 0.0 copy-done.16
  90.5 4.4 %update.1 = (bf16[1360,384]{1,0:T(8,128)(2,1)}, f32[24,1536]{1,0:T(8,128)}, f32[24,1536]{1,0:T(8,128)}, f32[24,1536]{1,0:T(8,128)}, f32[16,24]{1,0:T(8,128)}, /*...) custom-call(bf16[1360,384]{1,0:T(8,128)(2,1)S(1)} %get-tuple-element, ...), custom_call_target="tpu_custom_call" | custom-call | tf_op jit(solution)/shard_map/update/pallas_call | solution.py:1148
Async XLA Ops:
  0.7 18.6 %copy-start.14 = (s32[1,5]{1,0:T(1,128)S(1)}, s32[1,5]{1,0:T(1,128)}, u32[]{:S(2)}) copy-start(s32[1,5]{1,0:T(1,128)} %len_ref.3) | copy-start | bytes 64
  0.7 18.6 %copy-start.2 = (bf16[1360,384]{1,0:T(8,128)(2,1)S(1)}, bf16[1360,384]{1,0:T(8,128)(2,1)}, u32[]{:S(2)}) copy-start(bf16[1360,384]{1,0:T(8,128)(2,1)} %patch_ref.1) | copy-start | bytes 3133444
  19.3 10.4 %copy-start = (f32[1,384,768]{2,1,0:T(8,128)S(1)}, f32[1,384,768]{2,1,0:T(8,128)}, u32[]{:S(2)}) copy-start(f32[1,384,768]{2,1,0:T(8,128)} %refs_12_.1) | copy-start | bytes 3538948
  19.3 10.4 %copy-start.1 = (f32[1,768,384]{2,1,0:T(8,128)S(1)}, f32[1,768,384]{2,1,0:T(8,128)}, u32[]{:S(2)}) copy-start(f32[1,768,384]{2,1,0:T(8,128)} %refs_16_.1) | copy-start | bytes 3538948
  64.3 26.1 %copy-start.3 = (f32[1,384,768]{2,1,0:T(8,128)S(1)}, f32[1,384,768]{2,1,0:T(8,128)}, u32[]{:S(2)}) copy-start(f32[1,384,768]{2,1,0:T(8,128)} %refs_13_.1) | copy-start | bytes 3538948
  64.3 26.1 %copy-start.4 = (f32[1,384,768]{2,1,0:T(8,128)S(1)}, f32[1,384,768]{2,1,0:T(8,128)}, u32[]{:S(2)}) copy-start(f32[1,384,768]{2,1,0:T(8,128)} %refs_14_.1) | copy-start | bytes 3538948
  64.4 26.1 %copy-start.5 = (f32[1,768,384]{2,1,0:T(8,128)S(1)}, f32[1,768,384]{2,1,0:T(8,128)}, u32[]{:S(2)}) copy-start(f32[1,768,384]{2,1,0:T(8,128)} %refs_17_.1) | copy-start | bytes 3538948
  64.4 26.1 %copy-start.6 = (f32[1,768,384]{2,1,0:T(8,128)S(1)}, f32[1,768,384]{2,1,0:T(8,128)}, u32[]{:S(2)}) copy-start(f32[1,768,384]{2,1,0:T(8,128)} %refs_18_.1) | copy-start | bytes 3538948
  64.4 26.1 %copy-start.7 = (f32[24,1536]{1,0:T(8,128)S(1)}, f32[24,1536]{1,0:T(8,128)}, u32[]{:S(2)}) copy-start(f32[24,1536]{1,0:T(8,128)} %refs_0_.1) | copy-start | bytes 442372
  64.4 26.1 %copy-start.8 = (f32[24,1536]{1,0:T(8,128)S(1)}, f32[24,1536]{1,0:T(8,128)}, u32[]{:S(2)}) copy-start(f32[24,1536]{1,0:T(8,128)} %refs_1_.1) | copy-start | bytes 442372
  64.4 26.1 %copy-start.9 = (f32[24,1536]{1,0:T(8,128)S(1)}, f32[24,1536]{1,0:T(8,128)}, u32[]{:S(2)}) copy-start(f32[24,1536]{1,0:T(8,128)} %refs_2_.1) | copy-start | bytes 442372
  64.4 26.1 %copy-start.10 = (f32[24,16]{0,1:T(8,128)S(1)}, f32[24,16]{0,1:T(8,128)}, u32[]{:S(2)}) copy-start(f32[24,16]{0,1:T(8,128)} %param.23) | copy-start | bytes 4612
  64.4 26.1 %copy-start.11 = (f32[24,16]{0,1:T(8,128)S(1)}, f32[24,16]{0,1:T(8,128)}, u32[]{:S(2)}) copy-start(f32[24,16]{0,1:T(8,128)} %param.24) | copy-start | bytes 4612
  64.4 26.0 %copy-start.12 = (f32[24,16]{0,1:T(8,128)S(1)}, f32[24,16]{0,1:T(8,128)}, u32[]{:S(2)}) copy-start(f32[24,16]{0,1:T(8,128)} %param.25) | copy-start | bytes 4612
  64.5 26.0 %copy-start.13 = (f32[4,24]{1,0:T(4,128)S(1)}, f32[4,24]{1,0:T(4,128)}, u32[]{:S(2)}) copy-start(f32[4,24]{1,0:T(4,128)} %refs_8_.1) | copy-start | bytes 1156
  64.5 26.0 %copy-start.15 = (f32[4,24]{1,0:T(4,128)S(1)}, f32[4,24]{1,0:T(4,128)}, u32[]{:S(2)}) copy-start(f32[4,24]{1,0:T(4,128)} %refs_9_.1) | copy-start | bytes 1156
  64.5 26.0 %copy-start.16 = (f32[4,24]{1,0:T(4,128)S(1)}, f32[4,24]{1,0:T(4,128)}, u32[]{:S(2)}) copy-start(f32[4,24]{1,0:T(4,128)} %refs_10_.1) | copy-start | bytes 1156

commit v6 on v5

--- a/solution.py
+++ b/solution.py
@@ -350,8 +350,8 @@
         h1_all[rows, :] = (norm_ref[rows, :] * norms[0:1] + norms[1:2]).astype(BF16)
         return carry
 
-    over_rows(0, tokens, 0, first_norm)
     for t in range(5):
+        over_rows(t * tile, (t + 1) * tile, 0, first_norm)
         rows = pl.ds(t * tile, tile)
         qkv = mm(h1_all[rows, :], w_qkv).astype(BF16)
         for c in range(9):
@@ -405,7 +405,7 @@
 
     load.wait()
     w_o = w_ref[:, 3 * D :]
-    for t in range(5):
+    def project(t):
         rows = pl.ds(t * tile, tile)
         x1_ref[rows, :] = mm(o_ref[rows, :], w_o)
 
@@ -421,8 +421,13 @@
         gy_ref[rows, :] = jnp.where(valid, cot_ref[rows, :].astype(F32), 0.0).astype(BF16)
         return carry
 
-    over_rows(0, tokens, 0, second_norm)
-    logit[...] = mm_nt(h2_ref[...], phi)
+    project(0)
+    for t in range(5):
+        if t < 4:
+            project(t + 1)
+        over_rows(t * tile, (t + 1) * tile, 0, second_norm)
+        rows = pl.ds(t * tile, tile)
+        logit[rows, :] = mm_nt(h2_ref[rows, :], phi)
 
     def members(at, count):
         position = at + lax.broadcasted_iota(jnp.int32, (count, columns), 0)
@@ -729,13 +734,15 @@
         return gain + fold_rows(grad_h2 * normal), bias + fold_rows(grad_h2)
 
     zero = jnp.zeros((8, D), F32)
-    gain_two, bias_two = over_rows(0, tokens, (zero, zero), second_norm)
     w_o = w_ref[:, 3 * D :]
+    sums_two = (zero, zero)
     for t in range(5):
+        sums_two = over_rows(t * tile, (t + 1) * tile, sums_two, second_norm)
         rows = pl.ds(t * tile, tile)
         grad_o = mm_nt(branch[rows, :], w_o).astype(BF16)
         for c in range(PAIRS):
             go[c, rows, :] = grad_o[:, c * 128 : (c + 1) * 128]
+    gain_two, bias_two = sums_two
 
     small_rows = gw_ref.shape[2] - 6 * GROUP_ROWS
     row = lax.broadcasted_iota(jnp.int32, (columns, small_rows), 0)

time: 96.2 us -> 96.4 us (level)
    pallas_call x1, Pallas kernels: 14.9 us -> 18.7 us  [backward_local(): pl.pallas_call(functools.partial(backward_kernel, experts), out_shape=(sh...]
    pallas_call x1, Pallas kernels: 25.9 us -> 22.9 us  [reduce_grads(): pl.pallas_call(functools.partial(reduce_kernel, experts), out_shape=(shap...]
    pallas_call x1, Pallas kernels: 19.7 us -> 17.6 us  [run_experts(): pl.pallas_call(functools.partial(expert_kernel, experts), out_shape=(shap...]
    pallas_call x1, Pallas kernels: 10.3 us -> 12 us  [forward_local(): pl.pallas_call(functools.partial(forward_kernel, experts), out_shape=(sha...]
where the time goes in v6:
time: 96.4 us
  Pallas kernels  94.1 us (98%)
  between operations  2.13 us (2%)
    pallas_call x1, Pallas kernels, reduce_grads(): pl.pallas_call(functools.partial(reduce_kernel, experts), out_shape=(shap...  22.9 us
    pallas_call x1, Pallas kernels, backward_local(): pl.pallas_call(functools.partial(backward_kernel, experts), out_shape=(sh...  18.7 us
    pallas_call x1, Pallas kernels, gather_weights(): pl.pallas_call(functools.partial(gather_kernel, experts), out_shape=(jax....  18.6 us
    pallas_call x1, Pallas kernels, run_experts(): pl.pallas_call(functools.partial(expert_kernel, experts), out_shape=(shap...  17.6 us
    pallas_call x1, Pallas kernels, forward_local(): pl.pallas_call(functools.partial(forward_kernel, experts), out_shape=(sha...  12 us
    pallas_call x1, Pallas kernels, update(): pl.pallas_call(update_kernel, out_shape=(block_shape,) + tuple((jax.Shape...  4.44 us

profile of v6, /device:TPU:0, one launch (start us, length us, event | category | flops | bytes accessed | tf_op | source)
XLA Modules:
  0.0 96.4 jit_solution(6779396215814936705)
XLA Ops:
  0.7 0.0 copy-start.14
  0.7 0.0 copy-start.2
  0.7 18.6 %gather_weights.1 = (bf16[16,2,160,128]{3,2,1,0:T(8,128)(2,1)S(1)}, f32[1360,384]{1,0:T(8,128)S(1)}, f32[1360,128]{1,0:T(8,128)S(1)}) custom-call(f32[24,1536]{1,0:T(8,128)} %refs_0_.1, f32[16,24]{1,0:T(8,128)} %bitcast.10, f32[4,24]{1,0:T(4,128)} %refs_8_.1, bf16[1360,384]{1,0:T(8,128)(2,1)} %patch_ref.1), custom_call_target="tpu_custom_call" | custom-call | tf_op jit(solution)/shard_map/gather_weights/pallas_call | solution.py:194
  19.2 0.0 copy-done.14
  19.3 0.0 copy-done.2
  19.3 0.0 copy-start
  19.3 0.0 copy-start.1
  19.3 12.0 %forward_local.1 = (bf16[384,1536]{1,0:T(8,128)(2,1)S(1)}, bf16[128,384]{1,0:T(8,128)(2,1)S(1)}, f32[8,384]{1,0:T(8,128)S(1)}, f32[1360,384]{1,0:T(8,128)S(1)}, ...) custom-call(s32[1,5]{1,0:T(1,128)S(1)} %copy-done.14, ...), custom_call_target="tpu_custom_call" | custom-call | tf_op jit(solution)/shard_map/forward_local/pallas_call | solution.py:485
  31.3 0.0 copy-done
  31.3 0.0 copy-done.1
  31.3 17.6 %run_experts.1 = (bf16[128,384]{1,0:T(8,128)(2,1)S(1)}, bf16[128,384]{1,0:T(8,128)(2,1)S(1)}, f32[1,384,768]{2,1,0:T(8,128)S(1)}, f32[1,768,384]{2,1,0:T(8,128)S(1)}, f32[1,128]{1,0:T(1,128)S(1)}) custom-call(bf16[16,32,128]{2,1,0:T(8,128)(2,1)S(1)} %get-tuple-element.80.pack_ref, f32[1,384,768]{2,1,0:T(8,128)S(1)} %copy-done, f32[1,768,384]{2,1,0:T(8,128)S(1)} %copy-done.1), custom_call_target="tpu_custom_call" | custom-call | tf_op jit(solution)/shard_map/run_experts/pallas_call | solution.py:647
  48.9 18.7 %backward_local.1 = (bf16[1360,384]{1,0:T(8,128)(2,1)}, f32[2,16,160,128]{3,2,1,0:T(8,128)S(1)}) custom-call(s32[1,5]{1,0:T(1,128)S(1)} %copy-done.14, f32[1360,384]{1,0:T(8,128)S(1)} %get-tuple-element.64.norm_ref.normal_one, f32[1360,128]{1,0:T(8,128)S(1)} %get-tuple-element.65.inverse_one, bf16[384,1536]{1,0:T(8,128)(2,1)S(1)} %get-tuple-element.67.w_ref, ...), custom_call_target="tpu_custom_call" | custom-call | tf_op jit(solution)/shard_map/backward_local/pallas_call | solution.py:863
  67.6 0.0 copy-start.3
  67.6 0.0 copy-start.4
  67.6 0.0 copy-start.5
  67.6 0.0 copy-start.6
  67.7 0.0 copy-start.7
  67.7 0.0 copy-start.8
  67.7 0.0 copy-start.9
  67.7 0.0 copy-start.10
  67.7 0.0 copy-start.11
  67.7 0.0 copy-start.12
  67.7 0.0 copy-start.13
  67.7 0.0 copy-start.15
  67.8 0.0 copy-start.16
  67.8 22.9 %reduce_grads.1 = (f32[24,1536]{1,0:T(8,128)S(1)}, f32[16,24]{1,0:T(8,128)S(1)}, f32[4,24]{1,0:T(4,128)S(1)}, f32[1,128]{1,0:T(1,128)S(1)}, bf16[1360,384]{1,0:T(8,128)(2,1)S(1)}) custom-call(f32[2,4,4,160,128]{4,3,2,1,0:T(8,128)S(1)} %bitcast.9, f32[1,128]{1,0:T(1,128)S(1)} %get-tuple-element.84.square_ref, f32[1360,384]{1,0:T(8,128)S(1)} %get-tuple-element.85.x1_ref, ...), custom_call_target="tpu_custom_call" | custom-call | tf_op jit(solution)/shard_map/reduce_grads/pallas_call | solution.py:1059
  90.6 0.0 copy-done.3
  90.7 0.0 copy-done.4
  90.7 0.0 copy-done.5
  90.7 0.0 copy-done.6
  90.7 0.0 copy-done.7
  90.7 0.0 copy-done.8
  90.7 0.0 copy-done.9
  90.7 0.0 copy-done.10
  90.7 0.0 copy-done.11
  90.7 0.0 copy-done.12
  90.7 0.0 copy-done.13
  90.8 0.0 copy-done.15
  90.8 0.0 copy-done.16
  90.8 4.4 %update.1 = (bf16[1360,384]{1,0:T(8,128)(2,1)}, f32[24,1536]{1,0:T(8,128)}, f32[24,1536]{1,0:T(8,128)}, f32[24,1536]{1,0:T(8,128)}, f32[16,24]{1,0:T(8,128)}, /*...) custom-call(bf16[1360,384]{1,0:T(8,128)(2,1)S(1)} %get-tuple-element, ...), custom_call_target="tpu_custom_call" | custom-call | tf_op jit(solution)/shard_map/update/pallas_call | solution.py:1155
Async XLA Ops:
  0.7 18.6 %copy-start.14 = (s32[1,5]{1,0:T(1,128)S(1)}, s32[1,5]{1,0:T(1,128)}, u32[]{:S(2)}) copy-start(s32[1,5]{1,0:T(1,128)} %len_ref.3) | copy-start | bytes 64
  0.7 18.6 %copy-start.2 = (bf16[1360,384]{1,0:T(8,128)(2,1)S(1)}, bf16[1360,384]{1,0:T(8,128)(2,1)}, u32[]{:S(2)}) copy-start(bf16[1360,384]{1,0:T(8,128)(2,1)} %patch_ref.1) | copy-start | bytes 3133444
  19.3 12.0 %copy-start = (f32[1,384,768]{2,1,0:T(8,128)S(1)}, f32[1,384,768]{2,1,0:T(8,128)}, u32[]{:S(2)}) copy-start(f32[1,384,768]{2,1,0:T(8,128)} %refs_12_.1) | copy-start | bytes 3538948
  19.3 12.0 %copy-start.1 = (f32[1,768,384]{2,1,0:T(8,128)S(1)}, f32[1,768,384]{2,1,0:T(8,128)}, u32[]{:S(2)}) copy-start(f32[1,768,384]{2,1,0:T(8,128)} %refs_16_.1) | copy-start | bytes 3538948
  67.6 23.0 %copy-start.3 = (f32[1,384,768]{2,1,0:T(8,128)S(1)}, f32[1,384,768]{2,1,0:T(8,128)}, u32[]{:S(2)}) copy-start(f32[1,384,768]{2,1,0:T(8,128)} %refs_13_.1) | copy-start | bytes 3538948
  67.6 23.0 %copy-start.4 = (f32[1,384,768]{2,1,0:T(8,128)S(1)}, f32[1,384,768]{2,1,0:T(8,128)}, u32[]{:S(2)}) copy-start(f32[1,384,768]{2,1,0:T(8,128)} %refs_14_.1) | copy-start | bytes 3538948
  67.6 23.0 %copy-start.5 = (f32[1,768,384]{2,1,0:T(8,128)S(1)}, f32[1,768,384]{2,1,0:T(8,128)}, u32[]{:S(2)}) copy-start(f32[1,768,384]{2,1,0:T(8,128)} %refs_17_.1) | copy-start | bytes 3538948
  67.6 23.0 %copy-start.6 = (f32[1,768,384]{2,1,0:T(8,128)S(1)}, f32[1,768,384]{2,1,0:T(8,128)}, u32[]{:S(2)}) copy-start(f32[1,768,384]{2,1,0:T(8,128)} %refs_18_.1) | copy-start | bytes 3538948
  67.7 23.0 %copy-start.7 = (f32[24,1536]{1,0:T(8,128)S(1)}, f32[24,1536]{1,0:T(8,128)}, u32[]{:S(2)}) copy-start(f32[24,1536]{1,0:T(8,128)} %refs_0_.1) | copy-start | bytes 442372
  67.7 23.0 %copy-start.8 = (f32[24,1536]{1,0:T(8,128)S(1)}, f32[24,1536]{1,0:T(8,128)}, u32[]{:S(2)}) copy-start(f32[24,1536]{1,0:T(8,128)} %refs_1_.1) | copy-start | bytes 442372
  67.7 23.0 %copy-start.9 = (f32[24,1536]{1,0:T(8,128)S(1)}, f32[24,1536]{1,0:T(8,128)}, u32[]{:S(2)}) copy-start(f32[24,1536]{1,0:T(8,128)} %refs_2_.1) | copy-start | bytes 442372
  67.7 23.0 %copy-start.10 = (f32[24,16]{0,1:T(8,128)S(1)}, f32[24,16]{0,1:T(8,128)}, u32[]{:S(2)}) copy-start(f32[24,16]{0,1:T(8,128)} %param.23) | copy-start | bytes 4612
  67.7 23.0 %copy-start.11 = (f32[24,16]{0,1:T(8,128)S(1)}, f32[24,16]{0,1:T(8,128)}, u32[]{:S(2)}) copy-start(f32[24,16]{0,1:T(8,128)} %param.24) | copy-start | bytes 4612
  67.7 23.0 %copy-start.12 = (f32[24,16]{0,1:T(8,128)S(1)}, f32[24,16]{0,1:T(8,128)}, u32[]{:S(2)}) copy-start(f32[24,16]{0,1:T(8,128)} %param.25) | copy-start | bytes 4612
  67.7 23.0 %copy-start.13 = (f32[4,24]{1,0:T(4,128)S(1)}, f32[4,24]{1,0:T(4,128)}, u32[]{:S(2)}) copy-start(f32[4,24]{1,0:T(4,128)} %refs_8_.1) | copy-start | bytes 1156
  67.7 23.0 %copy-start.15 = (f32[4,24]{1,0:T(4,128)S(1)}, f32[4,24]{1,0:T(4,128)}, u32[]{:S(2)}) copy-start(f32[4,24]{1,0:T(4,128)} %refs_9_.1) | copy-start | bytes 1156
  67.8 23.0 %copy-start.16 = (f32[4,24]{1,0:T(4,128)S(1)}, f32[4,24]{1,0:T(4,128)}, u32[]{:S(2)}) copy-start(f32[4,24]{1,0:T(4,128)} %refs_10_.1) | copy-start | bytes 1156

commit v7 on v6

--- a/solution.py
+++ b/solution.py
@@ -1113,7 +1113,7 @@
     (4.0 / math.sqrt(D), WEIGHT_DECAY),
     (8.0 / math.sqrt(FF), WEIGHT_DECAY),
 )
-UPDATE_STEPS = 4
+UPDATE_STEPS = 8
 
 
 def update_kernel(block_ref, norm_ref, *refs):
@@ -1126,6 +1126,7 @@
         copies.append(pltpu.make_async_copy(source, target, sems.at[len(copies)]))
         copies[-1].start()
 
+    start(block_ref, block_out)
     for t in range(UPDATE_STEPS):
         for k in (3, 4):
             rate, decay = RATES[k]
@@ -1136,8 +1137,6 @@
             for c in range(3):
                 news[3 * k + c][part] = made[c]
                 start(news[3 * k + c].at[part], outputs[3 * k + c].at[part])
-        if t == 0:
-            start(block_ref, block_out)
     for k in range(3):
         rate, decay = RATES[k]
         weight, first, second, grad = (ref[...] for ref in inputs[4 * k : 4 * k + 4])

time: 96.4 us -> 96.2 us (level)
    pallas_call x1, Pallas kernels: 17.6 us -> 19 us  [run_experts(): pl.pallas_call(functools.partial(expert_kernel, experts), out_shape=(shap...]
    pallas_call x1, Pallas kernels: 18.7 us -> 17.5 us  [backward_local(): pl.pallas_call(functools.partial(backward_kernel, experts), out_shape=(sh...]
where the time goes in v7:
time: 96.2 us; the launch traced here: 95.9 us
  Pallas kernels  93.7 us (97%)
  between operations  2.13 us (2%)
    pallas_call x1, Pallas kernels, reduce_grads(): pl.pallas_call(functools.partial(reduce_kernel, experts), out_shape=(shap...  23.3 us
    pallas_call x1, Pallas kernels, run_experts(): pl.pallas_call(functools.partial(expert_kernel, experts), out_shape=(shap...  19 us
    pallas_call x1, Pallas kernels, gather_weights(): pl.pallas_call(functools.partial(gather_kernel, experts), out_shape=(jax....  18.6 us
    pallas_call x1, Pallas kernels, backward_local(): pl.pallas_call(functools.partial(backward_kernel, experts), out_shape=(sh...  17.5 us
    pallas_call x1, Pallas kernels, forward_local(): pl.pallas_call(functools.partial(forward_kernel, experts), out_shape=(sha...  11.2 us
    pallas_call x1, Pallas kernels, update(): pl.pallas_call(update_kernel, out_shape=(block_shape,) + tuple((jax.Shape...  4.09 us

profile of v7, /device:TPU:0, one launch (start us, length us, event | category | flops | bytes accessed | tf_op | source)
XLA Modules:
  0.0 95.9 jit_solution(7743374812589660912)
XLA Ops:
  0.7 0.0 copy-start.14
  0.7 0.0 copy-start.2
  0.7 18.6 %gather_weights.1 = (bf16[16,2,160,128]{3,2,1,0:T(8,128)(2,1)S(1)}, f32[1360,384]{1,0:T(8,128)S(1)}, f32[1360,128]{1,0:T(8,128)S(1)}) custom-call(f32[24,1536]{1,0:T(8,128)} %refs_0_.1, f32[16,24]{1,0:T(8,128)} %bitcast.10, f32[4,24]{1,0:T(4,128)} %refs_8_.1, bf16[1360,384]{1,0:T(8,128)(2,1)} %patch_ref.1), custom_call_target="tpu_custom_call" | custom-call | tf_op jit(solution)/shard_map/gather_weights/pallas_call | solution.py:194
  19.2 0.0 copy-done.14
  19.3 0.0 copy-done.2
  19.3 0.0 copy-start
  19.3 0.0 copy-start.1
  19.3 11.2 %forward_local.1 = (bf16[384,1536]{1,0:T(8,128)(2,1)S(1)}, bf16[128,384]{1,0:T(8,128)(2,1)S(1)}, f32[8,384]{1,0:T(8,128)S(1)}, f32[1360,384]{1,0:T(8,128)S(1)}, ...) custom-call(s32[1,5]{1,0:T(1,128)S(1)} %copy-done.14, ...), custom_call_target="tpu_custom_call" | custom-call | tf_op jit(solution)/shard_map/forward_local/pallas_call | solution.py:485
  30.5 0.0 copy-done
  30.5 0.0 copy-done.1
  30.5 19.0 %run_experts.1 = (bf16[128,384]{1,0:T(8,128)(2,1)S(1)}, bf16[128,384]{1,0:T(8,128)(2,1)S(1)}, f32[1,384,768]{2,1,0:T(8,128)S(1)}, f32[1,768,384]{2,1,0:T(8,128)S(1)}, f32[1,128]{1,0:T(1,128)S(1)}) custom-call(bf16[16,32,128]{2,1,0:T(8,128)(2,1)S(1)} %get-tuple-element.80.pack_ref, f32[1,384,768]{2,1,0:T(8,128)S(1)} %copy-done, f32[1,768,384]{2,1,0:T(8,128)S(1)} %copy-done.1), custom_call_target="tpu_custom_call" | custom-call | tf_op jit(solution)/shard_map/run_experts/pallas_call | solution.py:647
  49.5 17.5 %backward_local.1 = (bf16[1360,384]{1,0:T(8,128)(2,1)}, f32[2,16,160,128]{3,2,1,0:T(8,128)S(1)}) custom-call(s32[1,5]{1,0:T(1,128)S(1)} %copy-done.14, f32[1360,384]{1,0:T(8,128)S(1)} %get-tuple-element.64.norm_ref.normal_one, f32[1360,128]{1,0:T(8,128)S(1)} %get-tuple-element.65.inverse_one, bf16[384,1536]{1,0:T(8,128)(2,1)S(1)} %get-tuple-element.67.w_ref, ...), custom_call_target="tpu_custom_call" | custom-call | tf_op jit(solution)/shard_map/backward_local/pallas_call | solution.py:863
  67.0 0.0 copy-start.3
  67.0 0.0 copy-start.4
  67.0 0.0 copy-start.5
  67.0 0.0 copy-start.6
  67.1 0.0 copy-start.7
  67.1 0.0 copy-start.8
  67.1 0.0 copy-start.9
  67.1 0.0 copy-start.10
  67.1 0.0 copy-start.11
  67.1 0.0 copy-start.12
  67.1 0.0 copy-start.13
  67.1 0.0 copy-start.15
  67.2 0.0 copy-start.16
  67.2 23.3 %reduce_grads.1 = (f32[24,1536]{1,0:T(8,128)S(1)}, f32[16,24]{1,0:T(8,128)S(1)}, f32[4,24]{1,0:T(4,128)S(1)}, f32[1,128]{1,0:T(1,128)S(1)}, bf16[1360,384]{1,0:T(8,128)(2,1)S(1)}) custom-call(f32[2,4,4,160,128]{4,3,2,1,0:T(8,128)S(1)} %bitcast.9, f32[1,128]{1,0:T(1,128)S(1)} %get-tuple-element.84.square_ref, f32[1360,384]{1,0:T(8,128)S(1)} %get-tuple-element.85.x1_ref, ...), custom_call_target="tpu_custom_call" | custom-call | tf_op jit(solution)/shard_map/reduce_grads/pallas_call | solution.py:1059
  90.5 0.0 copy-done.3
  90.5 0.0 copy-done.4
  90.5 0.0 copy-done.5
  90.5 0.0 copy-done.6
  90.5 0.0 copy-done.7
  90.6 0.0 copy-done.8
  90.6 0.0 copy-done.9
  90.6 0.0 copy-done.10
  90.6 0.0 copy-done.11
  90.6 0.0 copy-done.12
  90.6 0.0 copy-done.13
  90.6 0.0 copy-done.15
  90.6 0.0 copy-done.16
  90.6 4.1 %update.1 = (bf16[1360,384]{1,0:T(8,128)(2,1)}, f32[24,1536]{1,0:T(8,128)}, f32[24,1536]{1,0:T(8,128)}, f32[24,1536]{1,0:T(8,128)}, f32[16,24]{1,0:T(8,128)}, /*...) custom-call(bf16[1360,384]{1,0:T(8,128)(2,1)S(1)} %get-tuple-element, ...), custom_call_target="tpu_custom_call" | custom-call | tf_op jit(solution)/shard_map/update/pallas_call | solution.py:1154
Async XLA Ops:
  0.7 18.6 %copy-start.14 = (s32[1,5]{1,0:T(1,128)S(1)}, s32[1,5]{1,0:T(1,128)}, u32[]{:S(2)}) copy-start(s32[1,5]{1,0:T(1,128)} %len_ref.3) | copy-start | bytes 64
  0.7 18.6 %copy-start.2 = (bf16[1360,384]{1,0:T(8,128)(2,1)S(1)}, bf16[1360,384]{1,0:T(8,128)(2,1)}, u32[]{:S(2)}) copy-start(bf16[1360,384]{1,0:T(8,128)(2,1)} %patch_ref.1) | copy-start | bytes 3133444
  19.3 11.3 %copy-start = (f32[1,384,768]{2,1,0:T(8,128)S(1)}, f32[1,384,768]{2,1,0:T(8,128)}, u32[]{:S(2)}) copy-start(f32[1,384,768]{2,1,0:T(8,128)} %refs_12_.1) | copy-start | bytes 3538948
  19.3 11.2 %copy-start.1 = (f32[1,768,384]{2,1,0:T(8,128)S(1)}, f32[1,768,384]{2,1,0:T(8,128)}, u32[]{:S(2)}) copy-start(f32[1,768,384]{2,1,0:T(8,128)} %refs_16_.1) | copy-start | bytes 3538948
  67.0 23.5 %copy-start.3 = (f32[1,384,768]{2,1,0:T(8,128)S(1)}, f32[1,384,768]{2,1,0:T(8,128)}, u32[]{:S(2)}) copy-start(f32[1,384,768]{2,1,0:T(8,128)} %refs_13_.1) | copy-start | bytes 3538948
  67.0 23.5 %copy-start.4 = (f32[1,384,768]{2,1,0:T(8,128)S(1)}, f32[1,384,768]{2,1,0:T(8,128)}, u32[]{:S(2)}) copy-start(f32[1,384,768]{2,1,0:T(8,128)} %refs_14_.1) | copy-start | bytes 3538948
  67.0 23.5 %copy-start.5 = (f32[1,768,384]{2,1,0:T(8,128)S(1)}, f32[1,768,384]{2,1,0:T(8,128)}, u32[]{:S(2)}) copy-start(f32[1,768,384]{2,1,0:T(8,128)} %refs_17_.1) | copy-start | bytes 3538948
  67.0 23.5 %copy-start.6 = (f32[1,768,384]{2,1,0:T(8,128)S(1)}, f32[1,768,384]{2,1,0:T(8,128)}, u32[]{:S(2)}) copy-start(f32[1,768,384]{2,1,0:T(8,128)} %refs_18_.1) | copy-start | bytes 3538948
  67.1 23.5 %copy-start.7 = (f32[24,1536]{1,0:T(8,128)S(1)}, f32[24,1536]{1,0:T(8,128)}, u32[]{:S(2)}) copy-start(f32[24,1536]{1,0:T(8,128)} %refs_0_.1) | copy-start | bytes 442372
  67.1 23.5 %copy-start.8 = (f32[24,1536]{1,0:T(8,128)S(1)}, f32[24,1536]{1,0:T(8,128)}, u32[]{:S(2)}) copy-start(f32[24,1536]{1,0:T(8,128)} %refs_1_.1) | copy-start | bytes 442372
  67.1 23.5 %copy-start.9 = (f32[24,1536]{1,0:T(8,128)S(1)}, f32[24,1536]{1,0:T(8,128)}, u32[]{:S(2)}) copy-start(f32[24,1536]{1,0:T(8,128)} %refs_2_.1) | copy-start | bytes 442372
  67.1 23.5 %copy-start.10 = (f32[24,16]{0,1:T(8,128)S(1)}, f32[24,16]{0,1:T(8,128)}, u32[]{:S(2)}) copy-start(f32[24,16]{0,1:T(8,128)} %param.23) | copy-start | bytes 4612
  67.1 23.5 %copy-start.11 = (f32[24,16]{0,1:T(8,128)S(1)}, f32[24,16]{0,1:T(8,128)}, u32[]{:S(2)}) copy-start(f32[24,16]{0,1:T(8,128)} %param.24) | copy-start | bytes 4612
  67.1 23.5 %copy-start.12 = (f32[24,16]{0,1:T(8,128)S(1)}, f32[24,16]{0,1:T(8,128)}, u32[]{:S(2)}) copy-start(f32[24,16]{0,1:T(8,128)} %param.25) | copy-start | bytes 4612
  67.1 23.5 %copy-start.13 = (f32[4,24]{1,0:T(4,128)S(1)}, f32[4,24]{1,0:T(4,128)}, u32[]{:S(2)}) copy-start(f32[4,24]{1,0:T(4,128)} %refs_8_.1) | copy-start | bytes 1156
  67.1 23.5 %copy-start.15 = (f32[4,24]{1,0:T(4,128)S(1)}, f32[4,24]{1,0:T(4,128)}, u32[]{:S(2)}) copy-start(f32[4,24]{1,0:T(4,128)} %refs_9_.1) | copy-start | bytes 1156
  67.2 23.5 %copy-start.16 = (f32[4,24]{1,0:T(4,128)S(1)}, f32[4,24]{1,0:T(4,128)}, u32[]{:S(2)}) copy-start(f32[4,24]{1,0:T(4,128)} %refs_10_.1) | copy-start | bytes 1156
